TPU v7x, 256 devices: a whole 4x4x8 slice. The times are simulated.
256 devices in a mesh: dp: 64 (over y, z, core), help: 4 (over x).
Axes of the slice: x: 4, y: 4, z: 8, core: 2. Of those that a mesh axis runs over, the one named last changes fastest.
Arguments:
- embeddings: bfloat16 [262144, 768], P(('dp', 'help')), may hold values from -6 to 6
- clusters: int32 [262144], P(('dp', 'help')), may hold values from 0 to 127, as said below
- send_order: int32 [262144], P(('dp', 'help')), may hold values from 0 to 1023, as said below
Outputs:
- nearest: float32 [262144], P(('dp', 'help'))
Inputs may be any that keep to these rules, and one draw needn't show every extreme that they name: Cluster c belongs to index c // 2 of dp; every device holds exactly 16 rows of each index's clusters. `send_order`: on each device, a permutation of its local row numbers; positions k * 16 to (k + 1) * 16 - 1 list the rows whose cluster belongs to index k of dp.
All inputs are finite; a program needn't handle non-finite values.
Results may differ from a plain program's by a relative error of at most 0.0014.
Values may be sent and summed in bfloat16 or wider, within the bound.
No kernel may reach another device: no remote copies, remote signals or barrier semaphores. Data moves between devices by JAX's collectives and lax.ppermute only.
A program may use at most 64 MiB of HBM per device.

v0:
```python
import jax
import jax.numpy as jnp
from jax import lax
from jax.sharding import PartitionSpec as P


def best_scores(queries, query_labels, query_index, keys, key_labels, key_index):
    block = min(256, queries.shape[0])
    count = queries.shape[0] // block

    def one_block(operands):
        vectors, labels, index = operands
        sims = jnp.einsum("qd,kd->qk", vectors, keys, preferred_element_type=jnp.float32)
        mask = (labels[:, None] == key_labels[None, :]) & (key_index[None, :] < index[:, None])
        return jnp.max(jnp.where(mask, sims, -1.0), axis=1)

    result = lax.map(
        one_block,
        (
            queries.reshape(count, block, -1),
            query_labels.reshape(count, block),
            query_index.reshape(count, block),
        ),
    )
    return result.reshape(-1)


def shards(embeddings, clusters, send_order):
    rows = embeddings.shape[0]
    owners = lax.axis_size("dp")
    helpers = lax.axis_size("help")
    width = rows // owners
    values = embeddings.astype(jnp.float32)
    unit = (values * lax.rsqrt(jnp.sum(values * values, axis=1, keepdims=True) + 1e-06)).astype(
        jnp.bfloat16
    )
    base = (lax.axis_index("dp") * helpers + lax.axis_index("help")) * rows
    global_rows = base + jnp.arange(rows, dtype=jnp.int32)
    outgoing = unit[send_order].reshape(owners, width, -1)
    out_labels = clusters[send_order].reshape(owners, width)
    out_index = global_rows[send_order].reshape(owners, width)
    pool_unit, pool_labels, pool_index = (
        lax.all_to_all(outgoing, "dp", split_axis=0, concat_axis=0, tiled=True),
        lax.all_to_all(out_labels, "dp", split_axis=0, concat_axis=0, tiled=True),
        lax.all_to_all(out_index, "dp", split_axis=0, concat_axis=0, tiled=True),
    )
    pool_unit = pool_unit.reshape(rows, -1)
    pool_labels = pool_labels.reshape(rows)
    pool_index = pool_index.reshape(rows)
    all_unit, all_labels, all_index = (
        lax.all_gather(pool_unit, "help", axis=0, tiled=True),
        lax.all_gather(pool_labels, "help", axis=0, tiled=True),
        lax.all_gather(pool_index, "help", axis=0, tiled=True),
    )
    best = best_scores(pool_unit, pool_labels, pool_index, all_unit, all_labels, all_index)
    returned = lax.all_to_all(
        best.reshape(owners, width), "dp", split_axis=0, concat_axis=0, tiled=True
    )
    return jnp.zeros((rows,), jnp.float32).at[send_order].set(returned.reshape(-1))


def solution(mesh):
    return jax.shard_map(
        shards,
        mesh=mesh,
        in_specs=(P(("dp", "help"), None), P(("dp", "help")), P(("dp", "help"))),
        out_specs=P(("dp", "help")),
        check_vma=False,
    )
```

profile of v0, /device:TPU:1, one launch (start us, length us, event | category | flops | bytes accessed | tf_op | source)
XLA Modules:
  0.0 185.8 jit_solution(16532945864425866190)
XLA Ops:
  6.5 0.0 copy-start
  6.5 0.0 copy-start.1
  6.5 0.0 all-gather.2.cloned.1.call-start
  6.5 1.8 fusion.4
  8.4 1.7 fusion.5
  10.1 0.0 copy-done.1
  10.1 4.0 %gather_fusion.2 = bf16[1024,768]{1,0:T(8,128)(2,1)S(1)} fusion(bf16[1024,768]{1,0:T(8,128)(2,1)S(1)} %fusion.5, s32[1024]{0:T(1024)S(1)} %get-tuple-element.66), kind=kCustom, calls=%fused_computation.2 | custom fusion | bytes 3149824 | tf_op jit(solution)/shard_map/gather | solution.py:39
  14.1 52.9 %all_to_all.32 = bf16[64,16,768]{2,1,0:T(8,128)(2,1)} all-to-all(bf16[64,16,768]{2,1,0:T(8,128)(2,1)S(1)} %bitcast.27), channel_id=1, replica_groups=mesh['dp'=64,'help'=4] {'dp'}, dimensions={0} | all-to-all | bytes 3145728 | tf_op jit(solution)/shard_map/all_to_all | solution.py:43
  67.0 0.0 all-gather.2.cloned.1.call-update
  67.0 0.0 copy-done
  67.0 4.5 %gather_fusion = s32[1024]{0:T(1024)S(1)} fusion(s32[1024]{0:T(1024)S(1)} %copy-done, s32[1024]{0:T(1024)S(1)} %get-tuple-element.66), kind=kCustom, calls=%fused_computation | custom fusion | bytes 12288 | tf_op jit(solution)/shard_map/gather | solution.py:40
  71.6 0.7 all_to_all.21
  72.3 6.1 %all-to-all-start = ((s32[64,1,16]{2,1,0:T(1,128)}), s32[64,1,16]{2,1,0:T(1,128)S(1)}, u32[]{:S(2)}, u32[]{:S(2)}) async-start(s32[64,1,16]{2,1,0:T(1,128)} %bitcast.4), calls=%async_computation | async-start | bytes 65536 | tf_op jit(solution)/shard_map/all_to_all | solution.py:44
  78.4 4.5 %gather_fusion.1 = s32[1024]{0:T(1024)S(1)} fusion(s32[1024]{0:T(1024)S(1)} %get-tuple-element.68, s32[1024]{0:T(1024)S(1)} %get-tuple-element.66), kind=kCustom, calls=%fused_computation.1 | custom fusion | bytes 12288 | tf_op jit(solution)/shard_map/gather | solution.py:41
  82.9 0.7 all_to_all.23
  83.6 4.1 %all-to-all-done = s32[64,1,16]{2,1,0:T(1,128)S(1)} async-done(((s32[64,1,16]{2,1,0:T(1,128)}), s32[64,1,16]{2,1,0:T(1,128)S(1)}, u32[]{:S(2)}, u32[]{:S(2)}) %all-to-all-start) | async-done | bytes 4128 | tf_op jit(solution)/shard_map/all_to_all | solution.py:44
  87.7 6.2 %all-to-all-start.1 = ((s32[64,1,16]{2,1,0:T(1,128)}), s32[64,1,16]{2,1,0:T(1,128)S(1)}, u32[]{:S(2)}, u32[]{:S(2)}) async-start(s32[64,1,16]{2,1,0:T(1,128)} %bitcast.5), calls=%async_computation.1 | async-start | bytes 65536 | tf_op jit(solution)/shard_map/all_to_all | solution.py:45
  93.9 0.5 broadcast.42
  94.4 0.6 reduce.13
  95.1 0.1 reshape_reshape.10
  95.1 0.1 reshape.43
  95.2 8.0 %all-to-all-done.1 = s32[64,1,16]{2,1,0:T(1,128)S(1)} async-done(((s32[64,1,16]{2,1,0:T(1,128)}), s32[64,1,16]{2,1,0:T(1,128)S(1)}, u32[]{:S(2)}, u32[]{:S(2)}) %all-to-all-start.1) | async-done | bytes 4128 | tf_op jit(solution)/shard_map/all_to_all | solution.py:45
  103.2 0.6 reduce.14
  103.8 0.1 reshape.44
  103.9 0.1 reshape_reshape.11
  104.0 10.3 %all_gather.9 = s32[4096]{0:T(1024)S(1)} all-gather(s32[1024]{0:T(1024)S(1)} %reshape.43), channel_id=1, replica_groups=mesh['dp'=64,'help'=4] {'help'}, dimensions={0}, use_global_device_ids=true | all-gather | bytes 20480 | tf_op jit(solution)/shard_map/all_gather | solution.py:52
  114.4 10.0 %all_gather.10 = s32[4096]{0:T(1024)S(1)} all-gather(s32[1024]{0:T(1024)S(1)} %reshape.44), channel_id=1, replica_groups=mesh['dp'=64,'help'=4] {'help'}, dimensions={0}, use_global_device_ids=true | all-gather | bytes 20480 | tf_op jit(solution)/shard_map/all_gather | solution.py:53
  124.4 8.0 %all-gather.2.cloned.1.call-done = bf16[4096,768]{1,0:T(8,128)(2,1)} async-done(((bf16[1024,768]{1,0:T(8,128)(2,1)}), bf16[4096,768]{1,0:T(8,128)(2,1)}) %all-gather.2.cloned.1.call-update) | async-done | bytes 6291472 | tf_op jit(solution)/shard_map/all_gather | solution.py:51
  132.4 20.4 %while.10 = (s32[]{:T(128)}, f32[4,256]{1,0:T(4,128)S(1)}, s32[4,256]{1,0:T(4,128)S(1)}, s32[4096]{0:T(1024)S(1)}, s32[4096]{0:T(1024)S(1)}, /*index=5*/s32[4,25...) while((s32[]{:T(128)}, f32[4,256]{1,0:T(4,128)S(1)}, ...), condition=%wide.region_3.4_spmd, body=%wide.region_1.3_spmd.sunk | while | flops 1615855360 | bytes 6726777 | solution.py:17
  132.4 5.0 %fusion.14 = f32[256]{0:T(256)S(1)} fusion(bf16[4096,768]{1,0:T(8,128)(2,1)} %get-tuple-element.149, s32[256]{0:T(256)S(1)} %bitcast.32, s32[4096]{0:T(1024)S(1)} %get-tuple-element.146, s32[4096]{0:T(1024)S(1)} %get-tuple-element.145, s32[256]{0:T(256)S(1)} %bitcast.33, bf16[4,256,768]{2,1,0:T(8,128)(2,1)} %get-tuple-element.148, s32[]{:T(128)S(6)} %copy.10), kind=kOutput, calls=%fused_computation.5.clone.1 | convolution fusion | flops 1615855360 | bytes 6720516 | tf_op jit(solution)/shard_map/while/body/eval_jaxpr/qd,kd->qk/dot_general | solution.py:13
  137.5 5.0 %fusion.14 = f32[256]{0:T(256)S(1)} fusion(bf16[4096,768]{1,0:T(8,128)(2,1)} %get-tuple-element.149, s32[256]{0:T(256)S(1)} %bitcast.32, s32[4096]{0:T(1024)S(1)} %get-tuple-element.146, s32[4096]{0:T(1024)S(1)} %get-tuple-element.145, s32[256]{0:T(256)S(1)} %bitcast.33, bf16[4,256,768]{2,1,0:T(8,128)(2,1)} %get-tuple-element.148, s32[]{:T(128)S(6)} %copy.10), kind=kOutput, calls=%fused_computation.5.clone.1 | convolution fusion | flops 1615855360 | bytes 6720516 | tf_op jit(solution)/shard_map/while/body/eval_jaxpr/qd,kd->qk/dot_general | solution.py:13
  142.6 5.0 %fusion.14 = f32[256]{0:T(256)S(1)} fusion(bf16[4096,768]{1,0:T(8,128)(2,1)} %get-tuple-element.149, s32[256]{0:T(256)S(1)} %bitcast.32, s32[4096]{0:T(1024)S(1)} %get-tuple-element.146, s32[4096]{0:T(1024)S(1)} %get-tuple-element.145, s32[256]{0:T(256)S(1)} %bitcast.33, bf16[4,256,768]{2,1,0:T(8,128)(2,1)} %get-tuple-element.148, s32[]{:T(128)S(6)} %copy.10), kind=kOutput, calls=%fused_computation.5.clone.1 | convolution fusion | flops 1615855360 | bytes 6720516 | tf_op jit(solution)/shard_map/while/body/eval_jaxpr/qd,kd->qk/dot_general | solution.py:13
  147.7 5.0 %fusion.14 = f32[256]{0:T(256)S(1)} fusion(bf16[4096,768]{1,0:T(8,128)(2,1)} %get-tuple-element.149, s32[256]{0:T(256)S(1)} %bitcast.32, s32[4096]{0:T(1024)S(1)} %get-tuple-element.146, s32[4096]{0:T(1024)S(1)} %get-tuple-element.145, s32[256]{0:T(256)S(1)} %bitcast.33, bf16[4,256,768]{2,1,0:T(8,128)(2,1)} %get-tuple-element.148, s32[]{:T(128)S(6)} %copy.10), kind=kOutput, calls=%fused_computation.5.clone.1 | convolution fusion | flops 1615855360 | bytes 6720516 | tf_op jit(solution)/shard_map/while/body/eval_jaxpr/qd,kd->qk/dot_general | solution.py:13
  152.8 0.1 all_to_all.26
  152.9 19.8 %all_to_all.33 = f32[64,1,16]{2,1,0:T(1,128)S(1)} all-to-all(f32[64,1,16]{2,1,0:T(1,128)S(1)} %bitcast.30), channel_id=1, replica_groups=mesh['dp'=64,'help'=4] {'dp'}, dimensions={0} | all-to-all | bytes 8192 | tf_op jit(solution)/shard_map/all_to_all | solution.py:56
  172.7 0.5 broadcast.44
  173.2 0.7 reduce.15
  174.0 0.1 reshape.76
  174.0 4.9 %scatter_custom_fusion = f32[1024]{0:T(1024)} fusion(s32[1024]{0:T(1024)S(1)} %get-tuple-element.67, f32[1024]{0:T(1024)S(1)} %reshape.76, f32[]{:T(128)} %constant.7.clone.1), kind=kCustom, calls=%fused_computation.19 | custom fusion | bytes 4100 | tf_op jit(solution)/shard_map/scatter | solution.py:59
  (11 shorter events, 0.2 us)
Async XLA Ops:
  6.5 60.5 %copy-start = (s32[1024]{0:T(1024)S(1)}, s32[1024]{0:T(1024)}, u32[]{:S(2)}) copy-start(s32[1024]{0:T(1024)} %param.6) | copy-start | bytes 12292
  6.5 3.6 %copy-start.1 = (s32[1024]{0:T(1024)S(1)}, s32[1024]{0:T(1024)}, u32[]{:S(2)}) copy-start(s32[1024]{0:T(1024)} %param.7) | copy-start | bytes 12292
  6.5 125.9 %all-gather.2.cloned.1.call-start = ((), (), s32[]{:S(2)}) async-start(), calls=%async_computation.4 | async-start | bytes 7864320 | tf_op jit(solution)/shard_map/all_gather | solution.py:51
  72.3 15.4 %all-to-all-start = ((s32[64,1,16]{2,1,0:T(1,128)}), s32[64,1,16]{2,1,0:T(1,128)S(1)}, u32[]{:S(2)}, u32[]{:S(2)}) async-start(s32[64,1,16]{2,1,0:T(1,128)} %bitcast.4), calls=%async_computation | async-start | bytes 65536 | tf_op jit(solution)/shard_map/all_to_all | solution.py:44
  87.7 15.5 %all-to-all-start.1 = ((s32[64,1,16]{2,1,0:T(1,128)}), s32[64,1,16]{2,1,0:T(1,128)S(1)}, u32[]{:S(2)}, u32[]{:S(2)}) async-start(s32[64,1,16]{2,1,0:T(1,128)} %bitcast.5), calls=%async_computation.1 | async-start | bytes 65536 | tf_op jit(solution)/shard_map/all_to_all | solution.py:45
Sparse Core Ops, SparseCore 0:
  67.1 65.2 all-gather.1
where the time goes:
time: 186 us
  blocking collectives  93 us (50%)
  local copies, waits for them, and re-layouts  21 us (11%)
  matrix products  20.2 us (11%)
  waiting for transfers between devices  20.1 us (11%)
  between operations  13.5 us (7%)
  starting transfers between devices  12.4 us (7%)
  other arithmetic  5.52 us (3%)
    all_to_all x1, blocking collectives, shards(): lax.all_to_all(outgoing, 'dp', split_axis=0, concat_axis=0, tiled=True)  52.9 us
    dot_general x4, matrix products, one_block(): jnp.einsum('qd,kd->qk', vectors, keys, preferred_element_type=jnp.float32)  20.2 us
    all_to_all x1, blocking collectives, shards(): lax.all_to_all(best.reshape(owners, width), 'dp', split_axis=0, concat_ax...  19.8 us
    all_gather x1, blocking collectives, shards(): lax.all_gather(pool_labels, 'help', axis=0, tiled=True)  10.3 us
    all_gather x1, blocking collectives, shards(): lax.all_gather(pool_index, 'help', axis=0, tiled=True)  10 us
    all_gather x1, waiting for transfers between devices, shards(): lax.all_gather(pool_unit, 'help', axis=0, tiled=True)  8.04 us
    all_to_all x1, waiting for transfers between devices, shards(): lax.all_to_all(out_index, 'dp', split_axis=0, concat_axis=0, tiled=True)  8 us
    all_to_all x1, starting transfers between devices, shards(): lax.all_to_all(out_index, 'dp', split_axis=0, concat_axis=0, tiled=True)  6.24 us
  transfers between devices with their start and end apart: 3, of which 3 were waited for; matrix products, arithmetic and copies ran while one was open for 6% of the time, Pallas kernels for 0%

commit v1 on v0

v1 whole, which is shorter than its diff:
```python
import jax
import jax.numpy as jnp
from jax import lax
from jax.experimental import pallas as pl
from jax.experimental.pallas import tpu as pltpu
from jax.sharding import PartitionSpec as P

LANES = 128
TILE = 256


def split3(x):
    high = x.astype(jnp.bfloat16)
    rest = x - high.astype(jnp.float32)
    mid = rest.astype(jnp.bfloat16)
    low = (rest - mid.astype(jnp.float32)).astype(jnp.bfloat16)
    return high, mid, low


def iota(shape, dim):
    return lax.broadcasted_iota(jnp.int32, shape, dim)


def dot(a, b, dims):
    return lax.dot_general(a, b, (dims, ((), ())), preferred_element_type=jnp.float32)


def owner_hot(clusters, owners):
    rows = clusters.shape[1]
    return (iota((owners, rows), 0) == clusters // 2).astype(jnp.bfloat16)


def pack_kernel(emb_ref, clu_ref, out_ref, lab_ref, rank_ref):
    rows = emb_ref.shape[0]
    owners = lab_ref.shape[0]
    width = rows // owners
    clusters = clu_ref[...]
    hot = owner_hot(clusters, owners)
    before = (iota((rows, rows), 0) < iota((rows, rows), 1)).astype(jnp.bfloat16)
    count = dot(hot, before, ((1,), (0,)))
    rank = jnp.sum(hot.astype(jnp.float32) * count, axis=0, keepdims=True).astype(jnp.int32)
    rank_ref[...] = rank
    place = (clusters // 2) * width + rank
    bit = (clusters % 2).astype(jnp.float32)
    spots = jnp.where(iota((LANES, rows), 0) == rank, bit, 0.0).astype(jnp.bfloat16)
    lab_ref[...] = dot(hot, spots, ((1,), (1,)))
    values = emb_ref[...].astype(jnp.float32)
    unit = (values * lax.rsqrt(jnp.sum(values * values, axis=1, keepdims=True) + 1e-06)).astype(
        jnp.bfloat16
    )
    for start in range(0, rows, TILE):
        pick = (iota((TILE, rows), 0) + start == place).astype(jnp.bfloat16)
        out_ref[start : start + TILE, :] = dot(pick, unit, ((1,), (0,))).astype(jnp.bfloat16)


def pack(embeddings, clusters, owners):
    rows, depth = embeddings.shape
    return pl.pallas_call(
        pack_kernel,
        out_shape=(
            jax.ShapeDtypeStruct((rows, depth), jnp.bfloat16),
            jax.ShapeDtypeStruct((owners, LANES), jnp.float32),
            jax.ShapeDtypeStruct((1, rows), jnp.int32),
        ),
        compiler_params=pltpu.CompilerParams(vmem_limit_bytes=48 * 2**20),
        name="pack",
    )(embeddings, clusters.reshape(1, rows))


def row_labels(lab, rows, width):
    owners = lab.shape[0]
    hot = (iota((owners, rows), 0) == iota((owners, rows), 1) // width).astype(jnp.bfloat16)
    spread = dot(lab.astype(jnp.bfloat16), hot, ((0,), (0,)))
    chosen = iota((LANES, rows), 0) == iota((LANES, rows), 1) % width
    return jnp.sum(jnp.where(chosen, spread, 0.0), axis=0, keepdims=True)


def column_labels(lab, rows, width):
    owners = lab.shape[0]
    hot = (iota((rows, owners), 1) == iota((rows, owners), 0) // width).astype(jnp.bfloat16)
    spread = dot(hot, lab.astype(jnp.bfloat16), ((1,), (0,)))
    chosen = iota((rows, LANES), 1) == iota((rows, LANES), 0) % width
    kept = jnp.where(chosen, spread, 0.0).astype(jnp.bfloat16)
    return dot(kept, jnp.ones((LANES, TILE), jnp.bfloat16), ((1,), (0,)))


def pair_best(query_ref, key_ref, query_labels, key_labels_ref, limit):
    rows = query_ref.shape[0]
    parts = []
    for start in range(0, rows, TILE):
        queries = query_ref[start : start + TILE, :]
        labels = query_labels[:, start : start + TILE]
        best = jnp.full((1, TILE), -1.0, jnp.float32)
        for low in range(0, start + TILE, TILE):
            sims = dot(key_ref[low : low + TILE, :], queries, ((1,), (1,)))
            mask = key_labels_ref[low : low + TILE, :] == labels
            if low == start:
                mask = mask & (iota((TILE, TILE), 0) + low < limit[:, start : start + TILE])
            sims = jnp.where(mask, sims, -1.0)
            best = jnp.maximum(best, jnp.max(sims, axis=0, keepdims=True))
        parts.append(best)
    return jnp.concatenate(parts, axis=1)


def limit_of(rows, width, query_help, key_help):
    place = iota((1, rows), 1)
    group = place // width * width
    return jnp.where(
        key_help == query_help, place, jnp.where(key_help < query_help, group + width, group)
    )


def store_groups(out_ref, best, width):
    owners = out_ref.shape[0]
    rows = best.shape[1]
    mine = iota((owners, rows), 0) == iota((owners, rows), 1) // width
    spots = (iota((rows, LANES), 0) % width == iota((rows, LANES), 1)).astype(jnp.bfloat16)
    total = jnp.zeros((owners, LANES), jnp.float32)
    for piece in split3(best):
        spread = jnp.where(mine, piece.astype(jnp.float32), 0.0).astype(jnp.bfloat16)
        total = total + dot(spread, spots, ((1,), (0,)))
    out_ref[...] = total


def cross_kernel(help_ref, left_ref, right_ref, lab_left_ref, lab_right_ref, out_ref, col_ref):
    rows = left_ref.shape[0]
    width = rows // lab_left_ref.shape[0]
    me, helpers = help_ref[0], help_ref[1]
    left, right = lax.rem(me + helpers - 1, helpers), lax.rem(me + 1, helpers)
    col_ref[...] = column_labels(lab_right_ref[...], rows, width)
    best = pair_best(
        left_ref,
        right_ref,
        row_labels(lab_left_ref[...], rows, width),
        col_ref,
        limit_of(rows, width, left, right),
    )
    store_groups(out_ref, best, width)


def own_kernel(
    help_ref, own_ref, left_ref, right_ref, lab_ref, lab_left_ref, lab_right_ref, out_ref, col_ref
):
    rows = own_ref.shape[0]
    width = rows // lab_ref.shape[0]
    me, helpers = help_ref[0], help_ref[1]
    left, right = lax.rem(me + helpers - 1, helpers), lax.rem(me + 1, helpers)
    labels = row_labels(lab_ref[...], rows, width)
    best = None
    for key_ref, key_lab_ref, place in (
        (own_ref, lab_ref, me),
        (left_ref, lab_left_ref, left),
        (right_ref, lab_right_ref, right),
    ):
        col_ref[...] = column_labels(key_lab_ref[...], rows, width)
        found = pair_best(own_ref, key_ref, labels, col_ref, limit_of(rows, width, me, place))
        best = found if best is None else jnp.maximum(best, found)
    store_groups(out_ref, best, width)


def sims_call(kernel, name, where, arrays, labels):
    rows = arrays[0].shape[0]
    vmem = pl.BlockSpec(memory_space=pltpu.VMEM)
    return pl.pallas_call(
        kernel,
        out_shape=jax.ShapeDtypeStruct(labels[0].shape, jnp.float32),
        in_specs=[pl.BlockSpec(memory_space=pltpu.SMEM)] + [vmem] * (len(arrays) + len(labels)),
        out_specs=vmem,
        scratch_shapes=[pltpu.VMEM((rows, TILE), jnp.float32)],
        compiler_params=pltpu.CompilerParams(vmem_limit_bytes=48 * 2**20),
        name=name,
    )(where, *arrays, *labels)


def unpack_kernel(clu_ref, rank_ref, res_ref, out_ref):
    owners = res_ref.shape[0]
    rows = clu_ref.shape[1]
    hot = owner_hot(clu_ref[...], owners)
    total = jnp.zeros((LANES, rows), jnp.float32)
    for piece in split3(res_ref[...]):
        total = total + dot(piece, hot, ((0,), (0,)))
    mine = iota((LANES, rows), 0) == rank_ref[...]
    out_ref[...] = jnp.sum(jnp.where(mine, total, 0.0), axis=0, keepdims=True)


def unpack(clusters, rank, result):
    rows = clusters.shape[0]
    return pl.pallas_call(
        unpack_kernel,
        out_shape=jax.ShapeDtypeStruct((1, rows), jnp.float32),
        name="unpack",
    )(clusters.reshape(1, rows), rank, result).reshape(rows)


def shards(embeddings, clusters, send_order):
    rows, depth = embeddings.shape
    owners = lax.axis_size("dp")
    helpers = lax.axis_size("help")
    width = rows // owners
    up = [(h, (h + 1) % helpers) for h in range(helpers)]
    down = [(h, (h - 1) % helpers) for h in range(helpers)]
    where = jnp.stack([lax.axis_index("help"), jnp.int32(helpers)])
    outgoing, out_labels, rank = pack(embeddings, clusters, owners)
    own = lax.all_to_all(
        outgoing.reshape(owners, width, depth), "dp", split_axis=0, concat_axis=0, tiled=True
    ).reshape(rows, depth)
    lab = lax.all_to_all(
        out_labels.reshape(owners, 1, LANES), "dp", split_axis=0, concat_axis=0, tiled=True
    ).reshape(owners, LANES)
    lab_left, lab_right = lax.ppermute(lab, "help", up), lax.ppermute(lab, "help", down)
    left, right = lax.ppermute(own, "help", up), lax.ppermute(own, "help", down)
    cross = sims_call(cross_kernel, "cross", where, (left, right), (lab_left, lab_right))
    cross = lax.ppermute(cross, "help", down)
    best = sims_call(own_kernel, "own", where, (own, left, right), (lab, lab_left, lab_right))
    best = jnp.maximum(best, cross)
    returned = lax.all_to_all(
        best.reshape(owners, 1, LANES), "dp", split_axis=0, concat_axis=0, tiled=True
    ).reshape(owners, LANES)
    return unpack(clusters, rank, returned)


def solution(mesh):
    return jax.shard_map(
        shards,
        mesh=mesh,
        in_specs=(P(("dp", "help"), None), P(("dp", "help")), P(("dp", "help"))),
        out_specs=P(("dp", "help")),
        check_vma=False,
    )
```

time: 186 us -> 125 us (0.67)
  blocking collectives: 93 us -> 68.5 us
  matrix products: 20.2 us -> 0 us
  local copies, waits for them, and re-layouts: 21 us -> 2.1 us
  between operations: 13.5 us -> 0.06 us
  Pallas kernels: 0 us -> 13.2 us
  waiting for transfers between devices: 20.1 us -> 28.1 us
  other arithmetic: 5.52 us -> 0.08 us
    all_gather x2 -> x0, blocking collectives: 20.3 us -> none  [the longest x1 10.3 us: shards(): lax.all_gather(pool_labels, 'help', axis=0, tiled=True)]
    dot_general x4 -> x0, matrix products: 20.2 us -> none  [one_block(): jnp.einsum('qd,kd->qk', vectors, keys, preferred_element_type=jnp.float32)]
    ppermute x0 -> x5, waiting for transfers between devices: none -> 18.8 us  [the longest x1 15.6 us: shards(): lax.ppermute(lab, 'help', down)]
    pallas_call x0 -> x4, Pallas kernels: none -> 13.2 us  [the longest x2 8.95 us: sims_call(): pl.pallas_call(kernel, out_shape=jax.ShapeDtypeStruct(labels[0].shape, jn...]
    gather x3 -> x0, local copies, waits for them, and re-layouts: 13.1 us -> none  [the longest x1 4.53 us: shards(): out_labels = clusters[send_order].reshape(owners, width)]
    all_gather x1 -> x0, waiting for transfers between devices: 8.04 us -> none  [shards(): lax.all_gather(pool_unit, 'help', axis=0, tiled=True)]
    all_to_all x2 -> x1, starting transfers between devices: 12.4 us -> 6.4 us  [shards(): lax.all_to_all(out_labels.reshape(owners, 1, LANES), 'dp', split_axis=0,...]
    ppermute x0 -> x5, starting transfers between devices: none -> 5.92 us  [the longest x1 2.95 us: shards(): lax.ppermute(lab, 'help', down)]
  transfers between devices with their start and end apart: 3 -> 6, of which waited for: 3 -> 3; matrix products, arithmetic and copies ran while one was open for 6% -> 0% of each run, Pallas kernels for 0% -> 5%
where the time goes in v1:
time: 125 us; the launch traced here: 124 us
  blocking collectives  68.5 us (55%)
  waiting for transfers between devices  28.1 us (22%)
  Pallas kernels  13.2 us (11%)
  starting transfers between devices  12.3 us (10%)
  local copies, waits for them, and re-layouts  2.1 us (2%)
    all_to_all x1, blocking collectives, shards(): lax.all_to_all(outgoing.reshape(owners, width, depth), 'dp', split_axis=0...  52.7 us
    all_to_all x1, blocking collectives, shards(): lax.all_to_all(best.reshape(owners, 1, LANES), 'dp', split_axis=0, concat...  15.8 us
    ppermute x1, waiting for transfers between devices, shards(): lax.ppermute(lab, 'help', down)  15.6 us
    all_to_all x1, waiting for transfers between devices, shards(): lax.all_to_all(out_labels.reshape(owners, 1, LANES), 'dp', split_axis=0,...  9.27 us
    pallas_call x2, Pallas kernels, sims_call(): pl.pallas_call(kernel, out_shape=jax.ShapeDtypeStruct(labels[0].shape, jn...  8.95 us
    all_to_all x1, starting transfers between devices, shards(): lax.all_to_all(out_labels.reshape(owners, 1, LANES), 'dp', split_axis=0,...  6.4 us
    ppermute x1, waiting for transfers between devices, shards(): lax.ppermute(lab, 'help', up)  3.2 us
    ppermute x1, starting transfers between devices, shards(): lax.ppermute(lab, 'help', down)  2.95 us
  transfers between devices with their start and end apart: 6, of which 3 were waited for; matrix products, arithmetic and copies ran while one was open for 0% of the time, Pallas kernels for 5%

profile of v1, /device:TPU:1, one launch (start us, length us, event | category | flops | bytes accessed | tf_op | source)
XLA Modules:
  0.0 124.4 jit_solution(5963210574893912850)
XLA Ops:
  0.0 0.0 copy-start
  0.0 1.4 %copy-done = bf16[1024,768]{1,0:T(8,128)(2,1)S(1)} copy-done((bf16[1024,768]{1,0:T(8,128)(2,1)S(1)}, bf16[1024,768]{1,0:T(8,128)(2,1)}, u32[]{:S(2)}) %copy-start) | copy-done | bytes 1572888
  1.4 0.0 copy-start.1
  1.4 0.7 copy-done.1
  2.1 2.4 %pack.1 = (bf16[1024,768]{1,0:T(8,128)(2,1)S(1)}, f32[64,128]{1,0:T(8,128)}, s32[1,1024]{1,0:T(1,128)S(1)}) custom-call(bf16[1024,768]{1,0:T(8,128)(2,1)S(1)} %copy-done, s32[1,1024]{1,0:T(1,128)S(1)} %bitcast.21), custom_call_target="tpu_custom_call" | custom-call | tf_op jit(solution)/shard_map/pack/pallas_call | solution.py:58
  4.5 0.0 copy-start.2
  4.6 52.7 %all_to_all.15 = bf16[64,16,768]{2,1,0:T(8,128)(2,1)S(1)} all-to-all(bf16[64,16,768]{2,1,0:T(8,128)(2,1)S(1)} %bitcast.16), channel_id=1, replica_groups=mesh['dp'=64,'help'=4] {'dp'}, dimensions={0} | all-to-all | bytes 3145728 | tf_op jit(solution)/shard_map/all_to_all | solution.py:204
  57.3 0.0 copy-done.2
  57.3 2.5 %collective-permute-start.1 = (bf16[1024,768]{1,0:T(8,128)(2,1)S(1)}, bf16[1024,768]{1,0:T(8,128)(2,1)S(1)}, u32[]{:S(2)}, u32[]{:S(2)}) collective-permute-start(bf16[1024,768]{1,0:T(8,128)(2,1)S(1)} %bitcast.13), channel_id=1, source_target_pairs={{0,3},{1,0},{2,1},{3,2},{4,7},{5,4},{6,5},{7,6},{8,11},{9,8},{10,9... | collective-permute-start | bytes 4718600 | tf_op jit(solution)/shard_map/ppermute | solution.py:211
  59.8 0.0 collective-permute-start
  59.8 6.4 %all-to-all-start.1 = ((f32[64,1,128]{2,1,0:T(1,128)}), f32[64,1,128]{2,1,0:T(1,128)S(1)}, u32[]{:S(2)}, u32[]{:S(2)}) async-start(f32[64,1,128]{2,1,0:T(1,128)} %bitcast.5), calls=%async_computation.1 | async-start | bytes 65536 | tf_op jit(solution)/shard_map/all_to_all | solution.py:207
  66.2 9.3 %all-to-all-done.1 = f32[64,1,128]{2,1,0:T(1,128)S(1)} async-done(((f32[64,1,128]{2,1,0:T(1,128)}), f32[64,1,128]{2,1,0:T(1,128)S(1)}, u32[]{:S(2)}, u32[]{:S(2)}) %all-to-all-start.1) | async-done | bytes 32800 | tf_op jit(solution)/shard_map/all_to_all | solution.py:207
  75.5 3.0 %collective-permute-start.3 = (f32[64,128]{1,0:T(8,128)S(1)}, f32[64,128]{1,0:T(8,128)S(1)}, u32[]{:S(2)}, u32[]{:S(2)}) collective-permute-start(f32[64,128]{1,0:T(8,128)S(1)} %bitcast.17), channel_id=1, source_target_pairs={{0,3},{1,0},{2,1},{3,2},{4,7},{5,4},{6,5},{7,6},{8,11},{9,8},{10,9... | collective-permute-start | bytes 98312 | tf_op jit(solution)/shard_map/ppermute | solution.py:210
  78.4 0.0 collective-permute-start.2
  78.4 0.1 pad_add_fusion.help_ref
  78.5 15.6 %collective-permute-done.3.lab_right_ref = f32[64,128]{1,0:T(8,128)S(1)} collective-permute-done((f32[64,128]{1,0:T(8,128)S(1)}, f32[64,128]{1,0:T(8,128)S(1)}, u32[]{:S(2)}, u32[]{:S(2)}) %collective-permute-start.3) | collective-permute-done | bytes 32800 | tf_op jit(solution)/shard_map/ppermute | solution.py:210
  94.1 3.2 %collective-permute-done.2.lab_left_ref = f32[64,128]{1,0:T(8,128)S(1)} collective-permute-done((f32[64,128]{1,0:T(8,128)S(1)}, f32[64,128]{1,0:T(8,128)S(1)}, u32[]{:S(2)}, u32[]{:S(2)}) %collective-permute-start.2) | collective-permute-done | bytes 32800 | tf_op jit(solution)/shard_map/ppermute | solution.py:210
  97.3 0.0 collective-permute-done.1.right_ref
  97.3 0.0 collective-permute-done.left_ref
  97.3 3.2 %cross.1 = f32[64,128]{1,0:T(8,128)S(1)} custom-call(s32[2]{0:T(128)S(1)} %pad_add_fusion.help_ref, bf16[1024,768]{1,0:T(8,128)(2,1)} %collective-permute-done.left_ref, bf16[1024,768]{1,0:T(8,128)(2,1)S(1)} %collective-permute-done.1.right_ref, f32[64,128]{1,0:T(8,128)S(1)} %collective-permute-done.2.lab_left_ref, ...), custom_call_target="tpu_custom_call" | custom-call | tf_op jit(solution)/shard_map/cross/pallas_call | solution.py:164
  100.5 0.5 collective-permute-start.4
  101.0 5.8 %own.1 = f32[64,128]{1,0:T(8,128)S(1)} custom-call(s32[2]{0:T(128)S(1)} %pad_add_fusion.help_ref, bf16[1024,768]{1,0:T(8,128)(2,1)S(1)} %bitcast.15, bf16[1024,768]{1,0:T(8,128)(2,1)} %collective-permute-done.left_ref, bf16[1024,768]{1,0:T(8,128)(2,1)S(1)} %collective-permute-done.1.right_ref, f32[64,128]{1,0:T(8,128)S(1)} %bitcast.19, ...), custom_call_target="tpu_custom_call" | custom-call | tf_op jit(solution)/shard_map/own/pallas_call | solution.py:164
  106.8 0.0 collective-permute-done.4
  106.8 15.8 %all_to_all.16 = f32[64,1,128]{2,1,0:T(1,128)} all-to-all(f32[64,1,128]{2,1,0:T(1,128)S(1)} %bitcast.22), channel_id=1, replica_groups=mesh['dp'=64,'help'=4] {'dp'}, dimensions={0} | all-to-all | bytes 65536 | tf_op jit(solution)/shard_map/all_to_all | solution.py:216
  122.6 1.8 %unpack.1 = f32[1,1024]{1,0:T(1,128)} custom-call(s32[1,1024]{1,0:T(1,128)} %bitcast.20, s32[1,1024]{1,0:T(1,128)} %copy-done.2, f32[64,128]{1,0:T(8,128)} %bitcast.23), custom_call_target="tpu_custom_call" | custom-call | tf_op jit(solution)/shard_map/unpack/pallas_call | solution.py:188
  (1 shorter events, 0.0 us)
Async XLA Ops:
  0.0 1.4 %copy-start = (bf16[1024,768]{1,0:T(8,128)(2,1)S(1)}, bf16[1024,768]{1,0:T(8,128)(2,1)}, u32[]{:S(2)}) copy-start(bf16[1024,768]{1,0:T(8,128)(2,1)} %emb_ref.1) | copy-start | bytes 4718596
  1.4 0.7 copy-start.1
  4.5 52.8 %copy-start.2 = (s32[1,1024]{1,0:T(1,128)}, s32[1,1024]{1,0:T(1,128)S(1)}, u32[]{:S(2)}) copy-start(s32[1,1024]{1,0:T(1,128)S(1)} %get-tuple-element.8.rank_ref) | copy-start | bytes 12292
  57.3 40.0 %collective-permute-start.1 = (bf16[1024,768]{1,0:T(8,128)(2,1)S(1)}, bf16[1024,768]{1,0:T(8,128)(2,1)S(1)}, u32[]{:S(2)}, u32[]{:S(2)}) collective-permute-start(bf16[1024,768]{1,0:T(8,128)(2,1)S(1)} %bitcast.13), channel_id=1, source_target_pairs={{0,3},{1,0},{2,1},{3,2},{4,7},{5,4},{6,5},{7,6},{8,11},{9,8},{10,9... | collective-permute-start | bytes 4718600 | tf_op jit(solution)/shard_map/ppermute | solution.py:211
  59.8 37.6 %collective-permute-start = (bf16[1024,768]{1,0:T(8,128)(2,1)S(1)}, bf16[1024,768]{1,0:T(8,128)(2,1)}, u32[]{:S(2)}, u32[]{:S(2)}) collective-permute-start(bf16[1024,768]{1,0:T(8,128)(2,1)S(1)} %bitcast.14), channel_id=1, source_target_pairs={{0,1},{1,2},{2,3},{3,0},{4,5},{5,6},{6,7},{7,4},{8,9},{9,10},{10,1... | collective-permute-start | bytes 4718600 | tf_op jit(solution)/shard_map/ppermute | solution.py:211
  59.8 15.7 %all-to-all-start.1 = ((f32[64,1,128]{2,1,0:T(1,128)}), f32[64,1,128]{2,1,0:T(1,128)S(1)}, u32[]{:S(2)}, u32[]{:S(2)}) async-start(f32[64,1,128]{2,1,0:T(1,128)} %bitcast.5), calls=%async_computation.1 | async-start | bytes 65536 | tf_op jit(solution)/shard_map/all_to_all | solution.py:207
  75.5 18.7 %collective-permute-start.3 = (f32[64,128]{1,0:T(8,128)S(1)}, f32[64,128]{1,0:T(8,128)S(1)}, u32[]{:S(2)}, u32[]{:S(2)}) collective-permute-start(f32[64,128]{1,0:T(8,128)S(1)} %bitcast.17), channel_id=1, source_target_pairs={{0,3},{1,0},{2,1},{3,2},{4,7},{5,4},{6,5},{7,6},{8,11},{9,8},{10,9... | collective-permute-start | bytes 98312 | tf_op jit(solution)/shard_map/ppermute | solution.py:210
  78.4 18.9 %collective-permute-start.2 = (f32[64,128]{1,0:T(8,128)S(1)}, f32[64,128]{1,0:T(8,128)S(1)}, u32[]{:S(2)}, u32[]{:S(2)}) collective-permute-start(f32[64,128]{1,0:T(8,128)S(1)} %bitcast.18), channel_id=1, source_target_pairs={{0,1},{1,2},{2,3},{3,0},{4,5},{5,6},{6,7},{7,4},{8,9},{9,10},{10,1... | collective-permute-start | bytes 98312 | tf_op jit(solution)/shard_map/ppermute | solution.py:210
  100.5 6.3 %collective-permute-start.4 = (f32[64,128]{1,0:T(8,128)S(1)}, f32[64,128]{1,0:T(8,128)S(1)}, u32[]{:S(2)}, u32[]{:S(2)}) collective-permute-start(f32[64,128]{1,0:T(8,128)S(1)} %cross.1), channel_id=1, source_target_pairs={{0,3},{1,0},{2,1},{3,2},{4,7},{5,4},{6,5},{7,6},{8,11},{9,8},{10,9... | collective-permute-start | bytes 98312 | tf_op jit(solution)/shard_map/ppermute | solution.py:213

commit v2 on v0

v2 whole, which is shorter than its diff:
```python
import jax
import jax.numpy as jnp
from jax import lax
from jax.experimental import pallas as pl
from jax.experimental.pallas import tpu as pltpu
from jax.sharding import PartitionSpec as P

LANES = 128
TILE = 256


def split3(x):
    high = x.astype(jnp.bfloat16)
    rest = x - high.astype(jnp.float32)
    mid = rest.astype(jnp.bfloat16)
    low = (rest - mid.astype(jnp.float32)).astype(jnp.bfloat16)
    return high, mid, low


def iota(shape, dim):
    return lax.broadcasted_iota(jnp.int32, shape, dim)


def dot(a, b, dims):
    return lax.dot_general(a, b, (dims, ((), ())), preferred_element_type=jnp.float32)


def slot_of(clusters, core, half):
    owner = clusters // 2
    away = jnp.where(owner // half == core, 0, 1)
    return owner % half + away * half, away


def pack_kernel(where_ref, emb_ref, clu_ref, keep_ref, send_ref, keep_lab_ref, send_lab_ref, spot_ref):
    rows = emb_ref.shape[0]
    half = keep_lab_ref.shape[0]
    width = keep_ref.shape[0] // half
    clusters = clu_ref[...]
    slot, away = slot_of(clusters, where_ref[1], half)
    hot = (iota((2 * half, rows), 0) == slot).astype(jnp.bfloat16)
    before = (iota((rows, rows), 0) < iota((rows, rows), 1)).astype(jnp.bfloat16)
    count = dot(hot, before, ((1,), (0,)))
    rank = jnp.sum(hot.astype(jnp.float32) * count, axis=0, keepdims=True).astype(jnp.int32)
    spot = rank + away * width
    spot_ref[...] = spot
    place = slot * width + rank
    bit = (clusters % 2).astype(jnp.float32)
    spots = jnp.where(iota((LANES, rows), 0) == spot, bit, 0.0).astype(jnp.bfloat16)
    labels = dot(hot, spots, ((1,), (1,)))
    keep_lab_ref[...] = labels[:half]
    send_lab_ref[...] = labels[half:]
    values = emb_ref[...].astype(jnp.float32)
    unit = (values * lax.rsqrt(jnp.sum(values * values, axis=1, keepdims=True) + 1e-06)).astype(
        jnp.bfloat16
    )
    for out_ref, base in ((send_ref, rows // 2), (keep_ref, 0)):
        for start in range(0, rows // 2, TILE):
            pick = (iota((TILE, rows), 0) + (base + start) == place).astype(jnp.bfloat16)
            out_ref[start : start + TILE, :] = dot(pick, unit, ((1,), (0,))).astype(jnp.bfloat16)


def pack(where, embeddings, clusters, owners):
    rows, depth = embeddings.shape
    vmem = pl.BlockSpec(memory_space=pltpu.VMEM)
    return pl.pallas_call(
        pack_kernel,
        out_shape=(
            jax.ShapeDtypeStruct((rows // 2, depth), jnp.bfloat16),
            jax.ShapeDtypeStruct((rows // 2, depth), jnp.bfloat16),
            jax.ShapeDtypeStruct((owners // 2, LANES), jnp.float32),
            jax.ShapeDtypeStruct((owners // 2, LANES), jnp.float32),
            jax.ShapeDtypeStruct((1, rows), jnp.int32),
        ),
        in_specs=[pl.BlockSpec(memory_space=pltpu.SMEM), vmem, vmem],
        compiler_params=pltpu.CompilerParams(vmem_limit_bytes=48 * 2**20),
        name="pack",
    )(where, embeddings, clusters.reshape(1, rows))


def order_of(place, core, part):
    source, flip, rank = place // 32, place // 16 % 2, place % 16
    from_core = jnp.where(flip == 0, core, 1 - core)
    by_row = (source * 2 + from_core) * 4 + part
    by_column = ((part * 8 + source // 4) * 2 + from_core) * 4 + source % 4
    return jnp.where(core == 0, by_row, by_column) * 16 + rank


def row_labels(lab, rows):
    sources = lab.shape[0]
    width = rows // sources
    hot = (iota((sources, rows), 0) == iota((sources, rows), 1) // width).astype(jnp.bfloat16)
    spread = dot(lab.astype(jnp.bfloat16), hot, ((0,), (0,)))
    chosen = iota((LANES, rows), 0) == iota((LANES, rows), 1) % width
    return jnp.sum(jnp.where(chosen, spread, 0.0), axis=0, keepdims=True)


def column_labels(lab, rows):
    sources = lab.shape[0]
    width = rows // sources
    hot = (iota((rows, sources), 1) == iota((rows, sources), 0) // width).astype(jnp.bfloat16)
    spread = dot(hot, lab.astype(jnp.bfloat16), ((1,), (0,)))
    chosen = iota((rows, LANES), 1) == iota((rows, LANES), 0) % width
    kept = jnp.where(chosen, spread, 0.0).astype(jnp.bfloat16)
    return dot(kept, jnp.ones((LANES, LANES), jnp.bfloat16), ((1,), (0,)))


def set_keys(order_ref, labels_ref, lab_ref, core, part):
    rows = order_ref.shape[0]
    order_ref[...] = order_of(iota((rows, LANES), 0), core, part)
    labels_ref[...] = column_labels(lab_ref[...], rows)


def scan(best_ref, query_ref, key_ref, query_labels, order_ref, labels_ref, core, part, pick):
    rows = query_ref.shape[0]
    order = order_of(iota((1, rows), 1), core, part)
    for start in range(0, rows, TILE):
        queries = query_ref[start : start + TILE, :]
        here = slice(start, start + TILE)
        best = best_ref[:, here]
        for low in range(0, rows, TILE):
            if not pick(low, start):
                continue
            sims = dot(key_ref[low : low + TILE, :], queries, ((1,), (1,)))
            wide = (
                jnp.concatenate([ref[low : low + TILE, :]] * (TILE // LANES), axis=1)
                for ref in (order_ref, labels_ref)
            )
            key_order, key_labels = wide
            mask = (key_labels == query_labels[:, here]) & (key_order < order[:, here])
            found = jnp.max(jnp.where(mask, sims, -1.0), axis=0, keepdims=True)
            best = jnp.maximum(best, found)
        best_ref[:, here] = best


def scan_pair(best_ref, query_ref, key_ref, query_labels, order_ref, labels_ref, core, part, key_part):
    args = (best_ref, query_ref, key_ref, query_labels, order_ref, labels_ref, core, part)

    @pl.when((core == 0) | (key_part < part))
    def _():
        scan(*args, lambda low, start: low <= start)

    @pl.when((core != 0) & (key_part < part))
    def _():
        scan(*args, lambda low, start: low > start)


def store_groups(out_ref, best):
    sources = out_ref.shape[0]
    rows = best.shape[1]
    width = rows // sources
    mine = iota((sources, rows), 0) == iota((sources, rows), 1) // width
    spots = (iota((rows, LANES), 0) % width == iota((rows, LANES), 1)).astype(jnp.bfloat16)
    total = jnp.zeros((sources, LANES), jnp.float32)
    for piece in split3(best):
        spread = jnp.where(mine, piece.astype(jnp.float32), 0.0).astype(jnp.bfloat16)
        total = total + dot(spread, spots, ((1,), (0,)))
    out_ref[...] = total


def parts_of(where_ref):
    me, core, parts = where_ref[0], where_ref[1], where_ref[2]
    return core, me, lax.rem(me + parts - 1, parts), lax.rem(me + 1, parts)


def alone_kernel(where_ref, own_ref, lab_ref, best_ref, order_ref, labels_ref):
    rows = own_ref.shape[0]
    core, me, _, _ = parts_of(where_ref)
    best_ref[...] = jnp.full((1, rows), -1.0, jnp.float32)
    set_keys(order_ref, labels_ref, lab_ref, core, me)
    scan(
        best_ref, own_ref, own_ref, row_labels(lab_ref[...], rows), order_ref, labels_ref, core, me,
        lambda low, start: low <= start,
    )


def cross_kernel(where_ref, left_ref, right_ref, lab_left_ref, lab_right_ref, out_ref, best_ref, order_ref, labels_ref):
    rows = left_ref.shape[0]
    core, _, left, right = parts_of(where_ref)
    best_ref[...] = jnp.full((1, rows), -1.0, jnp.float32)
    set_keys(order_ref, labels_ref, lab_left_ref, core, left)
    labels = row_labels(lab_right_ref[...], rows)
    scan_pair(best_ref, right_ref, left_ref, labels, order_ref, labels_ref, core, right, left)
    store_groups(out_ref, best_ref[...])


def sides_kernel(
    where_ref, alone_ref, own_ref, left_ref, right_ref, lab_ref, lab_left_ref, lab_right_ref,
    out_ref, best_ref, order_ref, labels_ref,
):
    rows = own_ref.shape[0]
    core, me, left, right = parts_of(where_ref)
    best_ref[...] = alone_ref[...]
    labels = row_labels(lab_ref[...], rows)
    for key_ref, key_lab_ref, part in ((left_ref, lab_left_ref, left), (right_ref, lab_right_ref, right)):
        set_keys(order_ref, labels_ref, key_lab_ref, core, part)
        scan_pair(best_ref, own_ref, key_ref, labels, order_ref, labels_ref, core, me, part)
    store_groups(out_ref, best_ref[...])


def sims_call(kernel, name, out_shape, where, arrays, rows, scratch):
    vmem = pl.BlockSpec(memory_space=pltpu.VMEM)
    best = [pltpu.VMEM((1, rows), jnp.float32)] if scratch else []
    return pl.pallas_call(
        kernel,
        out_shape=jax.ShapeDtypeStruct(out_shape, jnp.float32),
        in_specs=[pl.BlockSpec(memory_space=pltpu.SMEM)] + [vmem] * len(arrays),
        out_specs=vmem,
        scratch_shapes=best
        + [pltpu.VMEM((rows, LANES), jnp.int32), pltpu.VMEM((rows, LANES), jnp.float32)],
        compiler_params=pltpu.CompilerParams(vmem_limit_bytes=48 * 2**20),
        name=name,
    )(where, *arrays)


def unpack_kernel(where_ref, clu_ref, spot_ref, near_ref, far_ref, out_ref):
    half = near_ref.shape[0]
    rows = clu_ref.shape[1]
    slot, _ = slot_of(clu_ref[...], where_ref[1], half)
    hot = (iota((2 * half, rows), 0) == slot).astype(jnp.bfloat16)
    total = jnp.zeros((LANES, rows), jnp.float32)
    for piece in split3(jnp.concatenate([near_ref[...], far_ref[...]], axis=0)):
        total = total + dot(piece, hot, ((0,), (0,)))
    mine = iota((LANES, rows), 0) == spot_ref[...]
    out_ref[...] = jnp.sum(jnp.where(mine, total, 0.0), axis=0, keepdims=True)


def unpack(where, clusters, spot, near, far):
    rows = clusters.shape[0]
    vmem = pl.BlockSpec(memory_space=pltpu.VMEM)
    return pl.pallas_call(
        unpack_kernel,
        out_shape=jax.ShapeDtypeStruct((1, rows), jnp.float32),
        in_specs=[pl.BlockSpec(memory_space=pltpu.SMEM)] + [vmem] * 4,
        out_specs=vmem,
        name="unpack",
    )(where, clusters.reshape(1, rows), spot, near, far).reshape(rows)


AXES = ("dp", "help")
NY, NZ, NX = 4, 8, 4


def device(y, z, core, x):
    return ((y % NY * NZ + z % NZ) * 2 + core) * NX + x % NX


EVERY = [(y, z, c, x) for y in range(NY) for z in range(NZ) for c in range(2) for x in range(NX)]
SWAP = [(device(y, z, c, x), device(y, z, 1 - c, x)) for y, z, c, x in EVERY]
GROUPS = [[device(y, z, 0, x) for y in range(NY) for z in range(NZ)] for x in range(NX)] + [
    [device(y, z, 1, x) for z in range(NZ) for x in range(NX)] for y in range(NY)
]


def aside(step):
    return [
        (device(y, z, c, x), device(y, z, c, x + step) if c == 0 else device(y + step, z, c, x))
        for y, z, c, x in EVERY
    ]


def exchange(array):
    return lax.all_to_all(
        array, AXES, split_axis=0, concat_axis=0, axis_index_groups=GROUPS, tiled=True
    )


def shards(embeddings, clusters, send_order):
    rows, depth = embeddings.shape
    owners = lax.axis_size("dp")
    half = owners // 2
    width = rows // owners
    dp, x = lax.axis_index("dp"), lax.axis_index("help")
    core, y = dp % 2, dp // (2 * NZ)
    where = jnp.stack([jnp.where(core == 0, x, y), core, jnp.int32(NX)])
    keep, send, keep_lab, send_lab, spot = pack(where, embeddings, clusters, owners)
    got, got_lab = lax.ppermute(send, AXES, SWAP), lax.ppermute(send_lab, AXES, SWAP)
    outgoing = jnp.concatenate(
        [keep.reshape(half, width, depth), got.reshape(half, width, depth)], axis=1
    )
    own = exchange(outgoing).reshape(rows, depth)
    lab = exchange((keep_lab + got_lab).reshape(half, 1, LANES)).reshape(half, LANES)
    left, right = lax.ppermute(own, AXES, aside(1)), lax.ppermute(own, AXES, aside(-1))
    lab_left, lab_right = lax.ppermute(lab, AXES, aside(1)), lax.ppermute(lab, AXES, aside(-1))
    alone = sims_call(alone_kernel, "alone", (1, rows), where, (own, lab), rows, False)
    arrays = (left, right, lab_left, lab_right)
    cross = sims_call(cross_kernel, "cross", (half, LANES), where, arrays, rows, True)
    cross = lax.ppermute(cross, AXES, aside(1))
    arrays = (alone, own, left, right, lab, lab_left, lab_right)
    best = sims_call(sides_kernel, "sides", (half, LANES), where, arrays, rows, True)
    best = jnp.maximum(best, cross)
    near = exchange(best.reshape(half, 1, LANES)).reshape(half, LANES)
    far = lax.ppermute(near, AXES, SWAP)
    return unpack(where, clusters, spot, near, far)


def solution(mesh):
    return jax.shard_map(
        shards,
        mesh=mesh,
        in_specs=(P(("dp", "help"), None), P(("dp", "help")), P(("dp", "help"))),
        out_specs=P(("dp", "help")),
        check_vma=False,
    )
```

time: 186 us -> 114 us (0.61)
  matrix products: 20.2 us -> 0 us
  local copies, waits for them, and re-layouts: 21 us -> 2.7 us
  blocking collectives: 93 us -> 74.9 us
  between operations: 13.5 us -> 0.08 us
  waiting for transfers between devices: 20.1 us -> 7 us
  Pallas kernels: 0 us -> 10.5 us
  starting transfers between devices: 12.4 us -> 18.8 us
  other arithmetic: 5.52 us -> 0.29 us
    all_gather x2 -> x0, blocking collectives: 20.3 us -> none  [the longest x1 10.3 us: shards(): lax.all_gather(pool_labels, 'help', axis=0, tiled=True)]
    dot_general x4 -> x0, matrix products: 20.2 us -> none  [one_block(): jnp.einsum('qd,kd->qk', vectors, keys, preferred_element_type=jnp.float32)]
    ppermute x0 -> x8, starting transfers between devices: none -> 18.8 us  [the longest x1 7.15 us: shards(): far = lax.ppermute(near, AXES, SWAP)]
    gather x3 -> x0, local copies, waits for them, and re-layouts: 13.1 us -> none  [the longest x1 4.53 us: shards(): out_labels = clusters[send_order].reshape(owners, width)]
    all_to_all x2 -> x0, starting transfers between devices: 12.4 us -> none  [the longest x1 6.24 us: shards(): lax.all_to_all(out_index, 'dp', split_axis=0, concat_axis=0, tiled=True)]
    all_to_all x2 -> x0, waiting for transfers between devices: 12.1 us -> none  [the longest x1 8 us: shards(): lax.all_to_all(out_index, 'dp', split_axis=0, concat_axis=0, tiled=True)]
    pallas_call x0 -> x5, Pallas kernels: none -> 10.5 us  [the longest x3 5.69 us: sims_call(): pl.pallas_call(kernel, out_shape=jax.ShapeDtypeStruct(out_shape, jnp.floa...]
    all_gather x1 -> x0, waiting for transfers between devices: 8.04 us -> none  [shards(): lax.all_gather(pool_unit, 'help', axis=0, tiled=True)]
  transfers between devices with their start and end apart: 3 -> 8, of which waited for: 3 -> 5; matrix products, arithmetic and copies ran while one was open for 6% -> 0% of each run, Pallas kernels for 0% -> 4%
where the time goes in v2:
time: 114 us
  blocking collectives  74.9 us (66%)
  starting transfers between devices  18.8 us (16%)
  Pallas kernels  10.5 us (9%)
  waiting for transfers between devices  7 us (6%)
  local copies, waits for them, and re-layouts  2.7 us (2%)
    all_to_all x3, blocking collectives, exchange(): lax.all_to_all(array, AXES, split_axis=0, concat_axis=0, axis_index_group...  74.9 us
    ppermute x1, starting transfers between devices, shards(): far = lax.ppermute(near, AXES, SWAP)  7.15 us
    pallas_call x3, Pallas kernels, sims_call(): pl.pallas_call(kernel, out_shape=jax.ShapeDtypeStruct(out_shape, jnp.floa...  5.69 us
    ppermute x1, starting transfers between devices, shards(): lax.ppermute(send, AXES, SWAP)  3.33 us
    pallas_call x1, Pallas kernels, pack(): pl.pallas_call(pack_kernel, out_shape=(jax.ShapeDtypeStruct((rows // 2, d...  3 us
    ppermute x1, starting transfers between devices, shards(): lax.ppermute(own, AXES, aside(-1))  2.94 us
    unnamed x12, local copies, waits for them, and re-layouts  2.7 us
  transfers between devices with their start and end apart: 8, of which 5 were waited for; matrix products, arithmetic and copies ran while one was open for 0% of the time, Pallas kernels for 4%

profile of v2, /device:TPU:1, one launch (start us, length us, event | category | flops | bytes accessed | tf_op | source)
XLA Modules:
  0.0 114.2 jit_solution(7341739041055973629)
XLA Ops:
  0.0 0.1 pad_add_fusion.where_ref
  0.1 0.0 copy-start.1
  0.1 0.0 copy-start
  0.1 1.4 %copy-done = bf16[1024,768]{1,0:T(8,128)(2,1)S(1)} copy-done((bf16[1024,768]{1,0:T(8,128)(2,1)S(1)}, bf16[1024,768]{1,0:T(8,128)(2,1)}, u32[]{:S(2)}) %copy-start) | copy-done | bytes 1572888
  1.5 0.0 copy-start.2
  1.5 0.7 copy-done.2
  2.2 3.0 %pack.1 = (bf16[512,768]{1,0:T(8,128)(2,1)S(1)}, bf16[512,768]{1,0:T(8,128)(2,1)S(1)}, f32[32,128]{1,0:T(8,128)S(1)}, f32[32,128]{1,0:T(8,128)S(1)}, s32[1,1024]{1,0:T(1,128)S(1)}) custom-call(s32[3]{0:T(128)S(1)} %pad_add_fusion.where_ref, bf16[1024,768]{1,0:T(8,128)(2,1)S(1)} %copy-done, s32[1,1024]{1,0:T(1,128)S(1)} %bitcast.25), custom_call_target="tpu_custom_call" | custom-call | tf_op jit(solution)/shard_map/pack/pallas_call | solution.py:65
  5.2 0.0 copy-start.3
  5.2 3.3 %collective-permute-start = (bf16[512,768]{1,0:T(8,128)(2,1)S(1)}, bf16[512,768]{1,0:T(8,128)(2,1)S(1)}, u32[]{:S(2)}, u32[]{:S(2)}) collective-permute-start(bf16[512,768]{1,0:T(8,128)(2,1)S(1)} %get-tuple-element.12), channel_id=1, source_target_pairs={{0,4},{1,5},{2,6},{3,7},{4,0},{5,1},{6,2},{7,3},{8,12},{9,13},{10,... | collective-permute-start | bytes 2359304 | tf_op jit(solution)/shard_map/ppermute | solution.py:276
  8.5 1.9 %collective-permute-done = bf16[512,768]{1,0:T(8,128)(2,1)S(1)} collective-permute-done((bf16[512,768]{1,0:T(8,128)(2,1)S(1)}, bf16[512,768]{1,0:T(8,128)(2,1)S(1)}, u32[]{:S(2)}, u32[]{:S(2)}) %collective-permute-start) | collective-permute-done | bytes 786464 | tf_op jit(solution)/shard_map/ppermute | solution.py:276
  10.4 0.2 pad_maximum_fusion
  10.6 0.0 copy-done.3
  10.6 47.9 %all_to_all.15 = bf16[32,32,768]{2,1,0:T(8,128)(2,1)S(1)} all-to-all(bf16[32,32,768]{2,1,0:T(8,128)(2,1)S(1)} %pad_maximum_fusion), channel_id=1, replica_groups={{0,8,16,24,32,40,48,56,64,72,80,88,96,104,112,120,128,136,144,152,160,1..., dimensions={0} | all-to-all | bytes 3145728 | tf_op jit(solution)/shard_map/all_to_all | solution.py:262
  58.6 2.9 %collective-permute-start.3 = (bf16[1024,768]{1,0:T(8,128)(2,1)S(1)}, bf16[1024,768]{1,0:T(8,128)(2,1)S(1)}, u32[]{:S(2)}, u32[]{:S(2)}) collective-permute-start(bf16[1024,768]{1,0:T(8,128)(2,1)S(1)} %bitcast.15), channel_id=1, source_target_pairs={{0,3},{1,0},{2,1},{3,2},{4,196},{5,197},{6,198},{7,199},{8,11},{9,... | collective-permute-start | bytes 4718600 | tf_op jit(solution)/shard_map/ppermute | solution.py:282
  61.5 0.0 collective-permute-start.2
  61.5 1.6 %collective-permute-start.1 = (f32[32,128]{1,0:T(8,128)S(1)}, f32[32,128]{1,0:T(8,128)S(1)}, u32[]{:S(2)}, u32[]{:S(2)}) collective-permute-start(f32[32,128]{1,0:T(8,128)S(1)} %get-tuple-element.14), channel_id=1, source_target_pairs={{0,4},{1,5},{2,6},{3,7},{4,0},{5,1},{6,2},{7,3},{8,12},{9,13},{10,... | collective-permute-start | bytes 49160 | tf_op jit(solution)/shard_map/ppermute | solution.py:276
  63.1 0.8 collective-permute-done.1
  64.0 15.4 %all_to_all.16 = f32[32,1,128]{2,1,0:T(1,128)S(1)} all-to-all(f32[32,1,128]{2,1,0:T(1,128)S(1)} %bitcast.27), channel_id=1, replica_groups={{0,8,16,24,32,40,48,56,64,72,80,88,96,104,112,120,128,136,144,152,160,1..., dimensions={0} | all-to-all | bytes 32768 | tf_op jit(solution)/shard_map/all_to_all | solution.py:262
  79.4 0.8 collective-permute-start.5
  80.1 0.7 collective-permute-start.4
  80.8 1.4 %collective-permute-done.5.lab_right_ref = f32[32,128]{1,0:T(8,128)S(1)} collective-permute-done((f32[32,128]{1,0:T(8,128)S(1)}, f32[32,128]{1,0:T(8,128)S(1)}, u32[]{:S(2)}, u32[]{:S(2)}) %collective-permute-start.5) | collective-permute-done | bytes 16416 | tf_op jit(solution)/shard_map/ppermute | solution.py:283
  82.3 2.0 %collective-permute-done.4.lab_left_ref = f32[32,128]{1,0:T(8,128)S(1)} collective-permute-done((f32[32,128]{1,0:T(8,128)S(1)}, f32[32,128]{1,0:T(8,128)S(1)}, u32[]{:S(2)}, u32[]{:S(2)}) %collective-permute-start.4) | collective-permute-done | bytes 16416 | tf_op jit(solution)/shard_map/ppermute | solution.py:283
  84.2 0.0 collective-permute-done.3.right_ref
  84.2 0.0 collective-permute-done.2.left_ref
  84.2 1.4 %cross.1 = f32[32,128]{1,0:T(8,128)S(1)} custom-call(s32[3]{0:T(128)S(1)} %pad_add_fusion.where_ref, bf16[1024,768]{1,0:T(8,128)(2,1)S(1)} %collective-permute-done.2.left_ref, bf16[1024,768]{1,0:T(8,128)(2,1)S(1)} %collective-permute-done.3.right_ref, f32[32,128]{1,0:T(8,128)S(1)} %collective-permute-done.4.lab_left_ref, ...), custom_call_target="tpu_custom_call" | custom-call | tf_op jit(solution)/shard_map/cross/pallas_call | solution.py:203
  85.7 2.3 %collective-permute-start.6 = (f32[32,128]{1,0:T(8,128)S(1)}, f32[32,128]{1,0:T(8,128)S(1)}, u32[]{:S(2)}, u32[]{:S(2)}) collective-permute-start(f32[32,128]{1,0:T(8,128)S(1)} %cross.1), channel_id=1, source_target_pairs={{0,1},{1,2},{2,3},{3,0},{4,68},{5,69},{6,70},{7,71},{8,9},{9,10},{... | collective-permute-start | bytes 49160 | tf_op jit(solution)/shard_map/ppermute | solution.py:287
  87.9 2.3 %alone.1.alone_ref = f32[1,1024]{1,0:T(1,128)S(1)} custom-call(s32[3]{0:T(128)S(1)} %pad_add_fusion.where_ref, bf16[1024,768]{1,0:T(8,128)(2,1)S(1)} %bitcast.17, f32[32,128]{1,0:T(8,128)S(1)} %bitcast.22), custom_call_target="tpu_custom_call" | custom-call | tf_op jit(solution)/shard_map/alone/pallas_call | solution.py:203
  90.2 0.0 copy-done.1
  90.2 2.0 %sides.1 = f32[32,128]{1,0:T(8,128)S(1)} custom-call(s32[3]{0:T(128)S(1)} %pad_add_fusion.where_ref, f32[1,1024]{1,0:T(1,128)S(1)} %alone.1.alone_ref, bf16[1024,768]{1,0:T(8,128)(2,1)S(1)} %bitcast.18, bf16[1024,768]{1,0:T(8,128)(2,1)S(1)} %collective-permute-done.2.left_ref, bf16[1024,768]{1,0:T(8,128)(2,1)S(1)} %collective-permute-done.3.right_ref, ...), custom_call_target="tpu_custom_call" | custom-call | tf_op jit(solution)/shard_map/sides/pallas_call | solution.py:203
  92.2 0.0 collective-permute-done.6
  92.2 11.6 %all_to_all.17 = f32[32,1,128]{2,1,0:T(1,128)S(1)} all-to-all(f32[32,1,128]{2,1,0:T(1,128)S(1)} %bitcast.28), channel_id=1, replica_groups={{0,8,16,24,32,40,48,56,64,72,80,88,96,104,112,120,128,136,144,152,160,1..., dimensions={0} | all-to-all | bytes 32768 | tf_op jit(solution)/shard_map/all_to_all | solution.py:262
  103.8 0.0 copy-start.4
  103.8 7.1 %collective-permute-start.7 = (f32[32,128]{1,0:T(8,128)S(1)}, f32[32,128]{1,0:T(8,128)S(1)}, u32[]{:S(2)}, u32[]{:S(2)}) collective-permute-start(f32[32,128]{1,0:T(8,128)S(1)} %bitcast.29), channel_id=1, source_target_pairs={{0,4},{1,5},{2,6},{3,7},{4,0},{5,1},{6,2},{7,3},{8,12},{9,13},{10,... | collective-permute-start | bytes 49160 | tf_op jit(solution)/shard_map/ppermute | solution.py:292
  111.0 0.8 collective-permute-done.7.far_ref
  111.8 0.0 copy-start.5
  111.8 0.0 copy-done.4
  111.8 0.6 copy-done.5
  112.4 1.8 %unpack.1 = f32[1,1024]{1,0:T(1,128)} custom-call(s32[3]{0:T(128)} %copy-done.1, s32[1,1024]{1,0:T(1,128)} %bitcast.24, s32[1,1024]{1,0:T(1,128)} %copy-done.3, f32[32,128]{1,0:T(8,128)} %bitcast.30, f32[32,128]{1,0:T(8,128)} %copy-done.5), custom_call_target="tpu_custom_call" | custom-call | tf_op jit(solution)/shard_map/unpack/pallas_call | solution.py:230
  (2 shorter events, 0.0 us)
Async XLA Ops:
  0.1 90.1 %copy-start.1 = (s32[3]{0:T(128)}, s32[3]{0:T(128)S(1)}, u32[]{:S(2)}) copy-start(s32[3]{0:T(128)S(1)} %pad_add_fusion.where_ref) | copy-start | bytes 40
  0.1 1.4 %copy-start = (bf16[1024,768]{1,0:T(8,128)(2,1)S(1)}, bf16[1024,768]{1,0:T(8,128)(2,1)}, u32[]{:S(2)}) copy-start(bf16[1024,768]{1,0:T(8,128)(2,1)} %emb_ref.1) | copy-start | bytes 4718596
  1.5 0.7 copy-start.2
  5.2 5.5 %copy-start.3 = (s32[1,1024]{1,0:T(1,128)}, s32[1,1024]{1,0:T(1,128)S(1)}, u32[]{:S(2)}) copy-start(s32[1,1024]{1,0:T(1,128)S(1)} %get-tuple-element.10.spot_ref) | copy-start | bytes 12292
  5.2 5.2 %collective-permute-start = (bf16[512,768]{1,0:T(8,128)(2,1)S(1)}, bf16[512,768]{1,0:T(8,128)(2,1)S(1)}, u32[]{:S(2)}, u32[]{:S(2)}) collective-permute-start(bf16[512,768]{1,0:T(8,128)(2,1)S(1)} %get-tuple-element.12), channel_id=1, source_target_pairs={{0,4},{1,5},{2,6},{3,7},{4,0},{5,1},{6,2},{7,3},{8,12},{9,13},{10,... | collective-permute-start | bytes 2359304 | tf_op jit(solution)/shard_map/ppermute | solution.py:276
  58.6 25.7 %collective-permute-start.3 = (bf16[1024,768]{1,0:T(8,128)(2,1)S(1)}, bf16[1024,768]{1,0:T(8,128)(2,1)S(1)}, u32[]{:S(2)}, u32[]{:S(2)}) collective-permute-start(bf16[1024,768]{1,0:T(8,128)(2,1)S(1)} %bitcast.15), channel_id=1, source_target_pairs={{0,3},{1,0},{2,1},{3,2},{4,196},{5,197},{6,198},{7,199},{8,11},{9,... | collective-permute-start | bytes 4718600 | tf_op jit(solution)/shard_map/ppermute | solution.py:282
  61.5 22.7 %collective-permute-start.2 = (bf16[1024,768]{1,0:T(8,128)(2,1)S(1)}, bf16[1024,768]{1,0:T(8,128)(2,1)S(1)}, u32[]{:S(2)}, u32[]{:S(2)}) collective-permute-start(bf16[1024,768]{1,0:T(8,128)(2,1)S(1)} %bitcast.16), channel_id=1, source_target_pairs={{0,1},{1,2},{2,3},{3,0},{4,68},{5,69},{6,70},{7,71},{8,9},{9,10},{... | collective-permute-start | bytes 4718600 | tf_op jit(solution)/shard_map/ppermute | solution.py:282
  61.5 2.5 %collective-permute-start.1 = (f32[32,128]{1,0:T(8,128)S(1)}, f32[32,128]{1,0:T(8,128)S(1)}, u32[]{:S(2)}, u32[]{:S(2)}) collective-permute-start(f32[32,128]{1,0:T(8,128)S(1)} %get-tuple-element.14), channel_id=1, source_target_pairs={{0,4},{1,5},{2,6},{3,7},{4,0},{5,1},{6,2},{7,3},{8,12},{9,13},{10,... | collective-permute-start | bytes 49160 | tf_op jit(solution)/shard_map/ppermute | solution.py:276
  79.4 2.9 %collective-permute-start.5 = (f32[32,128]{1,0:T(8,128)S(1)}, f32[32,128]{1,0:T(8,128)S(1)}, u32[]{:S(2)}, u32[]{:S(2)}) collective-permute-start(f32[32,128]{1,0:T(8,128)S(1)} %bitcast.20), channel_id=1, source_target_pairs={{0,3},{1,0},{2,1},{3,2},{4,196},{5,197},{6,198},{7,199},{8,11},{9,... | collective-permute-start | bytes 49160 | tf_op jit(solution)/shard_map/ppermute | solution.py:283
  80.1 4.1 %collective-permute-start.4 = (f32[32,128]{1,0:T(8,128)S(1)}, f32[32,128]{1,0:T(8,128)S(1)}, u32[]{:S(2)}, u32[]{:S(2)}) collective-permute-start(f32[32,128]{1,0:T(8,128)S(1)} %bitcast.21), channel_id=1, source_target_pairs={{0,1},{1,2},{2,3},{3,0},{4,68},{5,69},{6,70},{7,71},{8,9},{9,10},{... | collective-permute-start | bytes 49160 | tf_op jit(solution)/shard_map/ppermute | solution.py:283
  85.7 6.5 %collective-permute-start.6 = (f32[32,128]{1,0:T(8,128)S(1)}, f32[32,128]{1,0:T(8,128)S(1)}, u32[]{:S(2)}, u32[]{:S(2)}) collective-permute-start(f32[32,128]{1,0:T(8,128)S(1)} %cross.1), channel_id=1, source_target_pairs={{0,1},{1,2},{2,3},{3,0},{4,68},{5,69},{6,70},{7,71},{8,9},{9,10},{... | collective-permute-start | bytes 49160 | tf_op jit(solution)/shard_map/ppermute | solution.py:287
  103.8 8.0 %copy-start.4 = (f32[32,1,128]{2,1,0:T(1,128)}, f32[32,1,128]{2,1,0:T(1,128)S(1)}, u32[]{:S(2)}) copy-start(f32[32,1,128]{2,1,0:T(1,128)S(1)} %all_to_all.17) | copy-start | bytes 49156
  103.8 8.0 %collective-permute-start.7 = (f32[32,128]{1,0:T(8,128)S(1)}, f32[32,128]{1,0:T(8,128)S(1)}, u32[]{:S(2)}, u32[]{:S(2)}) collective-permute-start(f32[32,128]{1,0:T(8,128)S(1)} %bitcast.29), channel_id=1, source_target_pairs={{0,4},{1,5},{2,6},{3,7},{4,0},{5,1},{6,2},{7,3},{8,12},{9,13},{10,... | collective-permute-start | bytes 49160 | tf_op jit(solution)/shard_map/ppermute | solution.py:292
  111.8 0.6 copy-start.5

commit v3 on v2

v3 whole, which is shorter than its diff:
```python
import jax
import jax.numpy as jnp
from jax import lax
from jax.experimental import pallas as pl
from jax.experimental.pallas import tpu as pltpu
from jax.sharding import PartitionSpec as P

LANES = 128
TILE = 256


def split3(x):
    high = x.astype(jnp.bfloat16)
    rest = x - high.astype(jnp.float32)
    mid = rest.astype(jnp.bfloat16)
    low = (rest - mid.astype(jnp.float32)).astype(jnp.bfloat16)
    return high, mid, low


def iota(shape, dim):
    return lax.broadcasted_iota(jnp.int32, shape, dim)


def dot(a, b, dims):
    return lax.dot_general(a, b, (dims, ((), ())), preferred_element_type=jnp.float32)


BITS = 4096.0
CHUNKS = 4


def slot_of(clusters, core, half):
    owner = clusters // 2
    away = jnp.where(owner // half == core, 0, 1)
    return owner % half + away * half, away


def pack_kernel(where_ref, emb_ref, clu_ref, keep_ref, send_ref, lab_ref, spot_ref, raw_ref, unit_ref, sems):
    rows = emb_ref.shape[0]
    devices = lab_ref.shape[0]
    step = rows // CHUNKS
    copies = [
        pltpu.make_async_copy(
            emb_ref.at[pl.ds(i * step, step)], raw_ref.at[pl.ds(i * step, step)], sems.at[i]
        )
        for i in range(CHUNKS)
    ]
    for copy in copies:
        copy.start()
    half = keep_ref.shape[0] // 16
    width = keep_ref.shape[0] // half
    clusters = clu_ref[...]
    slot, away = slot_of(clusters, where_ref[1], half)
    hot = (iota((2 * half, rows), 0) == slot).astype(jnp.bfloat16)
    before = (iota((rows, rows), 0) < iota((rows, rows), 1)).astype(jnp.bfloat16)
    count = dot(hot, before, ((1,), (0,)))
    rank = jnp.sum(hot.astype(jnp.float32) * count, axis=0, keepdims=True).astype(jnp.int32)
    spot_ref[...] = rank + away * width
    place = slot * width + rank
    bit = (clusters % 2).astype(jnp.float32)
    spots = jnp.where(iota((LANES, rows), 0) == rank, bit, 0.0).astype(jnp.bfloat16)
    target = iota((devices, rows), 0)
    line, last = target // 8, target % 4
    owner = jnp.where(target // 4 % 2 == 0, line, half + line % 8 * 4 + last)
    lab_ref[...] = dot((owner == clusters // 2).astype(jnp.bfloat16), spots, ((1,), (1,)))
    for i, copy in enumerate(copies):
        copy.wait()
        values = raw_ref[i * step : (i + 1) * step, :].astype(jnp.float32)
        scale = lax.rsqrt(jnp.sum(values * values, axis=1, keepdims=True) + 1e-06)
        unit_ref[i * step : (i + 1) * step, :] = (values * scale).astype(jnp.bfloat16)
    for out_ref, base in ((send_ref, rows // 2), (keep_ref, 0)):
        for start in range(0, rows // 2, TILE):
            pick = (iota((TILE, rows), 0) + (base + start) == place).astype(jnp.bfloat16)
            out_ref[start : start + TILE, :] = dot(pick, unit_ref[...], ((1,), (0,))).astype(
                jnp.bfloat16
            )


def smem():
    return pl.BlockSpec(memory_space=pltpu.SMEM)


def vmem():
    return pl.BlockSpec(memory_space=pltpu.VMEM)


def params():
    return pltpu.CompilerParams(vmem_limit_bytes=48 * 2**20)


def pack(where, embeddings, clusters, devices):
    rows, depth = embeddings.shape
    return pl.pallas_call(
        pack_kernel,
        out_shape=(
            jax.ShapeDtypeStruct((rows // 2, depth), jnp.bfloat16),
            jax.ShapeDtypeStruct((rows // 2, depth), jnp.bfloat16),
            jax.ShapeDtypeStruct((devices, LANES), jnp.float32),
            jax.ShapeDtypeStruct((1, rows), jnp.int32),
        ),
        in_specs=[smem(), pl.BlockSpec(memory_space=pl.ANY), vmem()],
        scratch_shapes=[
            pltpu.VMEM((rows, depth), jnp.bfloat16),
            pltpu.VMEM((rows, depth), jnp.bfloat16),
            pltpu.SemaphoreType.DMA((CHUNKS,)),
        ],
        compiler_params=params(),
        name="pack",
    )(where, embeddings, clusters.reshape(1, rows))


def order_of(place, core, part):
    source, flip, rank = place // 32, place // 16 % 2, place % 16
    from_core = jnp.where(flip == 0, core, 1 - core)
    by_row = (source * 2 + from_core) * 4 + part
    by_column = ((part * 8 + source // 4) * 2 + from_core) * 4 + source % 4
    return jnp.where(core == 0, by_row, by_column) * 16 + rank


def row_codes(lab, rows, core, part):
    devices = lab.shape[0]
    order = order_of(iota((1, rows), 1), core, part)
    hot = (iota((devices, rows), 0) == order // 16).astype(jnp.bfloat16)
    spread = dot(lab[:, :16], hot, ((0,), (0,)))
    label = jnp.sum(jnp.where(iota((16, rows), 0) == order % 16, spread, 0.0), axis=0, keepdims=True)
    return label * BITS, label * BITS + order.astype(jnp.float32)


def column_codes(lab, rows, core, part):
    devices = lab.shape[0]
    order = order_of(iota((rows, 1), 0), core, part)
    hot = (iota((rows, devices), 1) == order // 16).astype(jnp.bfloat16)
    spread = dot(hot, lab, ((1,), (0,)))
    kept = jnp.where(iota((rows, LANES), 1) == order % 16, spread, 0.0).astype(jnp.bfloat16)
    label = dot(kept, jnp.ones((LANES, LANES), jnp.bfloat16), ((1,), (0,)))
    return label * BITS + order.astype(jnp.float32)


def scan(best_ref, query_ref, key_ref, floor, ceiling, codes_ref, pick):
    rows = query_ref.shape[0]
    for start in range(0, rows, TILE):
        queries = query_ref[start : start + TILE, :]
        here = slice(start, start + TILE)
        best = best_ref[:, here]
        for low in range(0, rows, TILE):
            if not pick(low, start):
                continue
            sims = dot(key_ref[low : low + TILE, :], queries, ((1,), (1,)))
            codes = jnp.concatenate([codes_ref[low : low + TILE, :]] * (TILE // LANES), axis=1)
            mask = (codes >= floor[:, here]) & (codes < ceiling[:, here])
            found = jnp.max(jnp.where(mask, sims, -1.0), axis=0, keepdims=True)
            best = jnp.maximum(best, found)
        best_ref[:, here] = best


def scan_pair(best_ref, query_ref, key_ref, floor, ceiling, codes_ref, core, part, key_part):
    args = (best_ref, query_ref, key_ref, floor, ceiling, codes_ref)

    @pl.when((core == 0) | (key_part < part))
    def _():
        scan(*args, lambda low, start: low <= start)

    @pl.when((core != 0) & (key_part < part))
    def _():
        scan(*args, lambda low, start: low > start)


def store_groups(out_ref, best):
    sources = out_ref.shape[0]
    rows = best.shape[1]
    width = rows // sources
    mine = iota((sources, rows), 0) == iota((sources, rows), 1) // width
    spots = (iota((rows, LANES), 0) % width == iota((rows, LANES), 1)).astype(jnp.bfloat16)
    total = jnp.zeros((sources, LANES), jnp.float32)
    for piece in split3(best):
        spread = jnp.where(mine, piece.astype(jnp.float32), 0.0).astype(jnp.bfloat16)
        total = total + dot(spread, spots, ((1,), (0,)))
    out_ref[...] = total


def parts_of(where_ref):
    me, core, parts = where_ref[0], where_ref[1], where_ref[2]
    return core, me, lax.rem(me + parts - 1, parts), lax.rem(me + 1, parts)


def alone_kernel(where_ref, own_ref, lab_ref, best_ref, rows_ref, left_ref, right_ref, codes_ref):
    rows = own_ref.shape[0]
    core, me, left, right = parts_of(where_ref)
    lab = lab_ref[...].astype(jnp.bfloat16)
    floor, ceiling = row_codes(lab, rows, core, me)
    side_floor, side_ceiling = row_codes(lab, rows, core, right)
    rows_ref[...] = jnp.concatenate([floor, ceiling, side_floor, side_ceiling] * 2, axis=0)
    left_ref[...] = column_codes(lab, rows, core, left)
    right_ref[...] = column_codes(lab, rows, core, right)
    codes_ref[...] = column_codes(lab, rows, core, me)
    best_ref[...] = jnp.full((1, rows), -1.0, jnp.float32)
    scan(best_ref, own_ref, own_ref, floor, ceiling, codes_ref, lambda low, start: low <= start)


def alone(where, own, lab):
    rows = own.shape[0]
    return pl.pallas_call(
        alone_kernel,
        out_shape=(
            jax.ShapeDtypeStruct((1, rows), jnp.float32),
            jax.ShapeDtypeStruct((8, rows), jnp.float32),
            jax.ShapeDtypeStruct((rows, LANES), jnp.float32),
            jax.ShapeDtypeStruct((rows, LANES), jnp.float32),
        ),
        in_specs=[smem(), vmem(), vmem()],
        out_specs=(vmem(),) * 4,
        scratch_shapes=[pltpu.VMEM((rows, LANES), jnp.float32)],
        compiler_params=params(),
        cost_estimate=pl.CostEstimate(flops=2 * 10**9, bytes_accessed=4 * 10**6, transcendentals=0),
        name="alone",
    )(where, own, lab)


def cross_kernel(where_ref, left_ref, right_ref, rows_ref, left_codes_ref, out_ref, best_ref):
    rows = left_ref.shape[0]
    core, _, left, right = parts_of(where_ref)
    best_ref[...] = jnp.full((1, rows), -1.0, jnp.float32)
    scan_pair(
        best_ref, right_ref, left_ref, rows_ref[2:3, :], rows_ref[3:4, :], left_codes_ref, core, right, left
    )
    store_groups(out_ref, best_ref[...])


def sides_kernel(
    where_ref, alone_ref, own_ref, left_ref, right_ref, rows_ref, left_codes_ref, right_codes_ref,
    out_ref, best_ref,
):
    core, me, left, right = parts_of(where_ref)
    best_ref[...] = alone_ref[...]
    for key_ref, codes_ref, part in ((left_ref, left_codes_ref, left), (right_ref, right_codes_ref, right)):
        scan_pair(
            best_ref, own_ref, key_ref, rows_ref[0:1, :], rows_ref[1:2, :], codes_ref, core, me, part
        )
    store_groups(out_ref, best_ref[...])


def sims_call(kernel, name, groups, where, arrays, rows):
    return pl.pallas_call(
        kernel,
        out_shape=jax.ShapeDtypeStruct((groups, LANES), jnp.float32),
        in_specs=[smem()] + [vmem()] * len(arrays),
        out_specs=vmem(),
        scratch_shapes=[pltpu.VMEM((1, rows), jnp.float32)],
        compiler_params=params(),
        name=name,
    )(where, *arrays)


def unpack_kernel(where_ref, clu_ref, spot_ref, near_ref, far_ref, out_ref):
    half = near_ref.shape[0]
    rows = clu_ref.shape[1]
    slot, _ = slot_of(clu_ref[...], where_ref[1], half)
    hot = (iota((2 * half, rows), 0) == slot).astype(jnp.bfloat16)
    results = jnp.concatenate([near_ref[:, :32], far_ref[:, :32]], axis=0)
    total = jnp.zeros((32, rows), jnp.float32)
    for piece in split3(results):
        total = total + dot(piece, hot, ((0,), (0,)))
    mine = iota((32, rows), 0) == spot_ref[...]
    out_ref[...] = jnp.sum(jnp.where(mine, total, 0.0), axis=0, keepdims=True)


def unpack(where, clusters, spot, near, far):
    rows = clusters.shape[0]
    return pl.pallas_call(
        unpack_kernel,
        out_shape=jax.ShapeDtypeStruct((1, rows), jnp.float32),
        in_specs=[smem()] + [vmem()] * 4,
        out_specs=vmem(),
        name="unpack",
    )(where, clusters.reshape(1, rows), spot, near, far).reshape(rows)


AXES = ("dp", "help")
NY, NZ, NX = 4, 8, 4


def device(y, z, core, x):
    return ((y % NY * NZ + z % NZ) * 2 + core) * NX + x % NX


EVERY = [(y, z, c, x) for y in range(NY) for z in range(NZ) for c in range(2) for x in range(NX)]
SWAP = [(device(y, z, c, x), device(y, z, 1 - c, x)) for y, z, c, x in EVERY]
GROUPS = [[device(y, z, 0, x) for y in range(NY) for z in range(NZ)] for x in range(NX)] + [
    [device(y, z, 1, x) for z in range(NZ) for x in range(NX)] for y in range(NY)
]


def aside(step):
    return [
        (device(y, z, c, x), device(y, z, c, x + step) if c == 0 else device(y + step, z, c, x))
        for y, z, c, x in EVERY
    ]


def exchange(array):
    return lax.all_to_all(
        array, AXES, split_axis=0, concat_axis=0, axis_index_groups=GROUPS, tiled=True
    )


def shards(embeddings, clusters, send_order):
    rows, depth = embeddings.shape
    owners, helpers = lax.axis_size("dp"), lax.axis_size("help")
    half = owners // 2
    width = rows // owners
    devices = owners * helpers
    dp, x = lax.axis_index("dp"), lax.axis_index("help")
    core, y = dp % 2, dp // (2 * NZ)
    where = jnp.stack([jnp.where(core == 0, x, y), core, jnp.int32(NX)])
    keep, send, labels, spot = pack(where, embeddings, clusters, devices)
    got = lax.ppermute(send, AXES, SWAP)
    outgoing = jnp.concatenate(
        [keep.reshape(half, width, depth), got.reshape(half, width, depth)], axis=1
    )
    own = exchange(outgoing).reshape(rows, depth)
    left, right = lax.ppermute(own, AXES, aside(1)), lax.ppermute(own, AXES, aside(-1))
    labels = lax.all_to_all(
        labels.reshape(devices, 1, LANES), AXES, split_axis=0, concat_axis=0, tiled=True
    ).reshape(devices, LANES)
    best, codes, left_codes, right_codes = alone(where, own, labels)
    arrays = (left, right, codes, left_codes)
    cross = sims_call(cross_kernel, "cross", half, where, arrays, rows)
    cross = lax.ppermute(cross, AXES, aside(1))
    arrays = (best, own, left, right, codes, left_codes, right_codes)
    best = sims_call(sides_kernel, "sides", half, where, arrays, rows)
    best = jnp.maximum(best, cross)
    near = exchange(best.reshape(half, 1, LANES)).reshape(half, LANES)
    far = lax.ppermute(near, AXES, SWAP)
    return unpack(where, clusters, spot, near, far)


def solution(mesh):
    return jax.shard_map(
        shards,
        mesh=mesh,
        in_specs=(P(("dp", "help"), None), P(("dp", "help")), P(("dp", "help"))),
        out_specs=P(("dp", "help")),
        check_vma=False,
    )
```

time: 114 us -> 119 us (1.044)
  blocking collectives: 74.9 us -> 85.4 us
  waiting for transfers between devices: 7 us -> 3.06 us
  starting transfers between devices: 18.8 us -> 15.1 us
  Pallas kernels: 10.5 us -> 12.2 us
    all_to_all x0 -> x1, blocking collectives: none -> 24.6 us  [shards(): lax.all_to_all(labels.reshape(devices, 1, LANES), AXES, split_axis=0, con...]
    all_to_all x3 -> x2, blocking collectives: 74.9 us -> 60.8 us  [exchange(): lax.all_to_all(array, AXES, split_axis=0, concat_axis=0, axis_index_group...]
    ppermute x4 -> x1, waiting for transfers between devices: 6.15 us -> 1.91 us  [shards(): got = lax.ppermute(send, AXES, SWAP)]
    ppermute x4 -> x1, starting transfers between devices: 6.41 us -> 3.33 us  [shards(): got = lax.ppermute(send, AXES, SWAP)]
    pallas_call x1, Pallas kernels: 3 us -> 4.36 us  [pack(): pl.pallas_call(pack_kernel, out_shape=(jax.ShapeDtypeStruct((rows // 2, d...]
  transfers between devices with their start and end apart: 8 -> 5, of which waited for: 5 -> 3; matrix products, arithmetic and copies ran while one was open for 0% -> 0% of each run, Pallas kernels for 4% -> 4%
where the time goes in v3:
time: 119 us
  blocking collectives  85.4 us (72%)
  starting transfers between devices  15.1 us (13%)
  Pallas kernels  12.2 us (10%)
  waiting for transfers between devices  3.06 us (3%)
  local copies, waits for them, and re-layouts  2.71 us (2%)
    all_to_all x2, blocking collectives, exchange(): lax.all_to_all(array, AXES, split_axis=0, concat_axis=0, axis_index_group...  60.8 us
    all_to_all x1, blocking collectives, shards(): lax.all_to_all(labels.reshape(devices, 1, LANES), AXES, split_axis=0, con...  24.6 us
    ppermute x1, starting transfers between devices, shards(): far = lax.ppermute(near, AXES, SWAP)  6.14 us
    pallas_call x1, Pallas kernels, pack(): pl.pallas_call(pack_kernel, out_shape=(jax.ShapeDtypeStruct((rows // 2, d...  4.36 us
    pallas_call x1, Pallas kernels, alone(): pl.pallas_call(alone_kernel, out_shape=(jax.ShapeDtypeStruct((1, rows), j...  4.36 us
    ppermute x1, starting transfers between devices, shards(): got = lax.ppermute(send, AXES, SWAP)  3.33 us
    ppermute x1, starting transfers between devices, shards(): lax.ppermute(own, AXES, aside(-1))  2.94 us
    ppermute x1, starting transfers between devices, shards(): cross = lax.ppermute(cross, AXES, aside(1))  2.73 us
  transfers between devices with their start and end apart: 5, of which 3 were waited for; matrix products, arithmetic and copies ran while one was open for 0% of the time, Pallas kernels for 4%

profile of v3, /device:TPU:1, one launch (start us, length us, event | category | flops | bytes accessed | tf_op | source)
XLA Modules:
  0.0 118.9 jit_solution(4674800856673147262)
XLA Ops:
  0.0 0.1 pad_add_fusion.where_ref
  0.1 0.0 copy-start.2
  0.1 0.0 copy-start
  0.1 1.4 %copy-done = bf16[1024,768]{1,0:T(8,128)(2,1)S(1)} copy-done((bf16[1024,768]{1,0:T(8,128)(2,1)S(1)}, bf16[1024,768]{1,0:T(8,128)(2,1)}, u32[]{:S(2)}) %copy-start) | copy-done | bytes 1572888
  1.5 0.0 copy-start.1
  1.5 0.7 copy-done.1
  2.2 4.4 %pack.1 = (bf16[512,768]{1,0:T(8,128)(2,1)S(1)}, bf16[512,768]{1,0:T(8,128)(2,1)S(1)}, f32[256,128]{1,0:T(8,128)S(1)}, s32[1,1024]{1,0:T(1,128)S(1)}) custom-call(s32[3]{0:T(128)S(1)} %pad_add_fusion.where_ref, bf16[1024,768]{1,0:T(8,128)(2,1)S(1)} %copy-done, s32[1,1024]{1,0:T(1,128)S(1)} %bitcast.23), custom_call_target="tpu_custom_call" | custom-call | tf_op jit(solution)/shard_map/pack/pallas_call | solution.py:93
  6.5 0.0 copy-start.3
  6.6 3.3 %collective-permute-start = (bf16[512,768]{1,0:T(8,128)(2,1)S(1)}, bf16[512,768]{1,0:T(8,128)(2,1)S(1)}, u32[]{:S(2)}, u32[]{:S(2)}) collective-permute-start(bf16[512,768]{1,0:T(8,128)(2,1)S(1)} %get-tuple-element.15), channel_id=1, source_target_pairs={{0,4},{1,5},{2,6},{3,7},{4,0},{5,1},{6,2},{7,3},{8,12},{9,13},{10,... | collective-permute-start | bytes 2359304 | tf_op jit(solution)/shard_map/ppermute | solution.py:316
  9.9 1.9 %collective-permute-done = bf16[512,768]{1,0:T(8,128)(2,1)S(1)} collective-permute-done((bf16[512,768]{1,0:T(8,128)(2,1)S(1)}, bf16[512,768]{1,0:T(8,128)(2,1)S(1)}, u32[]{:S(2)}, u32[]{:S(2)}) %collective-permute-start) | collective-permute-done | bytes 786464 | tf_op jit(solution)/shard_map/ppermute | solution.py:316
  11.8 0.2 pad_maximum_fusion
  12.0 0.0 copy-done.3
  12.0 47.9 %all_to_all.15 = bf16[32,32,768]{2,1,0:T(8,128)(2,1)S(1)} all-to-all(bf16[32,32,768]{2,1,0:T(8,128)(2,1)S(1)} %pad_maximum_fusion), channel_id=1, replica_groups={{0,8,16,24,32,40,48,56,64,72,80,88,96,104,112,120,128,136,144,152,160,1..., dimensions={0} | all-to-all | bytes 3145728 | tf_op jit(solution)/shard_map/all_to_all | solution.py:301
  59.9 2.9 %collective-permute-start.2 = (bf16[1024,768]{1,0:T(8,128)(2,1)S(1)}, bf16[1024,768]{1,0:T(8,128)(2,1)S(1)}, u32[]{:S(2)}, u32[]{:S(2)}) collective-permute-start(bf16[1024,768]{1,0:T(8,128)(2,1)S(1)} %bitcast.15), channel_id=1, source_target_pairs={{0,3},{1,0},{2,1},{3,2},{4,196},{5,197},{6,198},{7,199},{8,11},{9,... | collective-permute-start | bytes 4718600 | tf_op jit(solution)/shard_map/ppermute | solution.py:321
  62.9 0.0 collective-permute-start.1
  62.9 24.6 %all_to_all.16 = f32[256,1,128]{2,1,0:T(1,128)S(1)} all-to-all(f32[256,1,128]{2,1,0:T(1,128)S(1)} %bitcast.20), channel_id=1, replica_groups=mesh['dp'=64,'help'=4] {'dp','help'}, dimensions={0} | all-to-all | bytes 262144 | tf_op jit(solution)/shard_map/all_to_all | solution.py:322
  87.4 4.4 %alone.1 = (f32[1,1024]{1,0:T(1,128)S(1)}, f32[8,1024]{1,0:T(8,128)S(1)}, f32[1024,128]{1,0:T(8,128)S(1)}, f32[1024,128]{1,0:T(8,128)S(1)}) custom-call(s32[3]{0:T(128)S(1)} %pad_add_fusion.where_ref, bf16[1024,768]{1,0:T(8,128)(2,1)S(1)} %bitcast.17, f32[256,128]{1,0:T(8,128)S(1)} %bitcast.21), custom_call_target="tpu_custom_call" | custom-call | flops 2000000000 | bytes 4000000 | tf_op jit(solution)/shard_map/alone/pallas_call | solution.py:202
  91.8 0.0 collective-permute-done.2.right_ref
  91.8 0.0 collective-permute-done.1.left_ref
  91.8 1.0 cross.1
  92.8 2.7 %collective-permute-start.3 = (f32[32,128]{1,0:T(8,128)S(1)}, f32[32,128]{1,0:T(8,128)S(1)}, u32[]{:S(2)}, u32[]{:S(2)}) collective-permute-start(f32[32,128]{1,0:T(8,128)S(1)} %cross.1), channel_id=1, source_target_pairs={{0,1},{1,2},{2,3},{3,0},{4,68},{5,69},{6,70},{7,71},{8,9},{9,10},{... | collective-permute-start | bytes 49160 | tf_op jit(solution)/shard_map/ppermute | solution.py:328
  95.6 0.0 copy-done.2
  95.6 0.8 sides.1
  96.4 0.3 collective-permute-done.3
  96.7 12.9 %all_to_all.17 = f32[32,1,128]{2,1,0:T(1,128)S(1)} all-to-all(f32[32,1,128]{2,1,0:T(1,128)S(1)} %bitcast.25), channel_id=1, replica_groups={{0,8,16,24,32,40,48,56,64,72,80,88,96,104,112,120,128,136,144,152,160,1..., dimensions={0} | all-to-all | bytes 32768 | tf_op jit(solution)/shard_map/all_to_all | solution.py:301
  109.7 0.0 copy-start.4
  109.7 6.1 %collective-permute-start.4 = (f32[32,128]{1,0:T(8,128)S(1)}, f32[32,128]{1,0:T(8,128)S(1)}, u32[]{:S(2)}, u32[]{:S(2)}) collective-permute-start(f32[32,128]{1,0:T(8,128)S(1)} %bitcast.26), channel_id=1, source_target_pairs={{0,4},{1,5},{2,6},{3,7},{4,0},{5,1},{6,2},{7,3},{8,12},{9,13},{10,... | collective-permute-start | bytes 49160 | tf_op jit(solution)/shard_map/ppermute | solution.py:333
  115.8 0.8 collective-permute-done.4.far_ref
  116.6 0.0 copy-start.5
  116.6 0.0 copy-done.4
  116.6 0.6 copy-done.5
  117.2 1.6 %unpack.1 = f32[1,1024]{1,0:T(1,128)} custom-call(s32[3]{0:T(128)} %copy-done.2, s32[1,1024]{1,0:T(1,128)} %bitcast.22, s32[1,1024]{1,0:T(1,128)} %copy-done.3, f32[32,128]{1,0:T(8,128)} %bitcast.27, f32[32,128]{1,0:T(8,128)} %copy-done.5), custom_call_target="tpu_custom_call" | custom-call | tf_op jit(solution)/shard_map/unpack/pallas_call | solution.py:269
  (1 shorter events, 0.0 us)
Async XLA Ops:
  0.1 95.5 %copy-start.2 = (s32[3]{0:T(128)}, s32[3]{0:T(128)S(1)}, u32[]{:S(2)}) copy-start(s32[3]{0:T(128)S(1)} %pad_add_fusion.where_ref) | copy-start | bytes 40
  0.1 1.4 %copy-start = (bf16[1024,768]{1,0:T(8,128)(2,1)S(1)}, bf16[1024,768]{1,0:T(8,128)(2,1)}, u32[]{:S(2)}) copy-start(bf16[1024,768]{1,0:T(8,128)(2,1)} %emb_ref.1) | copy-start | bytes 4718596
  1.5 0.7 copy-start.1
  6.5 5.4 %copy-start.3 = (s32[1,1024]{1,0:T(1,128)}, s32[1,1024]{1,0:T(1,128)S(1)}, u32[]{:S(2)}) copy-start(s32[1,1024]{1,0:T(1,128)S(1)} %get-tuple-element.13.spot_ref) | copy-start | bytes 12292
  6.6 5.2 %collective-permute-start = (bf16[512,768]{1,0:T(8,128)(2,1)S(1)}, bf16[512,768]{1,0:T(8,128)(2,1)S(1)}, u32[]{:S(2)}, u32[]{:S(2)}) collective-permute-start(bf16[512,768]{1,0:T(8,128)(2,1)S(1)} %get-tuple-element.15), channel_id=1, source_target_pairs={{0,4},{1,5},{2,6},{3,7},{4,0},{5,1},{6,2},{7,3},{8,12},{9,13},{10,... | collective-permute-start | bytes 2359304 | tf_op jit(solution)/shard_map/ppermute | solution.py:316
  59.9 31.9 %collective-permute-start.2 = (bf16[1024,768]{1,0:T(8,128)(2,1)S(1)}, bf16[1024,768]{1,0:T(8,128)(2,1)S(1)}, u32[]{:S(2)}, u32[]{:S(2)}) collective-permute-start(bf16[1024,768]{1,0:T(8,128)(2,1)S(1)} %bitcast.15), channel_id=1, source_target_pairs={{0,3},{1,0},{2,1},{3,2},{4,196},{5,197},{6,198},{7,199},{8,11},{9,... | collective-permute-start | bytes 4718600 | tf_op jit(solution)/shard_map/ppermute | solution.py:321
  62.9 29.0 %collective-permute-start.1 = (bf16[1024,768]{1,0:T(8,128)(2,1)S(1)}, bf16[1024,768]{1,0:T(8,128)(2,1)S(1)}, u32[]{:S(2)}, u32[]{:S(2)}) collective-permute-start(bf16[1024,768]{1,0:T(8,128)(2,1)S(1)} %bitcast.16), channel_id=1, source_target_pairs={{0,1},{1,2},{2,3},{3,0},{4,68},{5,69},{6,70},{7,71},{8,9},{9,10},{... | collective-permute-start | bytes 4718600 | tf_op jit(solution)/shard_map/ppermute | solution.py:321
  92.8 3.9 %collective-permute-start.3 = (f32[32,128]{1,0:T(8,128)S(1)}, f32[32,128]{1,0:T(8,128)S(1)}, u32[]{:S(2)}, u32[]{:S(2)}) collective-permute-start(f32[32,128]{1,0:T(8,128)S(1)} %cross.1), channel_id=1, source_target_pairs={{0,1},{1,2},{2,3},{3,0},{4,68},{5,69},{6,70},{7,71},{8,9},{9,10},{... | collective-permute-start | bytes 49160 | tf_op jit(solution)/shard_map/ppermute | solution.py:328
  109.7 7.0 %copy-start.4 = (f32[32,1,128]{2,1,0:T(1,128)}, f32[32,1,128]{2,1,0:T(1,128)S(1)}, u32[]{:S(2)}) copy-start(f32[32,1,128]{2,1,0:T(1,128)S(1)} %all_to_all.17) | copy-start | bytes 49156
  109.7 7.0 %collective-permute-start.4 = (f32[32,128]{1,0:T(8,128)S(1)}, f32[32,128]{1,0:T(8,128)S(1)}, u32[]{:S(2)}, u32[]{:S(2)}) collective-permute-start(f32[32,128]{1,0:T(8,128)S(1)} %bitcast.26), channel_id=1, source_target_pairs={{0,4},{1,5},{2,6},{3,7},{4,0},{5,1},{6,2},{7,3},{8,12},{9,13},{10,... | collective-permute-start | bytes 49160 | tf_op jit(solution)/shard_map/ppermute | solution.py:333
  116.6 0.6 copy-start.5

commit v4 on v3

--- a/solution.py
+++ b/solution.py
@@ -35,9 +35,10 @@
     return owner % half + away * half, away
 
 
-def pack_kernel(where_ref, emb_ref, clu_ref, keep_ref, send_ref, lab_ref, spot_ref, raw_ref, unit_ref, sems):
+def pack_kernel(
+    where_ref, emb_ref, clu_ref, keep_ref, send_ref, keep_lab_ref, send_lab_ref, spot_ref, raw_ref, unit_ref, sems
+):
     rows = emb_ref.shape[0]
-    devices = lab_ref.shape[0]
     step = rows // CHUNKS
     copies = [
         pltpu.make_async_copy(
@@ -47,7 +48,7 @@
     ]
     for copy in copies:
         copy.start()
-    half = keep_ref.shape[0] // 16
+    half = keep_lab_ref.shape[0]
     width = keep_ref.shape[0] // half
     clusters = clu_ref[...]
     slot, away = slot_of(clusters, where_ref[1], half)
@@ -55,14 +56,14 @@
     before = (iota((rows, rows), 0) < iota((rows, rows), 1)).astype(jnp.bfloat16)
     count = dot(hot, before, ((1,), (0,)))
     rank = jnp.sum(hot.astype(jnp.float32) * count, axis=0, keepdims=True).astype(jnp.int32)
-    spot_ref[...] = rank + away * width
+    spot = rank + away * width
+    spot_ref[...] = spot
     place = slot * width + rank
     bit = (clusters % 2).astype(jnp.float32)
-    spots = jnp.where(iota((LANES, rows), 0) == rank, bit, 0.0).astype(jnp.bfloat16)
-    target = iota((devices, rows), 0)
-    line, last = target // 8, target % 4
-    owner = jnp.where(target // 4 % 2 == 0, line, half + line % 8 * 4 + last)
-    lab_ref[...] = dot((owner == clusters // 2).astype(jnp.bfloat16), spots, ((1,), (1,)))
+    spots = jnp.where(iota((LANES, rows), 0) == spot, bit, 0.0).astype(jnp.bfloat16)
+    labels = dot(hot, spots, ((1,), (1,)))
+    keep_lab_ref[...] = labels[:half]
+    send_lab_ref[...] = labels[half:]
     for i, copy in enumerate(copies):
         copy.wait()
         values = raw_ref[i * step : (i + 1) * step, :].astype(jnp.float32)
@@ -84,18 +85,19 @@
     return pl.BlockSpec(memory_space=pltpu.VMEM)
 
 
-def params():
-    return pltpu.CompilerParams(vmem_limit_bytes=48 * 2**20)
-
-
-def pack(where, embeddings, clusters, devices):
+def params(size=48):
+    return pltpu.CompilerParams(vmem_limit_bytes=size * 2**20)
+
+
+def pack(where, embeddings, clusters, half):
     rows, depth = embeddings.shape
     return pl.pallas_call(
         pack_kernel,
         out_shape=(
             jax.ShapeDtypeStruct((rows // 2, depth), jnp.bfloat16),
             jax.ShapeDtypeStruct((rows // 2, depth), jnp.bfloat16),
-            jax.ShapeDtypeStruct((devices, LANES), jnp.float32),
+            jax.ShapeDtypeStruct((half, LANES), jnp.float32),
+            jax.ShapeDtypeStruct((half, LANES), jnp.float32),
             jax.ShapeDtypeStruct((1, rows), jnp.int32),
         ),
         in_specs=[smem(), pl.BlockSpec(memory_space=pl.ANY), vmem()],
@@ -104,7 +106,7 @@
             pltpu.VMEM((rows, depth), jnp.bfloat16),
             pltpu.SemaphoreType.DMA((CHUNKS,)),
         ],
-        compiler_params=params(),
+        compiler_params=params(60),
         name="pack",
     )(where, embeddings, clusters.reshape(1, rows))
 
@@ -118,22 +120,26 @@
 
 
 def row_codes(lab, rows, core, part):
-    devices = lab.shape[0]
-    order = order_of(iota((1, rows), 1), core, part)
-    hot = (iota((devices, rows), 0) == order // 16).astype(jnp.bfloat16)
-    spread = dot(lab[:, :16], hot, ((0,), (0,)))
-    label = jnp.sum(jnp.where(iota((16, rows), 0) == order % 16, spread, 0.0), axis=0, keepdims=True)
-    return label * BITS, label * BITS + order.astype(jnp.float32)
+    sources = lab.shape[0]
+    width = rows // sources
+    place = iota((1, rows), 1)
+    hot = (iota((sources, rows), 0) == place // width).astype(jnp.bfloat16)
+    spread = dot(lab[:, :width], hot, ((0,), (0,)))
+    chosen = iota((width, rows), 0) == place % width
+    label = jnp.sum(jnp.where(chosen, spread, 0.0), axis=0, keepdims=True)
+    return label * BITS, label * BITS + order_of(place, core, part).astype(jnp.float32)
 
 
 def column_codes(lab, rows, core, part):
-    devices = lab.shape[0]
-    order = order_of(iota((rows, 1), 0), core, part)
-    hot = (iota((rows, devices), 1) == order // 16).astype(jnp.bfloat16)
+    sources = lab.shape[0]
+    width = rows // sources
+    place = iota((rows, 1), 0)
+    hot = (iota((rows, sources), 1) == place // width).astype(jnp.bfloat16)
     spread = dot(hot, lab, ((1,), (0,)))
-    kept = jnp.where(iota((rows, LANES), 1) == order % 16, spread, 0.0).astype(jnp.bfloat16)
+    chosen = iota((rows, LANES), 1) == place % width
+    kept = jnp.where(chosen, spread, 0.0).astype(jnp.bfloat16)
     label = dot(kept, jnp.ones((LANES, LANES), jnp.bfloat16), ((1,), (0,)))
-    return label * BITS + order.astype(jnp.float32)
+    return label * BITS + order_of(iota((rows, LANES), 0), core, part).astype(jnp.float32)
 
 
 def scan(best_ref, query_ref, key_ref, floor, ceiling, codes_ref, pick):
@@ -186,12 +192,12 @@
 def alone_kernel(where_ref, own_ref, lab_ref, best_ref, rows_ref, left_ref, right_ref, codes_ref):
     rows = own_ref.shape[0]
     core, me, left, right = parts_of(where_ref)
-    lab = lab_ref[...].astype(jnp.bfloat16)
+    lab, left_lab, right_lab = (lab_ref[:, i, :].astype(jnp.bfloat16) for i in range(3))
     floor, ceiling = row_codes(lab, rows, core, me)
-    side_floor, side_ceiling = row_codes(lab, rows, core, right)
+    side_floor, side_ceiling = row_codes(right_lab, rows, core, right)
     rows_ref[...] = jnp.concatenate([floor, ceiling, side_floor, side_ceiling] * 2, axis=0)
-    left_ref[...] = column_codes(lab, rows, core, left)
-    right_ref[...] = column_codes(lab, rows, core, right)
+    left_ref[...] = column_codes(left_lab, rows, core, left)
+    right_ref[...] = column_codes(right_lab, rows, core, right)
     codes_ref[...] = column_codes(lab, rows, core, me)
     best_ref[...] = jnp.full((1, rows), -1.0, jnp.float32)
     scan(best_ref, own_ref, own_ref, floor, ceiling, codes_ref, lambda low, start: low <= start)
@@ -297,6 +303,13 @@
     ]
 
 
+def across(step):
+    return [
+        (device(y, z, c, x), device(y, z, 0, x + step) if c == 1 else device(y + step, z, 1, x))
+        for y, z, c, x in EVERY
+    ]
+
+
 def exchange(array):
     return lax.all_to_all(
         array, AXES, split_axis=0, concat_axis=0, axis_index_groups=GROUPS, tiled=True
@@ -305,23 +318,27 @@
 
 def shards(embeddings, clusters, send_order):
     rows, depth = embeddings.shape
-    owners, helpers = lax.axis_size("dp"), lax.axis_size("help")
+    owners = lax.axis_size("dp")
     half = owners // 2
     width = rows // owners
-    devices = owners * helpers
     dp, x = lax.axis_index("dp"), lax.axis_index("help")
     core, y = dp % 2, dp // (2 * NZ)
     where = jnp.stack([jnp.where(core == 0, x, y), core, jnp.int32(NX)])
-    keep, send, labels, spot = pack(where, embeddings, clusters, devices)
+    keep, send, keep_lab, send_lab, spot = pack(where, embeddings, clusters, half)
     got = lax.ppermute(send, AXES, SWAP)
+    labels = [keep_lab + lax.ppermute(send_lab, AXES, SWAP)]
+    for step in (1, -1):
+        labels.append(
+            lax.ppermute(keep_lab, AXES, aside(step)) + lax.ppermute(send_lab, AXES, across(step))
+        )
+    labels = jnp.stack(labels + [jnp.zeros_like(keep_lab)], axis=1)
     outgoing = jnp.concatenate(
         [keep.reshape(half, width, depth), got.reshape(half, width, depth)], axis=1
     )
+    outgoing, labels = lax.optimization_barrier((outgoing, labels))
     own = exchange(outgoing).reshape(rows, depth)
     left, right = lax.ppermute(own, AXES, aside(1)), lax.ppermute(own, AXES, aside(-1))
-    labels = lax.all_to_all(
-        labels.reshape(devices, 1, LANES), AXES, split_axis=0, concat_axis=0, tiled=True
-    ).reshape(devices, LANES)
+    labels = exchange(labels)
     best, codes, left_codes, right_codes = alone(where, own, labels)
     arrays = (left, right, codes, left_codes)
     cross = sims_call(cross_kernel, "cross", half, where, arrays, rows)

time: 119 us -> 117 us (0.983)
  blocking collectives: 85.4 us -> 75.8 us
  waiting for transfers between devices: 3.06 us -> 7.22 us
  starting transfers between devices: 15.1 us -> 19.1 us
  other arithmetic: 0.25 us -> 2.82 us
  local copies, waits for them, and re-layouts: 2.71 us -> 0.68 us
    all_to_all x1 -> x0, blocking collectives: 24.6 us -> none  [shards(): lax.all_to_all(labels.reshape(devices, 1, LANES), AXES, split_axis=0, con...]
    all_to_all x2 -> x3, blocking collectives: 60.8 us -> 75.8 us  [exchange(): lax.all_to_all(array, AXES, split_axis=0, concat_axis=0, axis_index_group...]
    ppermute x0 -> x5, starting transfers between devices: none -> 4.54 us  [the longest x2 2.29 us: shards(): lax.ppermute(keep_lab, AXES, aside(step))]
    ppermute x1, starting transfers between devices: 2.94 us -> 0.01 us  [shards(): lax.ppermute(own, AXES, aside(-1))]
    ppermute x0 -> x5, waiting for transfers between devices: none -> 2.49 us  [the longest x2 1.81 us: shards(): lax.ppermute(send_lab, AXES, across(step))]
    ppermute x1, waiting for transfers between devices: 0.01 us -> 2.11 us  [shards(): lax.ppermute(own, AXES, aside(-1))]
    unnamed x12 -> x6, local copies, waits for them, and re-layouts: 2.71 us -> 0.6 us
    ppermute x1, waiting for transfers between devices: 1.91 us -> 0.01 us  [shards(): got = lax.ppermute(send, AXES, SWAP)]
  transfers between devices with their start and end apart: 5 -> 10, of which waited for: 3 -> 6; matrix products, arithmetic and copies ran while one was open for 0% -> 1% of each run, Pallas kernels for 4% -> 3%
where the time goes in v4:
time: 117 us
  blocking collectives  75.8 us (65%)
  starting transfers between devices  19.1 us (16%)
  Pallas kernels  11.4 us (10%)
  waiting for transfers between devices  7.22 us (6%)
  other arithmetic  2.82 us (2%)
    all_to_all x3, blocking collectives, exchange(): lax.all_to_all(array, AXES, split_axis=0, concat_axis=0, axis_index_group...  75.8 us
    ppermute x1, starting transfers between devices, shards(): far = lax.ppermute(near, AXES, SWAP)  7.28 us
    pallas_call x1, Pallas kernels, pack(): pl.pallas_call(pack_kernel, out_shape=(jax.ShapeDtypeStruct((rows // 2, d...  5.01 us
    ppermute x1, starting transfers between devices, shards(): got = lax.ppermute(send, AXES, SWAP)  3.33 us
    pallas_call x1, Pallas kernels, alone(): pl.pallas_call(alone_kernel, out_shape=(jax.ShapeDtypeStruct((1, rows), j...  2.9 us
    ppermute x1, starting transfers between devices, shards(): cross = lax.ppermute(cross, AXES, aside(1))  2.47 us
  transfers between devices with their start and end apart: 10, of which 6 were waited for; matrix products, arithmetic and copies ran while one was open for 1% of the time, Pallas kernels for 3%

profile of v4, /device:TPU:1, one launch (start us, length us, event | category | flops | bytes accessed | tf_op | source)
XLA Modules:
  0.0 117.1 jit_solution(493162926012592609)
XLA Ops:
  0.0 0.7 pad_add_fusion.where_ref
  0.7 5.0 %pack.1 = (bf16[512,768]{1,0:T(8,128)(2,1)}, bf16[512,768]{1,0:T(8,128)(2,1)}, f32[32,128]{1,0:T(8,128)}, f32[32,128]{1,0:T(8,128)}, s32[1,1024]{1,0:T(1,128)}) custom-call(s32[3]{0:T(128)} %pad_add_fusion.where_ref, bf16[1024,768]{1,0:T(8,128)(2,1)} %emb_ref.1, s32[1,1024]{1,0:T(1,128)} %bitcast.27), custom_call_target="tpu_custom_call" | custom-call | tf_op jit(solution)/shard_map/pack/pallas_call | solution.py:94
  5.7 3.3 %collective-permute-start = (bf16[512,768]{1,0:T(8,128)(2,1)}, bf16[512,768]{1,0:T(8,128)(2,1)S(1)}, u32[]{:S(2)}, u32[]{:S(2)}) collective-permute-start(bf16[512,768]{1,0:T(8,128)(2,1)} %get-tuple-element.18), channel_id=1, source_target_pairs={{0,4},{1,5},{2,6},{3,7},{4,0},{5,1},{6,2},{7,3},{8,12},{9,13},{10,... | collective-permute-start | bytes 2359304 | tf_op jit(solution)/shard_map/ppermute | solution.py:328
  9.0 0.1 collective-permute-start.1
  9.1 1.0 collective-permute-start.4
  10.1 0.9 collective-permute-start.5
  11.0 1.3 %collective-permute-start.2 = (f32[32,128]{1,0:T(8,128)}, f32[32,128]{1,0:T(8,128)S(1)}, u32[]{:S(2)}, u32[]{:S(2)}) collective-permute-start(f32[32,128]{1,0:T(8,128)} %get-tuple-element.19), channel_id=1, source_target_pairs={{0,1},{1,2},{2,3},{3,0},{4,68},{5,69},{6,70},{7,71},{8,9},{9,10},{... | collective-permute-start | bytes 49160 | tf_op jit(solution)/shard_map/ppermute | solution.py:332
  12.3 0.0 collective-permute-done.1
  12.3 1.3 %collective-permute-start.3 = (f32[32,128]{1,0:T(8,128)}, f32[32,128]{1,0:T(8,128)S(1)}, u32[]{:S(2)}, u32[]{:S(2)}) collective-permute-start(f32[32,128]{1,0:T(8,128)} %get-tuple-element.20), channel_id=1, source_target_pairs={{0,68},{1,69},{2,70},{3,71},{4,1},{5,2},{6,3},{7,0},{8,76},{9,77},... | collective-permute-start | bytes 49160 | tf_op jit(solution)/shard_map/ppermute | solution.py:332
  13.6 0.1 pad.3.clone
  13.6 0.7 add.15
  14.4 0.0 collective-permute-done.4
  14.4 0.0 collective-permute-done.5
  14.4 0.7 collective-permute-done.2
  15.1 1.8 %collective-permute-done.3 = f32[32,128]{1,0:T(8,128)S(1)} collective-permute-done((f32[32,128]{1,0:T(8,128)}, f32[32,128]{1,0:T(8,128)S(1)}, u32[]{:S(2)}, u32[]{:S(2)}) %collective-permute-start.3) | collective-permute-done | bytes 16416 | tf_op jit(solution)/shard_map/ppermute | solution.py:332
  16.9 0.1 maximum_maximum_fusion
  17.0 0.0 collective-permute-done
  17.0 1.3 %pad_maximum_fusion = bf16[32,32,768]{2,1,0:T(8,128)(2,1)S(1)} fusion(bf16[32,16,768]{2,1,0:T(8,128)(2,1)S(1)} %bitcast.20, bf16[32,16,768]{2,1,0:T(8,128)(2,1)} %bitcast.19), kind=kLoop, calls=%fused_computation | loop fusion | flops 3145728 | bytes 3145728 | tf_op jit(solution)/shard_map/concatenate | solution.py:335
  18.3 0.0 copy-start
  18.3 48.7 %all_to_all.15 = bf16[32,32,768]{2,1,0:T(8,128)(2,1)S(1)} all-to-all(bf16[32,32,768]{2,1,0:T(8,128)(2,1)S(1)} %pad_maximum_fusion), channel_id=1, replica_groups={{0,8,16,24,32,40,48,56,64,72,80,88,96,104,112,120,128,136,144,152,160,1..., dimensions={0} | all-to-all | bytes 3145728 | tf_op jit(solution)/shard_map/all_to_all | solution.py:314
  67.0 0.0 collective-permute-start.7
  67.0 1.5 %collective-permute-start.6 = (bf16[1024,768]{1,0:T(8,128)(2,1)S(1)}, bf16[1024,768]{1,0:T(8,128)(2,1)S(1)}, u32[]{:S(2)}, u32[]{:S(2)}) collective-permute-start(bf16[1024,768]{1,0:T(8,128)(2,1)S(1)} %bitcast.16), channel_id=1, source_target_pairs={{0,1},{1,2},{2,3},{3,0},{4,68},{5,69},{6,70},{7,71},{8,9},{9,10},{... | collective-permute-start | bytes 4718600 | tf_op jit(solution)/shard_map/ppermute | solution.py:340
  68.5 13.4 %all_to_all.16.lab_ref = f32[32,4,128]{2,1,0:T(4,128)S(1)} all-to-all(f32[32,4,128]{2,1,0:T(4,128)S(1)} %maximum_maximum_fusion), channel_id=1, replica_groups={{0,8,16,24,32,40,48,56,64,72,80,88,96,104,112,120,128,136,144,152,160,1..., dimensions={0} | all-to-all | bytes 131072 | tf_op jit(solution)/shard_map/all_to_all | solution.py:314
  81.9 0.0 copy-done
  81.9 2.9 %alone.1 = (f32[1,1024]{1,0:T(1,128)S(1)}, f32[8,1024]{1,0:T(8,128)S(1)}, f32[1024,128]{1,0:T(8,128)S(1)}, f32[1024,128]{1,0:T(8,128)S(1)}) custom-call(s32[3]{0:T(128)S(1)} %copy-done, bf16[1024,768]{1,0:T(8,128)(2,1)S(1)} %bitcast.17, f32[32,4,128]{2,1,0:T(4,128)S(1)} %all_to_all.16.lab_ref), custom_call_target="tpu_custom_call" | custom-call | flops 2000000000 | bytes 4000000 | tf_op jit(solution)/shard_map/alone/pallas_call | solution.py:208
  84.8 2.1 %collective-permute-done.7.right_ref = bf16[1024,768]{1,0:T(8,128)(2,1)S(1)} collective-permute-done((bf16[1024,768]{1,0:T(8,128)(2,1)S(1)}, bf16[1024,768]{1,0:T(8,128)(2,1)S(1)}, u32[]{:S(2)}, u32[]{:S(2)}) %collective-permute-start.7) | collective-permute-done | bytes 1572896 | tf_op jit(solution)/shard_map/ppermute | solution.py:340
  86.9 1.2 %collective-permute-done.6.left_ref = bf16[1024,768]{1,0:T(8,128)(2,1)S(1)} collective-permute-done((bf16[1024,768]{1,0:T(8,128)(2,1)S(1)}, bf16[1024,768]{1,0:T(8,128)(2,1)S(1)}, u32[]{:S(2)}, u32[]{:S(2)}) %collective-permute-start.6) | collective-permute-done | bytes 1572896 | tf_op jit(solution)/shard_map/ppermute | solution.py:340
  88.1 1.0 cross.1
  89.2 2.5 %collective-permute-start.8 = (f32[32,128]{1,0:T(8,128)S(1)}, f32[32,128]{1,0:T(8,128)S(1)}, u32[]{:S(2)}, u32[]{:S(2)}) collective-permute-start(f32[32,128]{1,0:T(8,128)S(1)} %cross.1), channel_id=1, source_target_pairs={{0,1},{1,2},{2,3},{3,0},{4,68},{5,69},{6,70},{7,71},{8,9},{9,10},{... | collective-permute-start | bytes 49160 | tf_op jit(solution)/shard_map/ppermute | solution.py:345
  91.6 0.8 sides.1
  92.5 0.6 collective-permute-done.8
  93.0 13.6 %all_to_all.17 = f32[32,1,128]{2,1,0:T(1,128)S(1)} all-to-all(f32[32,1,128]{2,1,0:T(1,128)S(1)} %bitcast.24), channel_id=1, replica_groups={{0,8,16,24,32,40,48,56,64,72,80,88,96,104,112,120,128,136,144,152,160,1..., dimensions={0} | all-to-all | bytes 32768 | tf_op jit(solution)/shard_map/all_to_all | solution.py:314
  106.7 0.0 copy-start.1
  106.7 7.3 %collective-permute-start.9 = (f32[32,128]{1,0:T(8,128)S(1)}, f32[32,128]{1,0:T(8,128)S(1)}, u32[]{:S(2)}, u32[]{:S(2)}) collective-permute-start(f32[32,128]{1,0:T(8,128)S(1)} %bitcast.25), channel_id=1, source_target_pairs={{0,4},{1,5},{2,6},{3,7},{4,0},{5,1},{6,2},{7,3},{8,12},{9,13},{10,... | collective-permute-start | bytes 49160 | tf_op jit(solution)/shard_map/ppermute | solution.py:350
  114.0 0.8 collective-permute-done.9.far_ref
  114.8 0.0 copy-start.2
  114.8 0.0 copy-done.1
  114.8 0.6 copy-done.2
  115.4 1.6 %unpack.1 = f32[1,1024]{1,0:T(1,128)} custom-call(s32[3]{0:T(128)} %pad_add_fusion.where_ref, s32[1,1024]{1,0:T(1,128)} %bitcast.28, s32[1,1024]{1,0:T(1,128)} %get-tuple-element.16.spot_ref, f32[32,128]{1,0:T(8,128)} %bitcast.26, f32[32,128]{1,0:T(8,128)} %copy-done.2), custom_call_target="tpu_custom_call" | custom-call | tf_op jit(solution)/shard_map/unpack/pallas_call | solution.py:275
  (3 shorter events, 0.0 us)
Async XLA Ops:
  5.7 11.3 %collective-permute-start = (bf16[512,768]{1,0:T(8,128)(2,1)}, bf16[512,768]{1,0:T(8,128)(2,1)S(1)}, u32[]{:S(2)}, u32[]{:S(2)}) collective-permute-start(bf16[512,768]{1,0:T(8,128)(2,1)} %get-tuple-element.18), channel_id=1, source_target_pairs={{0,4},{1,5},{2,6},{3,7},{4,0},{5,1},{6,2},{7,3},{8,12},{9,13},{10,... | collective-permute-start | bytes 2359304 | tf_op jit(solution)/shard_map/ppermute | solution.py:328
  9.0 3.3 %collective-permute-start.1 = (f32[32,128]{1,0:T(8,128)}, f32[32,128]{1,0:T(8,128)S(1)}, u32[]{:S(2)}, u32[]{:S(2)}) collective-permute-start(f32[32,128]{1,0:T(8,128)} %get-tuple-element.20), channel_id=1, source_target_pairs={{0,4},{1,5},{2,6},{3,7},{4,0},{5,1},{6,2},{7,3},{8,12},{9,13},{10,... | collective-permute-start | bytes 49160 | tf_op jit(solution)/shard_map/ppermute | solution.py:329
  9.1 5.2 %collective-permute-start.4 = (f32[32,128]{1,0:T(8,128)}, f32[32,128]{1,0:T(8,128)S(1)}, u32[]{:S(2)}, u32[]{:S(2)}) collective-permute-start(f32[32,128]{1,0:T(8,128)} %get-tuple-element.19), channel_id=1, source_target_pairs={{0,3},{1,0},{2,1},{3,2},{4,196},{5,197},{6,198},{7,199},{8,11},{9,... | collective-permute-start | bytes 49160 | tf_op jit(solution)/shard_map/ppermute | solution.py:332
  10.1 4.3 %collective-permute-start.5 = (f32[32,128]{1,0:T(8,128)}, f32[32,128]{1,0:T(8,128)S(1)}, u32[]{:S(2)}, u32[]{:S(2)}) collective-permute-start(f32[32,128]{1,0:T(8,128)} %get-tuple-element.20), channel_id=1, source_target_pairs={{0,196},{1,197},{2,198},{3,199},{4,3},{5,0},{6,1},{7,2},{8,204},{9... | collective-permute-start | bytes 49160 | tf_op jit(solution)/shard_map/ppermute | solution.py:332
  11.0 4.1 %collective-permute-start.2 = (f32[32,128]{1,0:T(8,128)}, f32[32,128]{1,0:T(8,128)S(1)}, u32[]{:S(2)}, u32[]{:S(2)}) collective-permute-start(f32[32,128]{1,0:T(8,128)} %get-tuple-element.19), channel_id=1, source_target_pairs={{0,1},{1,2},{2,3},{3,0},{4,68},{5,69},{6,70},{7,71},{8,9},{9,10},{... | collective-permute-start | bytes 49160 | tf_op jit(solution)/shard_map/ppermute | solution.py:332
  12.3 4.6 %collective-permute-start.3 = (f32[32,128]{1,0:T(8,128)}, f32[32,128]{1,0:T(8,128)S(1)}, u32[]{:S(2)}, u32[]{:S(2)}) collective-permute-start(f32[32,128]{1,0:T(8,128)} %get-tuple-element.20), channel_id=1, source_target_pairs={{0,68},{1,69},{2,70},{3,71},{4,1},{5,2},{6,3},{7,0},{8,76},{9,77},... | collective-permute-start | bytes 49160 | tf_op jit(solution)/shard_map/ppermute | solution.py:332
  18.3 63.6 %copy-start = (s32[3]{0:T(128)S(1)}, s32[3]{0:T(128)}, u32[]{:S(2)}) copy-start(s32[3]{0:T(128)} %pad_add_fusion.where_ref) | copy-start | bytes 40
  67.0 19.9 %collective-permute-start.7 = (bf16[1024,768]{1,0:T(8,128)(2,1)S(1)}, bf16[1024,768]{1,0:T(8,128)(2,1)S(1)}, u32[]{:S(2)}, u32[]{:S(2)}) collective-permute-start(bf16[1024,768]{1,0:T(8,128)(2,1)S(1)} %bitcast.15), channel_id=1, source_target_pairs={{0,3},{1,0},{2,1},{3,2},{4,196},{5,197},{6,198},{7,199},{8,11},{9,... | collective-permute-start | bytes 4718600 | tf_op jit(solution)/shard_map/ppermute | solution.py:340
  67.0 21.1 %collective-permute-start.6 = (bf16[1024,768]{1,0:T(8,128)(2,1)S(1)}, bf16[1024,768]{1,0:T(8,128)(2,1)S(1)}, u32[]{:S(2)}, u32[]{:S(2)}) collective-permute-start(bf16[1024,768]{1,0:T(8,128)(2,1)S(1)} %bitcast.16), channel_id=1, source_target_pairs={{0,1},{1,2},{2,3},{3,0},{4,68},{5,69},{6,70},{7,71},{8,9},{9,10},{... | collective-permute-start | bytes 4718600 | tf_op jit(solution)/shard_map/ppermute | solution.py:340
  89.2 3.9 %collective-permute-start.8 = (f32[32,128]{1,0:T(8,128)S(1)}, f32[32,128]{1,0:T(8,128)S(1)}, u32[]{:S(2)}, u32[]{:S(2)}) collective-permute-start(f32[32,128]{1,0:T(8,128)S(1)} %cross.1), channel_id=1, source_target_pairs={{0,1},{1,2},{2,3},{3,0},{4,68},{5,69},{6,70},{7,71},{8,9},{9,10},{... | collective-permute-start | bytes 49160 | tf_op jit(solution)/shard_map/ppermute | solution.py:345
  106.7 8.1 %copy-start.1 = (f32[32,1,128]{2,1,0:T(1,128)}, f32[32,1,128]{2,1,0:T(1,128)S(1)}, u32[]{:S(2)}) copy-start(f32[32,1,128]{2,1,0:T(1,128)S(1)} %all_to_all.17) | copy-start | bytes 49156
  106.7 8.1 %collective-permute-start.9 = (f32[32,128]{1,0:T(8,128)S(1)}, f32[32,128]{1,0:T(8,128)S(1)}, u32[]{:S(2)}, u32[]{:S(2)}) collective-permute-start(f32[32,128]{1,0:T(8,128)S(1)} %bitcast.25), channel_id=1, source_target_pairs={{0,4},{1,5},{2,6},{3,7},{4,0},{5,1},{6,2},{7,3},{8,12},{9,13},{10,... | collective-permute-start | bytes 49160 | tf_op jit(solution)/shard_map/ppermute | solution.py:350
  114.8 0.6 copy-start.2

commit v5 on v0

v5 whole, which is shorter than its diff:
```python
import jax
import jax.numpy as jnp
from jax import lax
from jax.experimental import pallas as pl
from jax.experimental.pallas import tpu as pltpu
from jax.sharding import PartitionSpec as P

LANES = 128
TILE = 256


def split3(x):
    high = x.astype(jnp.bfloat16)
    rest = x - high.astype(jnp.float32)
    mid = rest.astype(jnp.bfloat16)
    low = (rest - mid.astype(jnp.float32)).astype(jnp.bfloat16)
    return high, mid, low


def iota(shape, dim):
    return lax.broadcasted_iota(jnp.int32, shape, dim)


def dot(a, b, dims):
    return lax.dot_general(a, b, (dims, ((), ())), preferred_element_type=jnp.float32)


BITS = 4096.0
GROUP = 16
NOTE = 8


def slot_of(clusters, core, half):
    owner = clusters // 2
    away = jnp.where(owner // half == core, 0, 1)
    return owner % half + away * half, away


def smem():
    return pl.BlockSpec(memory_space=pltpu.SMEM)


def vmem():
    return pl.BlockSpec(memory_space=pltpu.VMEM)


def call(kernel, name, ins, outs, scratch=(), flops=0):
    return pl.pallas_call(
        kernel,
        out_shape=tuple(jax.ShapeDtypeStruct(shape, kind) for shape, kind in outs),
        in_specs=[smem()] + [vmem()] * (len(ins) - 1),
        out_specs=(vmem(),) * len(outs),
        scratch_shapes=[pltpu.VMEM(shape, kind) for shape, kind in scratch],
        compiler_params=pltpu.CompilerParams(vmem_limit_bytes=48 * 2**20),
        cost_estimate=pl.CostEstimate(flops=flops, bytes_accessed=2**20, transcendentals=0),
        name=name,
    )(*ins)


def put_rows(out_ref, unit_ref, place, base):
    rows = unit_ref.shape[0]
    each = TILE // GROUP
    for start in range(0, rows // 2, TILE):
        pick = (iota((TILE, rows), 0) + (base + start) == place).astype(jnp.bfloat16)
        block = dot(pick, unit_ref[...], ((1,), (0,))).astype(jnp.bfloat16)
        first = start // GROUP
        for lane in range(block.shape[1] // LANES):
            out_ref[first : first + each, lane * GROUP : (lane + 1) * GROUP, :] = block[
                :, lane * LANES : (lane + 1) * LANES
            ].reshape(each, GROUP, LANES)


def send_kernel(where_ref, emb_ref, clu_ref, send_ref, notes_ref, unit_ref, rows_ref):
    rows = emb_ref.shape[0]
    half = send_ref.shape[0]
    clusters = clu_ref[...]
    slot, away = slot_of(clusters, where_ref[1], half)
    hot = (iota((2 * half, rows), 0) == slot).astype(jnp.bfloat16)
    before = (iota((rows, rows), 0) < iota((rows, rows), 1)).astype(jnp.bfloat16)
    count = dot(hot, before, ((1,), (0,)))
    rank = jnp.sum(hot.astype(jnp.float32) * count, axis=0, keepdims=True).astype(jnp.int32)
    spot = rank + away * GROUP
    place = slot * GROUP + rank
    rows_ref[...] = jnp.concatenate([slot, spot, place, place] * 2, axis=0)
    bit = (clusters % 2).astype(jnp.float32)
    spots = jnp.where(iota((LANES, rows), 0) == spot, bit, 0.0).astype(jnp.bfloat16)
    labels = dot(hot, spots, ((1,), (1,))).astype(jnp.bfloat16)
    notes_ref[...] = jnp.broadcast_to(labels[:half, None, :], (half, NOTE, LANES))
    values = emb_ref[...].astype(jnp.float32)
    scale = lax.rsqrt(jnp.sum(values * values, axis=1, keepdims=True) + 1e-06)
    unit_ref[...] = (values * scale).astype(jnp.bfloat16)
    put_rows(send_ref, unit_ref, place, rows // 2)
    data = send_ref.shape[1] - NOTE
    send_ref[:, data:, :] = jnp.broadcast_to(labels[half:, None, :], (half, NOTE, LANES))


def keep_kernel(where_ref, unit_ref, rows_ref, keep_ref):
    put_rows(keep_ref, unit_ref, rows_ref[2:3, :], 0)


def source_of(place):
    return place // TILE * (TILE // (2 * GROUP)) + place % (TILE // 2) // GROUP


def lane_of(place):
    return place // (TILE // 2) % 2 * GROUP + place % GROUP


def order_of(place, core, part):
    source, flip, rank = source_of(place), place // (TILE // 2) % 2, place % GROUP
    from_core = jnp.where(flip == 0, core, 1 - core)
    by_row = (source * 2 + from_core) * 4 + part
    by_column = ((part * 8 + source // 4) * 2 + from_core) * 4 + source % 4
    return jnp.where(core == 0, by_row, by_column) * GROUP + rank


def tile_of(ref, index):
    each = TILE // (2 * GROUP)
    data = (ref.shape[1] - NOTE) // 2
    here = slice(index * each, (index + 1) * each)
    lanes = []
    for base in range(0, data, GROUP):
        parts = [
            ref[here, start : start + GROUP, :].reshape(TILE // 2, LANES)
            for start in (base, data + base)
        ]
        lanes.append(jnp.concatenate(parts, axis=0))
    return jnp.concatenate(lanes, axis=1)


def notes_of(ref):
    data = ref.shape[1] - NOTE
    return (jnp.sum(ref[:, data:, :].astype(jnp.float32), axis=1) * (1.0 / NOTE)).astype(jnp.bfloat16)


def row_codes(lab, rows, core, part):
    sources = lab.shape[0]
    width = 2 * GROUP
    place = iota((1, rows), 1)
    hot = (iota((sources, rows), 0) == source_of(place)).astype(jnp.bfloat16)
    spread = dot(lab[:, :width], hot, ((0,), (0,)))
    chosen = iota((width, rows), 0) == lane_of(place)
    label = jnp.sum(jnp.where(chosen, spread, 0.0), axis=0, keepdims=True)
    return label * BITS, label * BITS + order_of(place, core, part).astype(jnp.float32)


def column_codes(lab, rows, core, part):
    sources = lab.shape[0]
    place = iota((rows, 1), 0)
    hot = (iota((rows, sources), 1) == source_of(place)).astype(jnp.bfloat16)
    spread = dot(hot, lab, ((1,), (0,)))
    chosen = iota((rows, LANES), 1) == lane_of(place)
    kept = jnp.where(chosen, spread, 0.0).astype(jnp.bfloat16)
    label = dot(kept, jnp.ones((LANES, LANES), jnp.bfloat16), ((1,), (0,)))
    return label * BITS + order_of(place, core, part).astype(jnp.float32)


def scan(best_ref, query_ref, key_ref, floor, ceiling, codes_ref, pick):
    tiles = best_ref.shape[1] // TILE
    for query in range(tiles):
        queries = tile_of(query_ref, query)
        here = slice(query * TILE, (query + 1) * TILE)
        best = best_ref[:, here]
        for key in range(tiles):
            if not pick(key, query):
                continue
            sims = dot(tile_of(key_ref, key), queries, ((1,), (1,)))
            codes = codes_ref[key * TILE : (key + 1) * TILE, :]
            codes = jnp.concatenate([codes] * (TILE // LANES), axis=1)
            mask = (codes >= floor[:, here]) & (codes < ceiling[:, here])
            found = jnp.max(jnp.where(mask, sims, -1.0), axis=0, keepdims=True)
            best = jnp.maximum(best, found)
        best_ref[:, here] = best


def scan_pair(best_ref, query_ref, key_ref, floor, ceiling, codes_ref, core, part, key_part):
    args = (best_ref, query_ref, key_ref, floor, ceiling, codes_ref)

    @pl.when((core == 0) | (key_part < part))
    def _():
        scan(*args, lambda key, query: key <= query)

    @pl.when((core != 0) & (key_part < part))
    def _():
        scan(*args, lambda key, query: key > query)


def store_groups(out_ref, best):
    sources = out_ref.shape[0]
    rows = best.shape[1]
    mine = iota((sources, rows), 0) == source_of(iota((1, rows), 1))
    spots = (iota((rows, LANES), 1) == lane_of(iota((rows, 1), 0))).astype(jnp.bfloat16)
    total = jnp.zeros((sources, LANES), jnp.float32)
    for piece in split3(best):
        spread = jnp.where(mine, piece.astype(jnp.float32), 0.0).astype(jnp.bfloat16)
        total = total + dot(spread, spots, ((1,), (0,)))
    out_ref[...] = total


def parts_of(where_ref):
    me, core, parts = where_ref[0], where_ref[1], where_ref[2]
    return core, me, lax.rem(me + parts - 1, parts), lax.rem(me + 1, parts)


def alone_kernel(where_ref, own_ref, back_ref, best_ref, rows_ref, kept_ref, codes_ref):
    rows = best_ref.shape[1]
    core, me, _, _ = parts_of(where_ref)
    kept_ref[...] = back_ref[...]
    lab = notes_of(own_ref)
    floor, ceiling = row_codes(lab, rows, core, me)
    rows_ref[...] = jnp.concatenate([floor, ceiling] * 4, axis=0)
    codes_ref[...] = column_codes(lab, rows, core, me)
    best_ref[...] = jnp.full((1, rows), -1.0, jnp.float32)
    scan(best_ref, own_ref, own_ref, floor, ceiling, codes_ref, lambda key, query: key <= query)


def right_kernel(where_ref, alone_ref, own_ref, right_ref, rows_ref, best_ref, right_rows_ref, codes_ref):
    rows = best_ref.shape[1]
    core, me, _, right = parts_of(where_ref)
    best_ref[...] = alone_ref[...]
    lab = notes_of(right_ref)
    floor, ceiling = row_codes(lab, rows, core, right)
    right_rows_ref[...] = jnp.concatenate([floor, ceiling] * 4, axis=0)
    codes_ref[...] = column_codes(lab, rows, core, right)
    scan_pair(
        best_ref, own_ref, right_ref, rows_ref[0:1, :], rows_ref[1:2, :], codes_ref, core, me, right
    )


def cross_kernel(where_ref, left_ref, right_ref, rows_ref, out_ref, codes_ref, best_ref):
    rows = best_ref.shape[1]
    core, _, left, right = parts_of(where_ref)
    codes_ref[...] = column_codes(notes_of(left_ref), rows, core, left)
    best_ref[...] = jnp.full((1, rows), -1.0, jnp.float32)
    scan_pair(
        best_ref, right_ref, left_ref, rows_ref[0:1, :], rows_ref[1:2, :], codes_ref, core, right, left
    )
    store_groups(out_ref, best_ref[...])


def left_kernel(where_ref, found_ref, own_ref, left_ref, rows_ref, codes_ref, out_ref, best_ref):
    core, me, left, _ = parts_of(where_ref)
    best_ref[...] = found_ref[...]
    scan_pair(
        best_ref, own_ref, left_ref, rows_ref[0:1, :], rows_ref[1:2, :], codes_ref, core, me, left
    )
    store_groups(out_ref, best_ref[...])


def unpack_kernel(where_ref, back_ref, near_ref, far_ref, out_ref):
    half = near_ref.shape[0]
    rows = back_ref.shape[1]
    width = 2 * GROUP
    hot = (iota((2 * half, rows), 0) == back_ref[0:1, :]).astype(jnp.bfloat16)
    results = jnp.concatenate([near_ref[:, :width], far_ref[:, :width]], axis=0)
    total = jnp.zeros((width, rows), jnp.float32)
    for piece in split3(results):
        total = total + dot(piece, hot, ((0,), (0,)))
    mine = iota((width, rows), 0) == back_ref[1:2, :]
    out_ref[...] = jnp.sum(jnp.where(mine, total, 0.0), axis=0, keepdims=True)


AXES = ("dp", "help")
NY, NZ, NX = 4, 8, 4


def device(y, z, core, x):
    return ((y % NY * NZ + z % NZ) * 2 + core) * NX + x % NX


EVERY = [(y, z, c, x) for y in range(NY) for z in range(NZ) for c in range(2) for x in range(NX)]
SWAP = [(device(y, z, c, x), device(y, z, 1 - c, x)) for y, z, c, x in EVERY]
GROUPS = [[device(y, z, 0, x) for y in range(NY) for z in range(NZ)] for x in range(NX)] + [
    [device(y, z, 1, x) for z in range(NZ) for x in range(NX)] for y in range(NY)
]


def aside(step):
    return [
        (device(y, z, c, x), device(y, z, c, x + step) if c == 0 else device(y + step, z, c, x))
        for y, z, c, x in EVERY
    ]


def exchange(array):
    return lax.all_to_all(
        array, AXES, split_axis=0, concat_axis=0, axis_index_groups=GROUPS, tiled=True
    )


def shards(embeddings, clusters, send_order):
    rows, depth = embeddings.shape
    half = lax.axis_size("dp") // 2
    data = GROUP * (depth // LANES)
    dp, x = lax.axis_index("dp"), lax.axis_index("help")
    core, y = dp % 2, dp // (2 * NZ)
    where = jnp.stack([jnp.where(core == 0, x, y), core, jnp.int32(NX)])
    half_float, full_float, whole = jnp.bfloat16, jnp.float32, jnp.int32
    send, notes, unit, back = call(
        send_kernel,
        "send",
        (where, embeddings, clusters.reshape(1, rows)),
        (
            ((half, data + NOTE, LANES), half_float),
            ((half, NOTE, LANES), half_float),
            ((rows, depth), half_float),
            ((8, rows), whole),
        ),
    )
    got = lax.ppermute(send, AXES, SWAP)
    (keep,) = call(
        keep_kernel, "keep", (where, unit, back), (((half, data, LANES), half_float),), flops=10**9
    )
    outgoing = jnp.concatenate([keep, got[:, :data], notes + got[:, data:]], axis=1)
    own = exchange(outgoing)
    left, right = lax.ppermute(own, AXES, aside(1)), lax.ppermute(own, AXES, aside(-1))
    row, lines = ((1, rows), full_float), ((8, rows), full_float)
    codes, groups = ((rows, LANES), full_float), ((half, LANES), full_float)
    best, own_rows, back = call(
        alone_kernel, "alone", (where, own, back), (row, lines, ((8, rows), whole)), (codes,), 10**9
    )
    best, right_rows = call(
        right_kernel, "right", (where, best, own, right, own_rows), (row, lines), (codes,), 10**9
    )
    cross, left_codes = call(
        cross_kernel, "cross", (where, left, right, right_rows), (groups, codes), (row,), 10**9
    )
    cross = lax.ppermute(cross, AXES, aside(1))
    (best,) = call(
        left_kernel, "left", (where, best, own, left, own_rows, left_codes), (groups,), (row,), 10**9
    )
    best = jnp.maximum(best, cross)
    near = exchange(best.reshape(half, 1, LANES)).reshape(half, LANES)
    far = lax.ppermute(near, AXES, SWAP)
    (out,) = call(unpack_kernel, "unpack", (where, back, near, far), (row,))
    return out.reshape(rows)


def solution(mesh):
    return jax.shard_map(
        shards,
        mesh=mesh,
        in_specs=(P(("dp", "help"), None), P(("dp", "help")), P(("dp", "help"))),
        out_specs=P(("dp", "help")),
        check_vma=False,
    )
```

time: 186 us -> 112 us (0.60)
  blocking collectives: 93 us -> 62.4 us
  matrix products: 20.2 us -> 0 us
  local copies, waits for them, and re-layouts: 21 us -> 2.15 us
  between operations: 13.5 us -> 0.07 us
  Pallas kernels: 0 us -> 12.6 us
  other arithmetic: 5.52 us -> 0.21 us
    ppermute x0 -> x5, waiting for transfers between devices: none -> 21.7 us  [the longest x1 15.3 us: shards(): lax.ppermute(own, AXES, aside(-1))]
    all_gather x2 -> x0, blocking collectives: 20.3 us -> none  [the longest x1 10.3 us: shards(): lax.all_gather(pool_labels, 'help', axis=0, tiled=True)]
    dot_general x4 -> x0, matrix products: 20.2 us -> none  [one_block(): jnp.einsum('qd,kd->qk', vectors, keys, preferred_element_type=jnp.float32)]
    gather x3 -> x0, local copies, waits for them, and re-layouts: 13.1 us -> none  [the longest x1 4.53 us: shards(): out_labels = clusters[send_order].reshape(owners, width)]
    ppermute x0 -> x5, starting transfers between devices: none -> 12.8 us  [the longest x1 5.3 us: shards(): far = lax.ppermute(near, AXES, SWAP)]
    pallas_call x0 -> x7, Pallas kernels: none -> 12.6 us  [call(): pl.pallas_call(kernel, out_shape=tuple((jax.ShapeDtypeStruct(shape, kind)...]
    all_to_all x2 -> x0, starting transfers between devices: 12.4 us -> none  [the longest x1 6.24 us: shards(): lax.all_to_all(out_index, 'dp', split_axis=0, concat_axis=0, tiled=True)]
    all_to_all x2 -> x0, waiting for transfers between devices: 12.1 us -> none  [the longest x1 8 us: shards(): lax.all_to_all(out_index, 'dp', split_axis=0, concat_axis=0, tiled=True)]
  transfers between devices with their start and end apart: 3 -> 5, of which waited for: 3 -> 5; matrix products, arithmetic and copies ran while one was open for 6% -> 0% of each run, Pallas kernels for 0% -> 6%
where the time goes in v5:
time: 112 us
  blocking collectives  62.4 us (56%)
  waiting for transfers between devices  21.7 us (19%)
  starting transfers between devices  12.8 us (11%)
  Pallas kernels  12.6 us (11%)
  local copies, waits for them, and re-layouts  2.15 us (2%)
    all_to_all x2, blocking collectives, exchange(): lax.all_to_all(array, AXES, split_axis=0, concat_axis=0, axis_index_group...  62.4 us
    ppermute x1, waiting for transfers between devices, shards(): lax.ppermute(own, AXES, aside(-1))  15.3 us
    pallas_call x7, Pallas kernels, call(): pl.pallas_call(kernel, out_shape=tuple((jax.ShapeDtypeStruct(shape, kind)...  12.6 us
    ppermute x1, starting transfers between devices, shards(): far = lax.ppermute(near, AXES, SWAP)  5.3 us
    ppermute x1, waiting for transfers between devices, shards(): cross = lax.ppermute(cross, AXES, aside(1))  3.38 us
    ppermute x1, starting transfers between devices, shards(): got = lax.ppermute(send, AXES, SWAP)  3.33 us
    ppermute x1, starting transfers between devices, shards(): lax.ppermute(own, AXES, aside(-1))  3.07 us
  transfers between devices with their start and end apart: 5, of which 5 were waited for; matrix products, arithmetic and copies ran while one was open for 0% of the time, Pallas kernels for 6%

profile of v5, /device:TPU:1, one launch (start us, length us, event | category | flops | bytes accessed | tf_op | source)
XLA Modules:
  0.0 111.9 jit_solution(607759563301125953)
XLA Ops:
  0.0 0.1 pad_add_fusion.where_ref
  0.1 0.0 copy-start
  0.1 1.4 %copy-done = bf16[1024,768]{1,0:T(8,128)(2,1)S(1)} copy-done((bf16[1024,768]{1,0:T(8,128)(2,1)S(1)}, bf16[1024,768]{1,0:T(8,128)(2,1)}, u32[]{:S(2)}) %copy-start) | copy-done | bytes 1572888
  1.5 0.0 copy-start.1
  1.5 0.7 copy-done.1
  2.2 2.3 %send.1 = (bf16[32,104,128]{2,1,0:T(8,128)(2,1)S(1)}, bf16[32,8,128]{2,1,0:T(8,128)(2,1)S(1)}, bf16[1024,768]{1,0:T(8,128)(2,1)S(1)}, s32[8,1024]{1,0:T(8,128)S(1)}) custom-call(s32[3]{0:T(128)S(1)} %pad_add_fusion.where_ref, bf16[1024,768]{1,0:T(8,128)(2,1)S(1)} %copy-done, s32[1,1024]{1,0:T(1,128)S(1)} %bitcast.10), custom_call_target="tpu_custom_call" | custom-call | bytes 1048576 | tf_op jit(solution)/shard_map/send/pallas_call | solution.py:48
  4.5 3.3 %collective-permute-start = (bf16[32,104,128]{2,1,0:T(8,128)(2,1)S(1)}, bf16[32,104,128]{2,1,0:T(8,128)(2,1)S(1)}, u32[]{:S(2)}, u32[]{:S(2)}) collective-permute-start(bf16[32,104,128]{2,1,0:T(8,128)(2,1)S(1)} %get-tuple-element.18), channel_id=1, source_target_pairs={{0,4},{1,5},{2,6},{3,7},{4,0},{5,1},{6,2},{7,3},{8,12},{9,13},{10,... | collective-permute-start | bytes 2555912 | tf_op jit(solution)/shard_map/ppermute | solution.py:310
  7.8 1.5 %keep.1 = bf16[32,96,128]{2,1,0:T(8,128)(2,1)S(1)} custom-call(s32[3]{0:T(128)S(1)} %pad_add_fusion.where_ref, bf16[1024,768]{1,0:T(8,128)(2,1)S(1)} %get-tuple-element.16.unit_ref, s32[8,1024]{1,0:T(8,128)S(1)} %get-tuple-element.17.rows_ref.back_ref), custom_call_target="tpu_custom_call" | custom-call | flops 1000000000 | bytes 1048576 | tf_op jit(solution)/shard_map/keep/pallas_call | solution.py:48
  9.4 0.5 collective-permute-done
  9.8 0.1 slice.8
  9.9 0.1 pad_maximum_fusion
  10.0 49.0 %all_to_all.10.own_ref = bf16[32,200,128]{2,1,0:T(8,128)(2,1)S(1)} all-to-all(bf16[32,200,128]{2,1,0:T(8,128)(2,1)S(1)} %pad_maximum_fusion), channel_id=1, replica_groups={{0,8,16,24,32,40,48,56,64,72,80,88,96,104,112,120,128,136,144,152,160,1..., dimensions={0} | all-to-all | bytes 3276800 | tf_op jit(solution)/shard_map/all_to_all | solution.py:286
  59.1 3.1 %collective-permute-start.1 = (bf16[32,200,128]{2,1,0:T(8,128)(2,1)S(1)}, bf16[32,200,128]{2,1,0:T(8,128)(2,1)S(1)}, u32[]{:S(2)}, u32[]{:S(2)}) collective-permute-start(bf16[32,200,128]{2,1,0:T(8,128)(2,1)S(1)} %all_to_all.10.own_ref), channel_id=1, source_target_pairs={{0,3},{1,0},{2,1},{3,2},{4,196},{5,197},{6,198},{7,199},{8,11},{9,... | collective-permute-start | bytes 4915208 | tf_op jit(solution)/shard_map/ppermute | solution.py:316
  62.1 0.0 collective-permute-start.2
  62.1 2.8 %alone.1 = (f32[1,1024]{1,0:T(1,128)S(1)}, f32[8,1024]{1,0:T(8,128)S(1)}, s32[8,1024]{1,0:T(8,128)S(1)}) custom-call(s32[3]{0:T(128)S(1)} %pad_add_fusion.where_ref, bf16[32,200,128]{2,1,0:T(8,128)(2,1)S(1)} %all_to_all.10.own_ref, s32[8,1024]{1,0:T(8,128)S(1)} %get-tuple-element.17.rows_ref.back_ref), custom_call_target="tpu_custom_call" | custom-call | flops 1000000000 | bytes 1048576 | tf_op jit(solution)/shard_map/alone/pallas_call | solution.py:48
  64.9 15.3 %collective-permute-done.1.right_ref = bf16[32,200,128]{2,1,0:T(8,128)(2,1)S(1)} collective-permute-done((bf16[32,200,128]{2,1,0:T(8,128)(2,1)S(1)}, bf16[32,200,128]{2,1,0:T(8,128)(2,1)S(1)}, u32[]{:S(2)}, u32[]{:S(2)}) %collective-permute-start.1) | collective-permute-done | bytes 1638432 | tf_op jit(solution)/shard_map/ppermute | solution.py:316
  80.2 1.6 %right.1 = (f32[1,1024]{1,0:T(1,128)S(1)}, f32[8,1024]{1,0:T(8,128)S(1)}) custom-call(s32[3]{0:T(128)S(1)} %pad_add_fusion.where_ref, f32[1,1024]{1,0:T(1,128)S(1)} %get-tuple-element.21.alone_ref, bf16[32,200,128]{2,1,0:T(8,128)(2,1)S(1)} %all_to_all.10.own_ref, bf16[32,200,128]{2,1,0:T(8,128)(2,1)S(1)} %collective-permute-done.1.right_ref, ...), custom_call_target="tpu_custom_call" | custom-call | flops 1000000000 | bytes 1048576 | tf_op jit(solution)/shard_map/right/pallas_call | solution.py:48
  81.8 1.8 %collective-permute-done.2.left_ref = bf16[32,200,128]{2,1,0:T(8,128)(2,1)S(1)} collective-permute-done((bf16[32,200,128]{2,1,0:T(8,128)(2,1)S(1)}, bf16[32,200,128]{2,1,0:T(8,128)(2,1)S(1)}, u32[]{:S(2)}, u32[]{:S(2)}) %collective-permute-start.2) | collective-permute-done | bytes 1638432 | tf_op jit(solution)/shard_map/ppermute | solution.py:316
  83.6 2.0 %cross.1 = (f32[32,128]{1,0:T(8,128)S(1)}, f32[1024,128]{1,0:T(8,128)S(1)}) custom-call(s32[3]{0:T(128)S(1)} %pad_add_fusion.where_ref, bf16[32,200,128]{2,1,0:T(8,128)(2,1)S(1)} %collective-permute-done.2.left_ref, bf16[32,200,128]{2,1,0:T(8,128)(2,1)S(1)} %collective-permute-done.1.right_ref, f32[8,1024]{1,0:T(8,128)S(1)} %get-tuple-element.24.rows_ref), custom_call_target="tpu_custom_call" | custom-call | flops 1000000000 | bytes 1048576 | tf_op jit(solution)/shard_map/cross/pallas_call | solution.py:48
  85.6 1.1 collective-permute-start.3
  86.7 0.9 left.1
  87.6 3.4 %collective-permute-done.3 = f32[32,128]{1,0:T(8,128)S(1)} collective-permute-done((f32[32,128]{1,0:T(8,128)S(1)}, f32[32,128]{1,0:T(8,128)S(1)}, u32[]{:S(2)}, u32[]{:S(2)}) %collective-permute-start.3) | collective-permute-done | bytes 16416 | tf_op jit(solution)/shard_map/ppermute | solution.py:328
  91.0 13.4 %all_to_all.11 = f32[32,1,128]{2,1,0:T(1,128)S(1)} all-to-all(f32[32,1,128]{2,1,0:T(1,128)S(1)} %bitcast.11), channel_id=1, replica_groups={{0,8,16,24,32,40,48,56,64,72,80,88,96,104,112,120,128,136,144,152,160,1..., dimensions={0} | all-to-all | bytes 32768 | tf_op jit(solution)/shard_map/all_to_all | solution.py:286
  104.4 5.3 %collective-permute-start.4 = (f32[32,128]{1,0:T(8,128)S(1)}, f32[32,128]{1,0:T(8,128)S(1)}, u32[]{:S(2)}, u32[]{:S(2)}) collective-permute-start(f32[32,128]{1,0:T(8,128)S(1)} %bitcast.8), channel_id=1, source_target_pairs={{0,4},{1,5},{2,6},{3,7},{4,0},{5,1},{6,2},{7,3},{8,12},{9,13},{10,... | collective-permute-start | bytes 49160 | tf_op jit(solution)/shard_map/ppermute | solution.py:334
  109.7 0.8 collective-permute-done.4.far_ref
  110.5 1.4 %unpack.1 = f32[1,1024]{1,0:T(1,128)} custom-call(s32[3]{0:T(128)S(1)} %pad_add_fusion.where_ref, s32[8,1024]{1,0:T(8,128)S(1)} %get-tuple-element.20.back_ref, f32[32,128]{1,0:T(8,128)S(1)} %bitcast.9, f32[32,128]{1,0:T(8,128)S(1)} %collective-permute-done.4.far_ref), custom_call_target="tpu_custom_call" | custom-call | bytes 1048576 | tf_op jit(solution)/shard_map/unpack/pallas_call | solution.py:48
  (2 shorter events, 0.0 us)
Async XLA Ops:
  0.1 1.4 %copy-start = (bf16[1024,768]{1,0:T(8,128)(2,1)S(1)}, bf16[1024,768]{1,0:T(8,128)(2,1)}, u32[]{:S(2)}) copy-start(bf16[1024,768]{1,0:T(8,128)(2,1)} %emb_ref.1) | copy-start | bytes 4718596
  1.5 0.7 copy-start.1
  4.5 5.3 %collective-permute-start = (bf16[32,104,128]{2,1,0:T(8,128)(2,1)S(1)}, bf16[32,104,128]{2,1,0:T(8,128)(2,1)S(1)}, u32[]{:S(2)}, u32[]{:S(2)}) collective-permute-start(bf16[32,104,128]{2,1,0:T(8,128)(2,1)S(1)} %get-tuple-element.18), channel_id=1, source_target_pairs={{0,4},{1,5},{2,6},{3,7},{4,0},{5,1},{6,2},{7,3},{8,12},{9,13},{10,... | collective-permute-start | bytes 2555912 | tf_op jit(solution)/shard_map/ppermute | solution.py:310
  59.1 21.1 %collective-permute-start.1 = (bf16[32,200,128]{2,1,0:T(8,128)(2,1)S(1)}, bf16[32,200,128]{2,1,0:T(8,128)(2,1)S(1)}, u32[]{:S(2)}, u32[]{:S(2)}) collective-permute-start(bf16[32,200,128]{2,1,0:T(8,128)(2,1)S(1)} %all_to_all.10.own_ref), channel_id=1, source_target_pairs={{0,3},{1,0},{2,1},{3,2},{4,196},{5,197},{6,198},{7,199},{8,11},{9,... | collective-permute-start | bytes 4915208 | tf_op jit(solution)/shard_map/ppermute | solution.py:316
  62.1 21.5 %collective-permute-start.2 = (bf16[32,200,128]{2,1,0:T(8,128)(2,1)S(1)}, bf16[32,200,128]{2,1,0:T(8,128)(2,1)S(1)}, u32[]{:S(2)}, u32[]{:S(2)}) collective-permute-start(bf16[32,200,128]{2,1,0:T(8,128)(2,1)S(1)} %all_to_all.10.own_ref), channel_id=1, source_target_pairs={{0,1},{1,2},{2,3},{3,0},{4,68},{5,69},{6,70},{7,71},{8,9},{9,10},{... | collective-permute-start | bytes 4915208 | tf_op jit(solution)/shard_map/ppermute | solution.py:316
  85.6 5.4 %collective-permute-start.3 = (f32[32,128]{1,0:T(8,128)S(1)}, f32[32,128]{1,0:T(8,128)S(1)}, u32[]{:S(2)}, u32[]{:S(2)}) collective-permute-start(f32[32,128]{1,0:T(8,128)S(1)} %get-tuple-element.26), channel_id=1, source_target_pairs={{0,1},{1,2},{2,3},{3,0},{4,68},{5,69},{6,70},{7,71},{8,9},{9,10},{... | collective-permute-start | bytes 49160 | tf_op jit(solution)/shard_map/ppermute | solution.py:328
  104.4 6.1 %collective-permute-start.4 = (f32[32,128]{1,0:T(8,128)S(1)}, f32[32,128]{1,0:T(8,128)S(1)}, u32[]{:S(2)}, u32[]{:S(2)}) collective-permute-start(f32[32,128]{1,0:T(8,128)S(1)} %bitcast.8), channel_id=1, source_target_pairs={{0,4},{1,5},{2,6},{3,7},{4,0},{5,1},{6,2},{7,3},{8,12},{9,13},{10,... | collective-permute-start | bytes 49160 | tf_op jit(solution)/shard_map/ppermute | solution.py:334

commit v6 on v5

--- a/solution.py
+++ b/solution.py
@@ -144,7 +144,13 @@
     return label * BITS, label * BITS + order_of(place, core, part).astype(jnp.float32)
 
 
-def column_codes(lab, rows, core, part):
+def column_orders(rows, core, part):
+    place = iota((rows, LANES), 0)
+    return order_of(place, core, part).astype(jnp.float32)
+
+
+def column_codes(lab, orders):
+    rows = orders.shape[0]
     sources = lab.shape[0]
     place = iota((rows, 1), 0)
     hot = (iota((rows, sources), 1) == source_of(place)).astype(jnp.bfloat16)
@@ -152,7 +158,7 @@
     chosen = iota((rows, LANES), 1) == lane_of(place)
     kept = jnp.where(chosen, spread, 0.0).astype(jnp.bfloat16)
     label = dot(kept, jnp.ones((LANES, LANES), jnp.bfloat16), ((1,), (0,)))
-    return label * BITS + order_of(place, core, part).astype(jnp.float32)
+    return label * BITS + orders
 
 
 def scan(best_ref, query_ref, key_ref, floor, ceiling, codes_ref, pick):
@@ -185,16 +191,14 @@
         scan(*args, lambda key, query: key > query)
 
 
-def store_groups(out_ref, best):
-    sources = out_ref.shape[0]
+def grouped(best, sources, shift):
     rows = best.shape[1]
     mine = iota((sources, rows), 0) == source_of(iota((1, rows), 1))
-    spots = (iota((rows, LANES), 1) == lane_of(iota((rows, 1), 0))).astype(jnp.bfloat16)
-    total = jnp.zeros((sources, LANES), jnp.float32)
-    for piece in split3(best):
-        spread = jnp.where(mine, piece.astype(jnp.float32), 0.0).astype(jnp.bfloat16)
-        total = total + dot(spread, spots, ((1,), (0,)))
-    out_ref[...] = total
+    spots = iota((rows, LANES), 1) == lane_of(iota((rows, 1), 0)) + shift
+    pieces = [jnp.where(mine, piece.astype(jnp.float32), 0.0) for piece in split3(best)]
+    spread = jnp.concatenate(pieces, axis=0).astype(jnp.bfloat16)
+    total = dot(spread, spots.astype(jnp.bfloat16), ((1,), (0,)))
+    return total[:sources] + total[sources : 2 * sources] + total[2 * sources :]
 
 
 def parts_of(where_ref):
@@ -209,50 +213,56 @@
     lab = notes_of(own_ref)
     floor, ceiling = row_codes(lab, rows, core, me)
     rows_ref[...] = jnp.concatenate([floor, ceiling] * 4, axis=0)
-    codes_ref[...] = column_codes(lab, rows, core, me)
+    codes_ref[...] = column_codes(lab, column_orders(rows, core, me))
     best_ref[...] = jnp.full((1, rows), -1.0, jnp.float32)
     scan(best_ref, own_ref, own_ref, floor, ceiling, codes_ref, lambda key, query: key <= query)
 
 
-def right_kernel(where_ref, alone_ref, own_ref, right_ref, rows_ref, best_ref, right_rows_ref, codes_ref):
+def right_kernel(
+    where_ref, alone_ref, own_ref, right_ref, rows_ref, best_ref, right_rows_ref, orders_ref, codes_ref
+):
     rows = best_ref.shape[1]
-    core, me, _, right = parts_of(where_ref)
+    core, me, left, right = parts_of(where_ref)
     best_ref[...] = alone_ref[...]
     lab = notes_of(right_ref)
     floor, ceiling = row_codes(lab, rows, core, right)
     right_rows_ref[...] = jnp.concatenate([floor, ceiling] * 4, axis=0)
-    codes_ref[...] = column_codes(lab, rows, core, right)
+    orders_ref[...] = column_orders(rows, core, left)
+    codes_ref[...] = column_codes(lab, column_orders(rows, core, right))
     scan_pair(
         best_ref, own_ref, right_ref, rows_ref[0:1, :], rows_ref[1:2, :], codes_ref, core, me, right
     )
 
 
-def cross_kernel(where_ref, left_ref, right_ref, rows_ref, out_ref, codes_ref, best_ref):
+def left_kernel(
+    where_ref, found_ref, own_ref, left_ref, right_ref, rows_ref, right_rows_ref, orders_ref,
+    out_ref, best_ref, cross_ref, codes_ref,
+):
     rows = best_ref.shape[1]
-    core, _, left, right = parts_of(where_ref)
-    codes_ref[...] = column_codes(notes_of(left_ref), rows, core, left)
-    best_ref[...] = jnp.full((1, rows), -1.0, jnp.float32)
-    scan_pair(
-        best_ref, right_ref, left_ref, rows_ref[0:1, :], rows_ref[1:2, :], codes_ref, core, right, left
-    )
-    store_groups(out_ref, best_ref[...])
-
-
-def left_kernel(where_ref, found_ref, own_ref, left_ref, rows_ref, codes_ref, out_ref, best_ref):
-    core, me, left, _ = parts_of(where_ref)
+    core, me, left, right = parts_of(where_ref)
     best_ref[...] = found_ref[...]
-    scan_pair(
-        best_ref, own_ref, left_ref, rows_ref[0:1, :], rows_ref[1:2, :], codes_ref, core, me, left
-    )
-    store_groups(out_ref, best_ref[...])
-
-
-def unpack_kernel(where_ref, back_ref, near_ref, far_ref, out_ref):
+    cross_ref[...] = jnp.full((1, rows), -1.0, jnp.float32)
+    codes_ref[...] = column_codes(notes_of(left_ref), orders_ref[...])
+    for bests, query_ref, lines_ref, part in (
+        (best_ref, own_ref, rows_ref, me),
+        (cross_ref, right_ref, right_rows_ref, right),
+    ):
+        scan_pair(
+            bests, query_ref, left_ref, lines_ref[0:1, :], lines_ref[1:2, :], codes_ref, core, part, left
+        )
+    sources = out_ref.shape[0]
+    out_ref[...] = grouped(best_ref[...], sources, 0) + grouped(cross_ref[...], sources, 2 * GROUP)
+
+
+def unpack_kernel(where_ref, back_ref, near_ref, far_ref, near_side_ref, far_side_ref, out_ref):
     half = near_ref.shape[0]
     rows = back_ref.shape[1]
     width = 2 * GROUP
     hot = (iota((2 * half, rows), 0) == back_ref[0:1, :]).astype(jnp.bfloat16)
-    results = jnp.concatenate([near_ref[:, :width], far_ref[:, :width]], axis=0)
+    results = jnp.maximum(
+        jnp.concatenate([near_ref[:, :width], far_ref[:, :width]], axis=0),
+        jnp.concatenate([near_side_ref[:, width : 2 * width], far_side_ref[:, width : 2 * width]], axis=0),
+    )
     total = jnp.zeros((width, rows), jnp.float32)
     for piece in split3(results):
         total = total + dot(piece, hot, ((0,), (0,)))
@@ -280,6 +290,12 @@
         (device(y, z, c, x), device(y, z, c, x + step) if c == 0 else device(y + step, z, c, x))
         for y, z, c, x in EVERY
     ]
+
+
+ACROSS = [
+    (device(y, z, c, x), device(y, z, 1, x + 1) if c == 0 else device(y + 1, z, 0, x))
+    for y, z, c, x in EVERY
+]
 
 
 def exchange(array):
@@ -319,20 +335,20 @@
     best, own_rows, back = call(
         alone_kernel, "alone", (where, own, back), (row, lines, ((8, rows), whole)), (codes,), 10**9
     )
-    best, right_rows = call(
-        right_kernel, "right", (where, best, own, right, own_rows), (row, lines), (codes,), 10**9
-    )
-    cross, left_codes = call(
-        cross_kernel, "cross", (where, left, right, right_rows), (groups, codes), (row,), 10**9
-    )
-    cross = lax.ppermute(cross, AXES, aside(1))
-    (best,) = call(
-        left_kernel, "left", (where, best, own, left, own_rows, left_codes), (groups,), (row,), 10**9
-    )
-    best = jnp.maximum(best, cross)
-    near = exchange(best.reshape(half, 1, LANES)).reshape(half, LANES)
-    far = lax.ppermute(near, AXES, SWAP)
-    (out,) = call(unpack_kernel, "unpack", (where, back, near, far), (row,))
+    best, right_rows, orders = call(
+        right_kernel, "right", (where, best, own, right, own_rows), (row, lines, codes), (codes,), 10**9
+    )
+    (found,) = call(
+        left_kernel,
+        "left",
+        (where, best, own, left, right, own_rows, right_rows, orders),
+        (groups,),
+        (row, row, codes),
+        10**9,
+    )
+    near = exchange(found.reshape(half, 1, LANES)).reshape(half, LANES)
+    sides = [lax.ppermute(near, AXES, pairs) for pairs in (SWAP, aside(1), ACROSS)]
+    (out,) = call(unpack_kernel, "unpack", (where, back, near, *sides), (row,))
     return out.reshape(rows)
 
 

time: 112 us -> 112 us (level)
  starting transfers between devices: 12.8 us -> 14.7 us
  Pallas kernels: 12.6 us -> 11.4 us
    ppermute x2 -> x3, starting transfers between devices: 6.38 us -> 8.29 us  [shards(): lax.ppermute(near, AXES, pairs)]
    pallas_call x7 -> x6, Pallas kernels: 12.6 us -> 11.4 us  [call(): pl.pallas_call(kernel, out_shape=tuple((jax.ShapeDtypeStruct(shape, kind)...]
    ppermute x2 -> x3, waiting for transfers between devices: 4.21 us -> 3.46 us  [shards(): lax.ppermute(near, AXES, pairs)]
  transfers between devices with their start and end apart: 5 -> 6, of which waited for: 5 -> 4; matrix products, arithmetic and copies ran while one was open for 0% -> 0% of each run, Pallas kernels for 6% -> 5%
where the time goes in v6:
time: 112 us
  blocking collectives  62.4 us (56%)
  waiting for transfers between devices  20.8 us (19%)
  starting transfers between devices  14.7 us (13%)
  Pallas kernels  11.4 us (10%)
  local copies, waits for them, and re-layouts  2.15 us (2%)
    all_to_all x2, blocking collectives, exchange(): lax.all_to_all(array, AXES, split_axis=0, concat_axis=0, axis_index_group...  62.4 us
    ppermute x1, waiting for transfers between devices, shards(): lax.ppermute(own, AXES, aside(-1))  15.3 us
    pallas_call x6, Pallas kernels, call(): pl.pallas_call(kernel, out_shape=tuple((jax.ShapeDtypeStruct(shape, kind)...  11.4 us
    ppermute x3, starting transfers between devices, shards(): lax.ppermute(near, AXES, pairs)  8.29 us
    ppermute x3, waiting for transfers between devices, shards(): lax.ppermute(near, AXES, pairs)  3.46 us
    ppermute x1, starting transfers between devices, shards(): got = lax.ppermute(send, AXES, SWAP)  3.33 us
    ppermute x1, starting transfers between devices, shards(): lax.ppermute(own, AXES, aside(-1))  3.07 us
  transfers between devices with their start and end apart: 6, of which 4 were waited for; matrix products, arithmetic and copies ran while one was open for 0% of the time, Pallas kernels for 5%

profile of v6, /device:TPU:1, one launch (start us, length us, event | category | flops | bytes accessed | tf_op | source)
XLA Modules:
  0.0 111.8 jit_solution(11551534110212572285)
XLA Ops:
  0.0 0.1 pad_add_fusion.where_ref
  0.1 0.0 copy-start
  0.1 1.4 %copy-done = bf16[1024,768]{1,0:T(8,128)(2,1)S(1)} copy-done((bf16[1024,768]{1,0:T(8,128)(2,1)S(1)}, bf16[1024,768]{1,0:T(8,128)(2,1)}, u32[]{:S(2)}) %copy-start) | copy-done | bytes 1572888
  1.5 0.0 copy-start.1
  1.5 0.7 copy-done.1
  2.2 2.3 %send.1 = (bf16[32,104,128]{2,1,0:T(8,128)(2,1)S(1)}, bf16[32,8,128]{2,1,0:T(8,128)(2,1)S(1)}, bf16[1024,768]{1,0:T(8,128)(2,1)S(1)}, s32[8,1024]{1,0:T(8,128)S(1)}) custom-call(s32[3]{0:T(128)S(1)} %pad_add_fusion.where_ref, bf16[1024,768]{1,0:T(8,128)(2,1)S(1)} %copy-done, s32[1,1024]{1,0:T(1,128)S(1)} %bitcast.13), custom_call_target="tpu_custom_call" | custom-call | bytes 1048576 | tf_op jit(solution)/shard_map/send/pallas_call | solution.py:48
  4.5 3.3 %collective-permute-start = (bf16[32,104,128]{2,1,0:T(8,128)(2,1)S(1)}, bf16[32,104,128]{2,1,0:T(8,128)(2,1)S(1)}, u32[]{:S(2)}, u32[]{:S(2)}) collective-permute-start(bf16[32,104,128]{2,1,0:T(8,128)(2,1)S(1)} %get-tuple-element.17), channel_id=1, source_target_pairs={{0,4},{1,5},{2,6},{3,7},{4,0},{5,1},{6,2},{7,3},{8,12},{9,13},{10,... | collective-permute-start | bytes 2555912 | tf_op jit(solution)/shard_map/ppermute | solution.py:326
  7.8 1.5 %keep.1 = bf16[32,96,128]{2,1,0:T(8,128)(2,1)S(1)} custom-call(s32[3]{0:T(128)S(1)} %pad_add_fusion.where_ref, bf16[1024,768]{1,0:T(8,128)(2,1)S(1)} %get-tuple-element.15.unit_ref, s32[8,1024]{1,0:T(8,128)S(1)} %get-tuple-element.16.rows_ref.back_ref), custom_call_target="tpu_custom_call" | custom-call | flops 1000000000 | bytes 1048576 | tf_op jit(solution)/shard_map/keep/pallas_call | solution.py:48
  9.4 0.5 collective-permute-done
  9.8 0.1 slice.8
  9.9 0.1 pad_maximum_fusion
  10.0 49.0 %all_to_all.10.own_ref = bf16[32,200,128]{2,1,0:T(8,128)(2,1)S(1)} all-to-all(bf16[32,200,128]{2,1,0:T(8,128)(2,1)S(1)} %pad_maximum_fusion), channel_id=1, replica_groups={{0,8,16,24,32,40,48,56,64,72,80,88,96,104,112,120,128,136,144,152,160,1..., dimensions={0} | all-to-all | bytes 3276800 | tf_op jit(solution)/shard_map/all_to_all | solution.py:302
  59.0 3.1 %collective-permute-start.1 = (bf16[32,200,128]{2,1,0:T(8,128)(2,1)S(1)}, bf16[32,200,128]{2,1,0:T(8,128)(2,1)S(1)}, u32[]{:S(2)}, u32[]{:S(2)}) collective-permute-start(bf16[32,200,128]{2,1,0:T(8,128)(2,1)S(1)} %all_to_all.10.own_ref), channel_id=1, source_target_pairs={{0,3},{1,0},{2,1},{3,2},{4,196},{5,197},{6,198},{7,199},{8,11},{9,... | collective-permute-start | bytes 4915208 | tf_op jit(solution)/shard_map/ppermute | solution.py:332
  62.1 0.0 collective-permute-start.2
  62.1 2.8 %alone.1 = (f32[1,1024]{1,0:T(1,128)S(1)}, f32[8,1024]{1,0:T(8,128)S(1)}, s32[8,1024]{1,0:T(8,128)S(1)}) custom-call(s32[3]{0:T(128)S(1)} %pad_add_fusion.where_ref, bf16[32,200,128]{2,1,0:T(8,128)(2,1)S(1)} %all_to_all.10.own_ref, s32[8,1024]{1,0:T(8,128)S(1)} %get-tuple-element.16.rows_ref.back_ref), custom_call_target="tpu_custom_call" | custom-call | flops 1000000000 | bytes 1048576 | tf_op jit(solution)/shard_map/alone/pallas_call | solution.py:48
  64.9 15.3 %collective-permute-done.1.right_ref = bf16[32,200,128]{2,1,0:T(8,128)(2,1)S(1)} collective-permute-done((bf16[32,200,128]{2,1,0:T(8,128)(2,1)S(1)}, bf16[32,200,128]{2,1,0:T(8,128)(2,1)S(1)}, u32[]{:S(2)}, u32[]{:S(2)}) %collective-permute-start.1) | collective-permute-done | bytes 1638432 | tf_op jit(solution)/shard_map/ppermute | solution.py:332
  80.2 1.8 %right.1 = (f32[1,1024]{1,0:T(1,128)S(1)}, f32[8,1024]{1,0:T(8,128)S(1)}, f32[1024,128]{1,0:T(8,128)S(1)}) custom-call(s32[3]{0:T(128)S(1)} %pad_add_fusion.where_ref, f32[1,1024]{1,0:T(1,128)S(1)} %get-tuple-element.20.alone_ref, bf16[32,200,128]{2,1,0:T(8,128)(2,1)S(1)} %all_to_all.10.own_ref, bf16[32,200,128]{2,1,0:T(8,128)(2,1)S(1)} %collective-permute-done.1.right_ref, ...), custom_call_target="tpu_custom_call" | custom-call | flops 1000000000 | bytes 1048576 | tf_op jit(solution)/shard_map/right/pallas_call | solution.py:48
  82.0 1.6 %collective-permute-done.2.left_ref = bf16[32,200,128]{2,1,0:T(8,128)(2,1)S(1)} collective-permute-done((bf16[32,200,128]{2,1,0:T(8,128)(2,1)S(1)}, bf16[32,200,128]{2,1,0:T(8,128)(2,1)S(1)}, u32[]{:S(2)}, u32[]{:S(2)}) %collective-permute-start.2) | collective-permute-done | bytes 1638432 | tf_op jit(solution)/shard_map/ppermute | solution.py:332
  83.6 1.5 %left.1 = f32[32,128]{1,0:T(8,128)S(1)} custom-call(s32[3]{0:T(128)S(1)} %pad_add_fusion.where_ref, f32[1,1024]{1,0:T(1,128)S(1)} %get-tuple-element.22.found_ref, bf16[32,200,128]{2,1,0:T(8,128)(2,1)S(1)} %all_to_all.10.own_ref, bf16[32,200,128]{2,1,0:T(8,128)(2,1)S(1)} %collective-permute-done.2.left_ref, ...), custom_call_target="tpu_custom_call" | custom-call | flops 1000000000 | bytes 1048576 | tf_op jit(solution)/shard_map/left/pallas_call | solution.py:48
  85.1 13.4 %all_to_all.11 = f32[32,1,128]{2,1,0:T(1,128)S(1)} all-to-all(f32[32,1,128]{2,1,0:T(1,128)S(1)} %bitcast.8), channel_id=1, replica_groups={{0,8,16,24,32,40,48,56,64,72,80,88,96,104,112,120,128,136,144,152,160,1..., dimensions={0} | all-to-all | bytes 32768 | tf_op jit(solution)/shard_map/all_to_all | solution.py:302
  98.6 7.6 %collective-permute-start.5 = (f32[32,128]{1,0:T(8,128)S(1)}, f32[32,128]{1,0:T(8,128)S(1)}, u32[]{:S(2)}, u32[]{:S(2)}) collective-permute-start(f32[32,128]{1,0:T(8,128)S(1)} %bitcast.9), channel_id=1, source_target_pairs={{0,5},{1,6},{2,7},{3,4},{4,64},{5,65},{6,66},{7,67},{8,13},{9,14},... | collective-permute-start | bytes 49160 | tf_op jit(solution)/shard_map/ppermute | solution.py:350
  106.1 0.3 collective-permute-start.4
  106.4 0.4 collective-permute-start.3
  106.8 3.5 %collective-permute-done.5.far_side_ref = f32[32,128]{1,0:T(8,128)S(1)} collective-permute-done((f32[32,128]{1,0:T(8,128)S(1)}, f32[32,128]{1,0:T(8,128)S(1)}, u32[]{:S(2)}, u32[]{:S(2)}) %collective-permute-start.5) | collective-permute-done | bytes 16416 | tf_op jit(solution)/shard_map/ppermute | solution.py:350
  110.3 0.0 collective-permute-done.4.near_side_ref
  110.3 0.0 collective-permute-done.3.far_ref
  110.3 1.5 %unpack.1 = f32[1,1024]{1,0:T(1,128)} custom-call(s32[3]{0:T(128)S(1)} %pad_add_fusion.where_ref, s32[8,1024]{1,0:T(8,128)S(1)} %get-tuple-element.19.back_ref, f32[32,128]{1,0:T(8,128)S(1)} %bitcast.12, f32[32,128]{1,0:T(8,128)S(1)} %collective-permute-done.3.far_ref, f32[32,128]{1,0:T(8,128)S(1)} %collective-permute-done.4.near_side_ref, ...), custom_call_target="tpu_custom_call" | custom-call | bytes 1048576 | tf_op jit(solution)/shard_map/unpack/pallas_call | solution.py:48
  (1 shorter events, 0.0 us)
Async XLA Ops:
  0.1 1.4 %copy-start = (bf16[1024,768]{1,0:T(8,128)(2,1)S(1)}, bf16[1024,768]{1,0:T(8,128)(2,1)}, u32[]{:S(2)}) copy-start(bf16[1024,768]{1,0:T(8,128)(2,1)} %emb_ref.1) | copy-start | bytes 4718596
  1.5 0.7 copy-start.1
  4.5 5.3 %collective-permute-start = (bf16[32,104,128]{2,1,0:T(8,128)(2,1)S(1)}, bf16[32,104,128]{2,1,0:T(8,128)(2,1)S(1)}, u32[]{:S(2)}, u32[]{:S(2)}) collective-permute-start(bf16[32,104,128]{2,1,0:T(8,128)(2,1)S(1)} %get-tuple-element.17), channel_id=1, source_target_pairs={{0,4},{1,5},{2,6},{3,7},{4,0},{5,1},{6,2},{7,3},{8,12},{9,13},{10,... | collective-permute-start | bytes 2555912 | tf_op jit(solution)/shard_map/ppermute | solution.py:326
  59.0 21.1 %collective-permute-start.1 = (bf16[32,200,128]{2,1,0:T(8,128)(2,1)S(1)}, bf16[32,200,128]{2,1,0:T(8,128)(2,1)S(1)}, u32[]{:S(2)}, u32[]{:S(2)}) collective-permute-start(bf16[32,200,128]{2,1,0:T(8,128)(2,1)S(1)} %all_to_all.10.own_ref), channel_id=1, source_target_pairs={{0,3},{1,0},{2,1},{3,2},{4,196},{5,197},{6,198},{7,199},{8,11},{9,... | collective-permute-start | bytes 4915208 | tf_op jit(solution)/shard_map/ppermute | solution.py:332
  62.1 21.5 %collective-permute-start.2 = (bf16[32,200,128]{2,1,0:T(8,128)(2,1)S(1)}, bf16[32,200,128]{2,1,0:T(8,128)(2,1)S(1)}, u32[]{:S(2)}, u32[]{:S(2)}) collective-permute-start(bf16[32,200,128]{2,1,0:T(8,128)(2,1)S(1)} %all_to_all.10.own_ref), channel_id=1, source_target_pairs={{0,1},{1,2},{2,3},{3,0},{4,68},{5,69},{6,70},{7,71},{8,9},{9,10},{... | collective-permute-start | bytes 4915208 | tf_op jit(solution)/shard_map/ppermute | solution.py:332
  98.6 11.7 %collective-permute-start.5 = (f32[32,128]{1,0:T(8,128)S(1)}, f32[32,128]{1,0:T(8,128)S(1)}, u32[]{:S(2)}, u32[]{:S(2)}) collective-permute-start(f32[32,128]{1,0:T(8,128)S(1)} %bitcast.9), channel_id=1, source_target_pairs={{0,5},{1,6},{2,7},{3,4},{4,64},{5,65},{6,66},{7,67},{8,13},{9,14},... | collective-permute-start | bytes 49160 | tf_op jit(solution)/shard_map/ppermute | solution.py:350
  106.1 4.1 %collective-permute-start.4 = (f32[32,128]{1,0:T(8,128)S(1)}, f32[32,128]{1,0:T(8,128)S(1)}, u32[]{:S(2)}, u32[]{:S(2)}) collective-permute-start(f32[32,128]{1,0:T(8,128)S(1)} %bitcast.10), channel_id=1, source_target_pairs={{0,1},{1,2},{2,3},{3,0},{4,68},{5,69},{6,70},{7,71},{8,9},{9,10},{... | collective-permute-start | bytes 49160 | tf_op jit(solution)/shard_map/ppermute | solution.py:350
  106.4 3.9 %collective-permute-start.3 = (f32[32,128]{1,0:T(8,128)S(1)}, f32[32,128]{1,0:T(8,128)S(1)}, u32[]{:S(2)}, u32[]{:S(2)}) collective-permute-start(f32[32,128]{1,0:T(8,128)S(1)} %bitcast.11), channel_id=1, source_target_pairs={{0,4},{1,5},{2,6},{3,7},{4,0},{5,1},{6,2},{7,3},{8,12},{9,13},{10,... | collective-permute-start | bytes 49160 | tf_op jit(solution)/shard_map/ppermute | solution.py:350

commit v7 on v6

--- a/solution.py
+++ b/solution.py
@@ -30,10 +30,19 @@
 NOTE = 8
 
 
-def slot_of(clusters, core, half):
+STEPS = (0, 1, 7, 2, 6, 3, 5, 4)
+CUT = 5
+
+
+def slot_of(clusters, where_ref, half):
+    core, deep = where_ref[1], where_ref[4]
     owner = clusters // 2
-    away = jnp.where(owner // half == core, 0, 1)
-    return owner % half + away * half, away
+    kind, index = owner // half, owner % half
+    away = jnp.where(kind == core, 0, 1)
+    by_row = kind == 0
+    side = jnp.where(by_row, index // 8, index % 4) - jnp.where(by_row, where_ref[5], where_ref[6])
+    ahead = jnp.where(by_row, index % 8, index // 4) - deep
+    return index + away * half, (ahead & 7) * 4 + (side & 3) + away * half, away
 
 
 def smem():
@@ -74,14 +83,14 @@
     rows = emb_ref.shape[0]
     half = send_ref.shape[0]
     clusters = clu_ref[...]
-    slot, away = slot_of(clusters, where_ref[1], half)
+    home, slot, away = slot_of(clusters, where_ref, half)
     hot = (iota((2 * half, rows), 0) == slot).astype(jnp.bfloat16)
     before = (iota((rows, rows), 0) < iota((rows, rows), 1)).astype(jnp.bfloat16)
     count = dot(hot, before, ((1,), (0,)))
     rank = jnp.sum(hot.astype(jnp.float32) * count, axis=0, keepdims=True).astype(jnp.int32)
     spot = rank + away * GROUP
     place = slot * GROUP + rank
-    rows_ref[...] = jnp.concatenate([slot, spot, place, place] * 2, axis=0)
+    rows_ref[...] = jnp.concatenate([home, spot, place, place] * 2, axis=0)
     bit = (clusters % 2).astype(jnp.float32)
     spots = jnp.where(iota((LANES, rows), 0) == spot, bit, 0.0).astype(jnp.bfloat16)
     labels = dot(hot, spots, ((1,), (1,))).astype(jnp.bfloat16)
@@ -98,26 +107,38 @@
     put_rows(keep_ref, unit_ref, rows_ref[2:3, :], 0)
 
 
-def source_of(place):
-    return place // TILE * (TILE // (2 * GROUP)) + place % (TILE // 2) // GROUP
+def cell_of(place, spot):
+    turn = place // TILE - spot[0]
+    return (turn & 3) * 8 + place % (TILE // 2) // GROUP
+
+
+def origin_of(place, spot):
+    k = place % (TILE // 2) // GROUP
+    step = jnp.where(k % 2 == 1, (k + 1) // 2, 8 - k // 2)
+    return place // TILE, (spot[1] - step) & 7
+
+
+def source_of(place, spot, core):
+    side, deep = origin_of(place, spot)
+    return jnp.where(core == 0, side * 8 + deep, deep * 4 + side)
 
 
 def lane_of(place):
     return place // (TILE // 2) % 2 * GROUP + place % GROUP
 
 
-def order_of(place, core, part):
-    source, flip, rank = source_of(place), place // (TILE // 2) % 2, place % GROUP
+def order_of(place, spot, core, part):
+    side, deep = origin_of(place, spot)
+    flip, rank = place // (TILE // 2) % 2, place % GROUP
     from_core = jnp.where(flip == 0, core, 1 - core)
-    by_row = (source * 2 + from_core) * 4 + part
-    by_column = ((part * 8 + source // 4) * 2 + from_core) * 4 + source % 4
-    return jnp.where(core == 0, by_row, by_column) * GROUP + rank
-
-
-def tile_of(ref, index):
+    y, x = jnp.where(core == 0, side, part), jnp.where(core == 0, part, side)
+    return (((y * 8 + deep) * 2 + from_core) * 4 + x) * GROUP + rank
+
+
+def tile_of(ref, index, spot):
     each = TILE // (2 * GROUP)
     data = (ref.shape[1] - NOTE) // 2
-    here = slice(index * each, (index + 1) * each)
+    here = pl.ds(((index - spot[0]) & 3) * each, each)
     lanes = []
     for base in range(0, data, GROUP):
         parts = [
@@ -133,27 +154,27 @@
     return (jnp.sum(ref[:, data:, :].astype(jnp.float32), axis=1) * (1.0 / NOTE)).astype(jnp.bfloat16)
 
 
-def row_codes(lab, rows, core, part):
+def row_codes(lab, rows, spot, core, part):
     sources = lab.shape[0]
     width = 2 * GROUP
     place = iota((1, rows), 1)
-    hot = (iota((sources, rows), 0) == source_of(place)).astype(jnp.bfloat16)
+    hot = (iota((sources, rows), 0) == cell_of(place, spot)).astype(jnp.bfloat16)
     spread = dot(lab[:, :width], hot, ((0,), (0,)))
     chosen = iota((width, rows), 0) == lane_of(place)
     label = jnp.sum(jnp.where(chosen, spread, 0.0), axis=0, keepdims=True)
-    return label * BITS, label * BITS + order_of(place, core, part).astype(jnp.float32)
-
-
-def column_orders(rows, core, part):
+    return label * BITS, label * BITS + order_of(place, spot, core, part).astype(jnp.float32)
+
+
+def column_orders(rows, spot, core, part):
     place = iota((rows, LANES), 0)
-    return order_of(place, core, part).astype(jnp.float32)
-
-
-def column_codes(lab, orders):
+    return order_of(place, spot, core, part).astype(jnp.float32)
+
+
+def column_codes(lab, orders, spot):
     rows = orders.shape[0]
     sources = lab.shape[0]
     place = iota((rows, 1), 0)
-    hot = (iota((rows, sources), 1) == source_of(place)).astype(jnp.bfloat16)
+    hot = (iota((rows, sources), 1) == cell_of(place, spot)).astype(jnp.bfloat16)
     spread = dot(hot, lab, ((1,), (0,)))
     chosen = iota((rows, LANES), 1) == lane_of(place)
     kept = jnp.where(chosen, spread, 0.0).astype(jnp.bfloat16)
@@ -161,16 +182,16 @@
     return label * BITS + orders
 
 
-def scan(best_ref, query_ref, key_ref, floor, ceiling, codes_ref, pick):
+def scan(best_ref, query_ref, key_ref, floor, ceiling, codes_ref, spot, pick):
     tiles = best_ref.shape[1] // TILE
     for query in range(tiles):
-        queries = tile_of(query_ref, query)
+        queries = tile_of(query_ref, query, spot)
         here = slice(query * TILE, (query + 1) * TILE)
         best = best_ref[:, here]
         for key in range(tiles):
             if not pick(key, query):
                 continue
-            sims = dot(tile_of(key_ref, key), queries, ((1,), (1,)))
+            sims = dot(tile_of(key_ref, key, spot), queries, ((1,), (1,)))
             codes = codes_ref[key * TILE : (key + 1) * TILE, :]
             codes = jnp.concatenate([codes] * (TILE // LANES), axis=1)
             mask = (codes >= floor[:, here]) & (codes < ceiling[:, here])
@@ -179,8 +200,8 @@
         best_ref[:, here] = best
 
 
-def scan_pair(best_ref, query_ref, key_ref, floor, ceiling, codes_ref, core, part, key_part):
-    args = (best_ref, query_ref, key_ref, floor, ceiling, codes_ref)
+def scan_pair(best_ref, query_ref, key_ref, floor, ceiling, codes_ref, spot, core, part, key_part):
+    args = (best_ref, query_ref, key_ref, floor, ceiling, codes_ref, spot)
 
     @pl.when((core == 0) | (key_part < part))
     def _():
@@ -191,9 +212,9 @@
         scan(*args, lambda key, query: key > query)
 
 
-def grouped(best, sources, shift):
+def grouped(best, sources, spot, core, shift):
     rows = best.shape[1]
-    mine = iota((sources, rows), 0) == source_of(iota((1, rows), 1))
+    mine = iota((sources, rows), 0) == source_of(iota((1, rows), 1), spot, core)
     spots = iota((rows, LANES), 1) == lane_of(iota((rows, 1), 0)) + shift
     pieces = [jnp.where(mine, piece.astype(jnp.float32), 0.0) for piece in split3(best)]
     spread = jnp.concatenate(pieces, axis=0).astype(jnp.bfloat16)
@@ -203,34 +224,40 @@
 
 def parts_of(where_ref):
     me, core, parts = where_ref[0], where_ref[1], where_ref[2]
-    return core, me, lax.rem(me + parts - 1, parts), lax.rem(me + 1, parts)
+    spot = where_ref[3], where_ref[4]
+    return spot, core, me, lax.rem(me + parts - 1, parts), lax.rem(me + 1, parts)
 
 
 def alone_kernel(where_ref, own_ref, back_ref, best_ref, rows_ref, kept_ref, codes_ref):
     rows = best_ref.shape[1]
-    core, me, _, _ = parts_of(where_ref)
+    spot, core, me, _, _ = parts_of(where_ref)
     kept_ref[...] = back_ref[...]
     lab = notes_of(own_ref)
-    floor, ceiling = row_codes(lab, rows, core, me)
+    floor, ceiling = row_codes(lab, rows, spot, core, me)
     rows_ref[...] = jnp.concatenate([floor, ceiling] * 4, axis=0)
-    codes_ref[...] = column_codes(lab, column_orders(rows, core, me))
+    codes_ref[...] = column_codes(lab, column_orders(rows, spot, core, me), spot)
     best_ref[...] = jnp.full((1, rows), -1.0, jnp.float32)
-    scan(best_ref, own_ref, own_ref, floor, ceiling, codes_ref, lambda key, query: key <= query)
+    args = (best_ref, own_ref, own_ref, floor, ceiling, codes_ref, spot)
+    scan(*args, lambda key, query: key <= query)
+
+    @pl.when(core != 0)
+    def _():
+        scan(*args, lambda key, query: key > query)
 
 
 def right_kernel(
     where_ref, alone_ref, own_ref, right_ref, rows_ref, best_ref, right_rows_ref, orders_ref, codes_ref
 ):
     rows = best_ref.shape[1]
-    core, me, left, right = parts_of(where_ref)
+    spot, core, me, left, right = parts_of(where_ref)
     best_ref[...] = alone_ref[...]
     lab = notes_of(right_ref)
-    floor, ceiling = row_codes(lab, rows, core, right)
+    floor, ceiling = row_codes(lab, rows, spot, core, right)
     right_rows_ref[...] = jnp.concatenate([floor, ceiling] * 4, axis=0)
-    orders_ref[...] = column_orders(rows, core, left)
-    codes_ref[...] = column_codes(lab, column_orders(rows, core, right))
+    orders_ref[...] = column_orders(rows, spot, core, left)
+    codes_ref[...] = column_codes(lab, column_orders(rows, spot, core, right), spot)
     scan_pair(
-        best_ref, own_ref, right_ref, rows_ref[0:1, :], rows_ref[1:2, :], codes_ref, core, me, right
+        best_ref, own_ref, right_ref, rows_ref[0:1, :], rows_ref[1:2, :], codes_ref, spot, core, me, right
     )
 
 
@@ -239,19 +266,21 @@
     out_ref, best_ref, cross_ref, codes_ref,
 ):
     rows = best_ref.shape[1]
-    core, me, left, right = parts_of(where_ref)
+    spot, core, me, left, right = parts_of(where_ref)
     best_ref[...] = found_ref[...]
     cross_ref[...] = jnp.full((1, rows), -1.0, jnp.float32)
-    codes_ref[...] = column_codes(notes_of(left_ref), orders_ref[...])
+    codes_ref[...] = column_codes(notes_of(left_ref), orders_ref[...], spot)
     for bests, query_ref, lines_ref, part in (
         (best_ref, own_ref, rows_ref, me),
         (cross_ref, right_ref, right_rows_ref, right),
     ):
         scan_pair(
-            bests, query_ref, left_ref, lines_ref[0:1, :], lines_ref[1:2, :], codes_ref, core, part, left
+            bests, query_ref, left_ref, lines_ref[0:1, :], lines_ref[1:2, :], codes_ref, spot, core, part, left
         )
     sources = out_ref.shape[0]
-    out_ref[...] = grouped(best_ref[...], sources, 0) + grouped(cross_ref[...], sources, 2 * GROUP)
+    out_ref[...] = grouped(
+        best_ref[...], sources, spot, core, 0
+    ) + grouped(cross_ref[...], sources, spot, core, 2 * GROUP)
 
 
 def unpack_kernel(where_ref, back_ref, near_ref, far_ref, near_side_ref, far_side_ref, out_ref):
@@ -298,9 +327,32 @@
 ]
 
 
+def ahead(step):
+    return [(device(y, z, c, x), device(y, z + step, c, x)) for y, z, c, x in EVERY]
+
+
+def sideways(step):
+    return [
+        (device(y, z, c, x), device(y + step, z, c, x) if c == 0 else device(y, z, c, x + step))
+        for y, z, c, x in EVERY
+    ]
+
+
 def exchange(array):
     return lax.all_to_all(
         array, AXES, split_axis=0, concat_axis=0, axis_index_groups=GROUPS, tiled=True
+    )
+
+
+def merge(early, late):
+    rest = NZ - CUT
+    return jnp.concatenate(
+        [
+            cells[turn * size : (turn + 1) * size]
+            for turn in range(NY)
+            for cells, size in ((early, CUT), (late, rest))
+        ],
+        axis=0,
     )
 
 
@@ -310,7 +362,9 @@
     data = GROUP * (depth // LANES)
     dp, x = lax.axis_index("dp"), lax.axis_index("help")
     core, y = dp % 2, dp // (2 * NZ)
-    where = jnp.stack([jnp.where(core == 0, x, y), core, jnp.int32(NX)])
+    deep, first = dp // 2 % NZ, core == 0
+    part, side = jnp.where(first, x, y), jnp.where(first, y, x)
+    where = jnp.stack([part, core, jnp.int32(NX), side, deep, y, x])
     half_float, full_float, whole = jnp.bfloat16, jnp.float32, jnp.int32
     send, notes, unit, back = call(
         send_kernel,
@@ -328,8 +382,22 @@
         keep_kernel, "keep", (where, unit, back), (((half, data, LANES), half_float),), flops=10**9
     )
     outgoing = jnp.concatenate([keep, got[:, :data], notes + got[:, data:]], axis=1)
-    own = exchange(outgoing)
-    left, right = lax.ppermute(own, AXES, aside(1)), lax.ppermute(own, AXES, aside(-1))
+    passed = {
+        step: outgoing[step * NY : (step + 1) * NY]
+        if step == 0
+        else lax.ppermute(outgoing[step * NY : (step + 1) * NY], AXES, ahead(step))
+        for step in STEPS
+    }
+    halves = []
+    for steps in (STEPS[:CUT], STEPS[CUT:]):
+        turned = []
+        for turn in (0, 3, 2, 1):
+            cells = jnp.concatenate([passed[step][turn : turn + 1] for step in steps], axis=0)
+            turned.append(lax.ppermute(cells, AXES, sideways(turn)) if turn else cells)
+        halves.append(jnp.concatenate(turned, axis=0))
+    own = merge(*halves)
+    left = merge(*[lax.ppermute(cells, AXES, aside(1)) for cells in halves])
+    right = merge(*[lax.ppermute(cells, AXES, aside(-1)) for cells in halves])
     row, lines = ((1, rows), full_float), ((8, rows), full_float)
     codes, groups = ((rows, LANES), full_float), ((half, LANES), full_float)
     best, own_rows, back = call(

time: 112 us -> 127 us (1.13)
  blocking collectives: 62.4 us -> 15.4 us
  waiting for transfers between devices: 20.8 us -> 52.7 us
  starting transfers between devices: 14.7 us -> 41.9 us
  Pallas kernels: 11.4 us -> 13.2 us
  local copies, waits for them, and re-layouts: 2.15 us -> 3.55 us
    all_to_all x2 -> x1, blocking collectives: 62.4 us -> 15.4 us  [exchange(): lax.all_to_all(array, AXES, split_axis=0, concat_axis=0, axis_index_group...]
    ppermute x2 -> x17, waiting for transfers between devices: 16.9 us -> 47.9 us  [the longest x7 20.8 us: shards(): lax.ppermute(outgoing[step * NY:(step + 1) * NY], AXES, ahead(step))]
    ppermute x2 -> x17, starting transfers between devices: 3.07 us -> 27.4 us  [the longest x7 15 us: shards(): lax.ppermute(outgoing[step * NY:(step + 1) * NY], AXES, ahead(step))]
    ppermute x3, starting transfers between devices: 8.29 us -> 11.2 us  [shards(): lax.ppermute(near, AXES, pairs)]
    pallas_call x6, Pallas kernels: 11.4 us -> 13.2 us  [call(): pl.pallas_call(kernel, out_shape=tuple((jax.ShapeDtypeStruct(shape, kind)...]
    unnamed x4 -> x30, local copies, waits for them, and re-layouts: 2.1 us -> 3.1 us
  transfers between devices with their start and end apart: 6 -> 21, of which waited for: 4 -> 16; matrix products, arithmetic and copies ran while one was open for 0% -> 1% of each run, Pallas kernels for 5% -> 6%
where the time goes in v7:
time: 127 us
  waiting for transfers between devices  52.7 us (41%)
  starting transfers between devices  41.9 us (33%)
  blocking collectives  15.4 us (12%)
  Pallas kernels  13.2 us (10%)
  local copies, waits for them, and re-layouts  3.55 us (3%)
    ppermute x7, waiting for transfers between devices, shards(): lax.ppermute(outgoing[step * NY:(step + 1) * NY], AXES, ahead(step))  20.8 us
    all_to_all x1, blocking collectives, exchange(): lax.all_to_all(array, AXES, split_axis=0, concat_axis=0, axis_index_group...  15.4 us
    ppermute x7, starting transfers between devices, shards(): lax.ppermute(outgoing[step * NY:(step + 1) * NY], AXES, ahead(step))  15 us
    pallas_call x6, Pallas kernels, call(): pl.pallas_call(kernel, out_shape=tuple((jax.ShapeDtypeStruct(shape, kind)...  13.2 us
    ppermute x6, waiting for transfers between devices, shards(): turned.append(lax.ppermute(cells, AXES, sideways(turn)) if turn else cells)  13.2 us
    ppermute x3, starting transfers between devices, shards(): lax.ppermute(near, AXES, pairs)  11.2 us
    ppermute x6, starting transfers between devices, shards(): turned.append(lax.ppermute(cells, AXES, sideways(turn)) if turn else cells)  8.26 us
    ppermute x2, waiting for transfers between devices, shards(): left = merge(*[lax.ppermute(cells, AXES, aside(1)) for cells in halves])  7.03 us
  transfers between devices with their start and end apart: 21, of which 16 were waited for; matrix products, arithmetic and copies ran while one was open for 1% of the time, Pallas kernels for 6%

profile of v7, /device:TPU:1, one launch (start us, length us, event | category | flops | bytes accessed | tf_op | source)
XLA Modules:
  0.0 127.3 jit_solution(1534824828330207265)
XLA Ops:
  0.0 0.1 stack.27.where_ref
  0.1 1.4 %copy-done = bf16[1024,768]{1,0:T(8,128)(2,1)S(1)} copy-done((bf16[1024,768]{1,0:T(8,128)(2,1)S(1)}, bf16[1024,768]{1,0:T(8,128)(2,1)}, u32[]{:S(2)}) %copy-start) | copy-done | bytes 1572888
  1.5 0.7 copy-done.1
  2.2 2.3 %send.1 = (bf16[32,104,128]{2,1,0:T(8,128)(2,1)S(1)}, bf16[32,8,128]{2,1,0:T(8,128)(2,1)S(1)}, bf16[1024,768]{1,0:T(8,128)(2,1)S(1)}, s32[8,1024]{1,0:T(8,128)S(1)}) custom-call(s32[7]{0:T(128)S(1)} %stack.27.where_ref, bf16[1024,768]{1,0:T(8,128)(2,1)S(1)} %copy-done, s32[1,1024]{1,0:T(1,128)S(1)} %bitcast.17), custom_call_target="tpu_custom_call" | custom-call | bytes 1048576 | tf_op jit(solution)/shard_map/send/pallas_call | solution.py:57
  4.5 3.3 %collective-permute-start = (bf16[32,104,128]{2,1,0:T(8,128)(2,1)S(1)}, bf16[32,104,128]{2,1,0:T(8,128)(2,1)S(1)}, u32[]{:S(2)}, u32[]{:S(2)}) collective-permute-start(bf16[32,104,128]{2,1,0:T(8,128)(2,1)S(1)} %get-tuple-element.17), channel_id=1, source_target_pairs={{0,4},{1,5},{2,6},{3,7},{4,0},{5,1},{6,2},{7,3},{8,12},{9,13},{10,... | collective-permute-start | bytes 2555912 | tf_op jit(solution)/shard_map/ppermute | solution.py:380
  7.9 1.5 %keep.1 = bf16[32,96,128]{2,1,0:T(8,128)(2,1)S(1)} custom-call(s32[7]{0:T(128)S(1)} %stack.27.where_ref, bf16[1024,768]{1,0:T(8,128)(2,1)S(1)} %get-tuple-element.15.unit_ref, s32[8,1024]{1,0:T(8,128)S(1)} %get-tuple-element.16.rows_ref.back_ref), custom_call_target="tpu_custom_call" | custom-call | flops 1000000000 | bytes 1048576 | tf_op jit(solution)/shard_map/keep/pallas_call | solution.py:57
  9.4 0.5 collective-permute-done
  9.9 0.1 pad_maximum_fusion
  10.1 0.1 fusion
  10.2 0.1 collective-permute-start.1
  10.3 3.9 %collective-permute-start.2 = (bf16[4,200,128]{2,1,0:T(8,128)(2,1)S(1)}, bf16[4,200,128]{2,1,0:T(8,128)(2,1)S(1)}, u32[]{:S(2)}, u32[]{:S(2)}) collective-permute-start(bf16[4,200,128]{2,1,0:T(8,128)(2,1)S(1)} %get-tuple-element.37), channel_id=1, source_target_pairs={{0,56},{1,57},{2,58},{3,59},{4,60},{5,61},{6,62},{7,63},{8,0},{9,1... | collective-permute-start | bytes 614408 | tf_op jit(solution)/shard_map/ppermute | solution.py:388
  14.2 3.6 %collective-permute-start.4 = (bf16[4,200,128]{2,1,0:T(8,128)(2,1)S(1)}, bf16[4,200,128]{2,1,0:T(8,128)(2,1)S(1)}, u32[]{:S(2)}, u32[]{:S(2)}) collective-permute-start(bf16[4,200,128]{2,1,0:T(8,128)(2,1)S(1)} %get-tuple-element.35), channel_id=1, source_target_pairs={{0,48},{1,49},{2,50},{3,51},{4,52},{5,53},{6,54},{7,55},{8,56},{9,... | collective-permute-start | bytes 614408 | tf_op jit(solution)/shard_map/ppermute | solution.py:388
  17.7 0.3 collective-permute-start.5
  18.1 1.1 collective-permute-done.1
  19.2 3.1 %collective-permute-start.6 = (bf16[4,200,128]{2,1,0:T(8,128)(2,1)S(1)}, bf16[4,200,128]{2,1,0:T(8,128)(2,1)S(1)}, u32[]{:S(2)}, u32[]{:S(2)}) collective-permute-start(bf16[4,200,128]{2,1,0:T(8,128)(2,1)S(1)} %get-tuple-element.33), channel_id=1, source_target_pairs={{0,40},{1,41},{2,42},{3,43},{4,44},{5,45},{6,46},{7,47},{8,48},{9,... | collective-permute-start | bytes 614408 | tf_op jit(solution)/shard_map/ppermute | solution.py:388
  22.4 4.0 %collective-permute-start.7 = (bf16[4,200,128]{2,1,0:T(8,128)(2,1)S(1)}, bf16[4,200,128]{2,1,0:T(8,128)(2,1)S(1)}, u32[]{:S(2)}, u32[]{:S(2)}) collective-permute-start(bf16[4,200,128]{2,1,0:T(8,128)(2,1)S(1)} %get-tuple-element.32), channel_id=1, source_target_pairs={{0,32},{1,33},{2,34},{3,35},{4,36},{5,37},{6,38},{7,39},{8,40},{9,... | collective-permute-start | bytes 614408 | tf_op jit(solution)/shard_map/ppermute | solution.py:388
  26.5 2.6 %collective-permute-done.4 = bf16[4,200,128]{2,1,0:T(8,128)(2,1)S(1)} collective-permute-done((bf16[4,200,128]{2,1,0:T(8,128)(2,1)S(1)}, bf16[4,200,128]{2,1,0:T(8,128)(2,1)S(1)}, u32[]{:S(2)}, u32[]{:S(2)}) %collective-permute-start.4) | collective-permute-done | bytes 204832 | tf_op jit(solution)/shard_map/ppermute | solution.py:388
  29.2 2.6 %collective-permute-start.8 = (bf16[5,200,128]{2,1,0:T(8,128)(2,1)S(1)}, bf16[5,200,128]{2,1,0:T(8,128)(2,1)S(1)}, u32[]{:S(2)}, u32[]{:S(2)}) collective-permute-start(bf16[5,200,128]{2,1,0:T(8,128)(2,1)S(1)} %get-tuple-element.63), channel_id=1, source_target_pairs={{0,192},{1,193},{2,194},{3,195},{4,7},{5,4},{6,5},{7,6},{8,200},{9... | collective-permute-start | bytes 768008 | tf_op jit(solution)/shard_map/ppermute | solution.py:396
  31.8 11.0 %collective-permute-done.5 = bf16[4,200,128]{2,1,0:T(8,128)(2,1)S(1)} collective-permute-done((bf16[4,200,128]{2,1,0:T(8,128)(2,1)S(1)}, bf16[4,200,128]{2,1,0:T(8,128)(2,1)S(1)}, u32[]{:S(2)}, u32[]{:S(2)}) %collective-permute-start.5) | collective-permute-done | bytes 204832 | tf_op jit(solution)/shard_map/ppermute | solution.py:388
  42.8 6.0 %collective-permute-done.6 = bf16[4,200,128]{2,1,0:T(8,128)(2,1)S(1)} collective-permute-done((bf16[4,200,128]{2,1,0:T(8,128)(2,1)S(1)}, bf16[4,200,128]{2,1,0:T(8,128)(2,1)S(1)}, u32[]{:S(2)}, u32[]{:S(2)}) %collective-permute-start.6) | collective-permute-done | bytes 204832 | tf_op jit(solution)/shard_map/ppermute | solution.py:388
  49.0 2.6 %collective-permute-start.9 = (bf16[3,200,128]{2,1,0:T(8,128)(2,1)S(1)}, bf16[3,200,128]{2,1,0:T(8,128)(2,1)S(1)}, u32[]{:S(2)}, u32[]{:S(2)}) collective-permute-start(bf16[3,200,128]{2,1,0:T(8,128)(2,1)S(1)} %pad_maximum_fusion.1), channel_id=1, source_target_pairs={{0,192},{1,193},{2,194},{3,195},{4,7},{5,4},{6,5},{7,6},{8,200},{9... | collective-permute-start | bytes 460808 | tf_op jit(solution)/shard_map/ppermute | solution.py:396
  51.5 0.5 collective-permute-start.10
  52.0 2.5 %collective-permute-start.11 = (bf16[3,200,128]{2,1,0:T(8,128)(2,1)S(1)}, bf16[3,200,128]{2,1,0:T(8,128)(2,1)S(1)}, u32[]{:S(2)}, u32[]{:S(2)}) collective-permute-start(bf16[3,200,128]{2,1,0:T(8,128)(2,1)S(1)} %pad_maximum_fusion.2), channel_id=1, source_target_pairs={{0,128},{1,129},{2,130},{3,131},{4,6},{5,7},{6,4},{7,5},{8,136},{9... | collective-permute-start | bytes 460808 | tf_op jit(solution)/shard_map/ppermute | solution.py:396
  54.6 0.1 constant_dynamic-update-slice_fusion.31
  54.7 3.4 %collective-permute-done.9 = bf16[3,200,128]{2,1,0:T(8,128)(2,1)S(1)} collective-permute-done((bf16[3,200,128]{2,1,0:T(8,128)(2,1)S(1)}, bf16[3,200,128]{2,1,0:T(8,128)(2,1)S(1)}, u32[]{:S(2)}, u32[]{:S(2)}) %collective-permute-start.9) | collective-permute-done | bytes 153632 | tf_op jit(solution)/shard_map/ppermute | solution.py:396
  58.1 0.3 collective-permute-done.10
  58.5 0.1 constant_dynamic-update-slice_fusion.30
  58.6 1.6 %collective-permute-done.11 = bf16[3,200,128]{2,1,0:T(8,128)(2,1)S(1)} collective-permute-done((bf16[3,200,128]{2,1,0:T(8,128)(2,1)S(1)}, bf16[3,200,128]{2,1,0:T(8,128)(2,1)S(1)}, u32[]{:S(2)}, u32[]{:S(2)}) %collective-permute-start.11) | collective-permute-done | bytes 153632 | tf_op jit(solution)/shard_map/ppermute | solution.py:396
  60.2 2.7 %collective-permute-done.12 = bf16[5,200,128]{2,1,0:T(8,128)(2,1)S(1)} collective-permute-done((bf16[5,200,128]{2,1,0:T(8,128)(2,1)S(1)}, bf16[5,200,128]{2,1,0:T(8,128)(2,1)S(1)}, u32[]{:S(2)}, u32[]{:S(2)}) %collective-permute-start.12) | collective-permute-done | bytes 256032 | tf_op jit(solution)/shard_map/ppermute | solution.py:396
  62.9 0.1 constant_dynamic-update-slice_fusion.29
  63.0 2.5 %collective-permute-start.14 = (bf16[20,200,128]{2,1,0:T(8,128)(2,1)S(1)}, bf16[20,200,128]{2,1,0:T(8,128)(2,1)S(1)}, u32[]{:S(2)}, u32[]{:S(2)}) collective-permute-start(bf16[20,200,128]{2,1,0:T(8,128)(2,1)S(1)} %get-tuple-element.39), channel_id=1, source_target_pairs={{0,3},{1,0},{2,1},{3,2},{4,196},{5,197},{6,198},{7,199},{8,11},{9,... | collective-permute-start | bytes 3072008 | tf_op jit(solution)/shard_map/ppermute | solution.py:400
  65.5 0.1 collective-permute-start.13
  65.6 5.3 %collective-permute-done.13 = bf16[3,200,128]{2,1,0:T(8,128)(2,1)S(1)} collective-permute-done((bf16[3,200,128]{2,1,0:T(8,128)(2,1)S(1)}, bf16[3,200,128]{2,1,0:T(8,128)(2,1)S(1)}, u32[]{:S(2)}, u32[]{:S(2)}) %collective-permute-start.13) | collective-permute-done | bytes 153632 | tf_op jit(solution)/shard_map/ppermute | solution.py:396
  70.9 0.5 collective-permute-start.15
  71.4 1.0 collective-permute-start.17
  72.5 4.2 %alone.1 = (f32[1,1024]{1,0:T(1,128)S(1)}, f32[8,1024]{1,0:T(8,128)S(1)}, s32[8,1024]{1,0:T(8,128)S(1)}) custom-call(s32[7]{0:T(128)S(1)} %stack.27.where_ref, bf16[32,200,128]{2,1,0:T(8,128)(2,1)S(1)} %get-tuple-element.81.own_ref, s32[8,1024]{1,0:T(8,128)S(1)} %get-tuple-element.16.rows_ref.back_ref), custom_call_target="tpu_custom_call" | custom-call | flops 1000000000 | bytes 1048576 | tf_op jit(solution)/shard_map/alone/pallas_call | solution.py:57
  76.7 0.3 collective-permute-done.14
  77.0 6.6 %collective-permute-done.15 = bf16[12,200,128]{2,1,0:T(8,128)(2,1)S(1)} collective-permute-done((bf16[12,200,128]{2,1,0:T(8,128)(2,1)S(1)}, bf16[12,200,128]{2,1,0:T(8,128)(2,1)S(1)}, u32[]{:S(2)}, u32[]{:S(2)}) %collective-permute-start.15) | collective-permute-done | bytes 614432 | tf_op jit(solution)/shard_map/ppermute | solution.py:400
  83.8 2.1 %right.1 = (f32[1,1024]{1,0:T(1,128)S(1)}, f32[8,1024]{1,0:T(8,128)S(1)}, f32[1024,128]{1,0:T(8,128)S(1)}) custom-call(s32[7]{0:T(128)S(1)} %stack.27.where_ref, f32[1,1024]{1,0:T(1,128)S(1)} %get-tuple-element.20.alone_ref, bf16[32,200,128]{2,1,0:T(8,128)(2,1)S(1)} %get-tuple-element.81.own_ref, ...), custom_call_target="tpu_custom_call" | custom-call | flops 1000000000 | bytes 1048576 | tf_op jit(solution)/shard_map/right/pallas_call | solution.py:57
  85.9 7.0 %collective-permute-done.16 = bf16[20,200,128]{2,1,0:T(8,128)(2,1)S(1)} collective-permute-done((bf16[20,200,128]{2,1,0:T(8,128)(2,1)S(1)}, bf16[20,200,128]{2,1,0:T(8,128)(2,1)S(1)}, u32[]{:S(2)}, u32[]{:S(2)}) %collective-permute-start.16) | collective-permute-done | bytes 1024032 | tf_op jit(solution)/shard_map/ppermute | solution.py:399
  93.2 1.6 %left.1 = f32[32,128]{1,0:T(8,128)S(1)} custom-call(s32[7]{0:T(128)S(1)} %stack.27.where_ref, f32[1,1024]{1,0:T(1,128)S(1)} %get-tuple-element.22.found_ref, bf16[32,200,128]{2,1,0:T(8,128)(2,1)S(1)} %get-tuple-element.81.own_ref, bf16[32,200,128]{2,1,0:T(8,128)(2,1)S(1)} %slice_dynamic-update-slice_fusion.8.left_ref, ...), custom_call_target="tpu_custom_call" | custom-call | flops 1000000000 | bytes 1048576 | tf_op jit(solution)/shard_map/left/pallas_call | solution.py:57
  94.8 15.4 %all_to_all.5 = f32[32,1,128]{2,1,0:T(1,128)S(1)} all-to-all(f32[32,1,128]{2,1,0:T(1,128)S(1)} %bitcast.12), channel_id=1, replica_groups={{0,8,16,24,32,40,48,56,64,72,80,88,96,104,112,120,128,136,144,152,160,1..., dimensions={0} | all-to-all | bytes 32768 | tf_op jit(solution)/shard_map/all_to_all | solution.py:342
  110.2 10.9 %collective-permute-start.18 = (f32[32,128]{1,0:T(8,128)S(1)}, f32[32,128]{1,0:T(8,128)S(1)}, u32[]{:S(2)}, u32[]{:S(2)}) collective-permute-start(f32[32,128]{1,0:T(8,128)S(1)} %bitcast.13), channel_id=1, source_target_pairs={{0,4},{1,5},{2,6},{3,7},{4,0},{5,1},{6,2},{7,3},{8,12},{9,13},{10,... | collective-permute-start | bytes 49160 | tf_op jit(solution)/shard_map/ppermute | solution.py:418
  121.1 0.3 collective-permute-start.19
  121.5 0.5 collective-permute-done.18.far_ref
  122.0 3.0 %collective-permute-done.19.near_side_ref = f32[32,128]{1,0:T(8,128)S(1)} collective-permute-done((f32[32,128]{1,0:T(8,128)S(1)}, f32[32,128]{1,0:T(8,128)S(1)}, u32[]{:S(2)}, u32[]{:S(2)}) %collective-permute-start.19) | collective-permute-done | bytes 16416 | tf_op jit(solution)/shard_map/ppermute | solution.py:418
  124.9 0.9 collective-permute-done.20.far_side_ref
  125.8 1.5 %unpack.1 = f32[1,1024]{1,0:T(1,128)} custom-call(s32[7]{0:T(128)S(1)} %stack.27.where_ref, s32[8,1024]{1,0:T(8,128)S(1)} %get-tuple-element.19.back_ref, f32[32,128]{1,0:T(8,128)S(1)} %bitcast.16, f32[32,128]{1,0:T(8,128)S(1)} %collective-permute-done.18.far_ref, f32[32,128]{1,0:T(8,128)S(1)} %collective-permute-done.19.near_side_ref, ...), custom_call_target="tpu_custom_call" | custom-call | bytes 1048576 | tf_op jit(solution)/shard_map/unpack/pallas_call | solution.py:57
  (44 shorter events, 1.1 us)
Async XLA Ops:
  0.1 1.4 %copy-start = (bf16[1024,768]{1,0:T(8,128)(2,1)S(1)}, bf16[1024,768]{1,0:T(8,128)(2,1)}, u32[]{:S(2)}) copy-start(bf16[1024,768]{1,0:T(8,128)(2,1)} %emb_ref.1) | copy-start | bytes 4718596
  1.5 0.7 copy-start.1
  4.5 5.3 %collective-permute-start = (bf16[32,104,128]{2,1,0:T(8,128)(2,1)S(1)}, bf16[32,104,128]{2,1,0:T(8,128)(2,1)S(1)}, u32[]{:S(2)}, u32[]{:S(2)}) collective-permute-start(bf16[32,104,128]{2,1,0:T(8,128)(2,1)S(1)} %get-tuple-element.17), channel_id=1, source_target_pairs={{0,4},{1,5},{2,6},{3,7},{4,0},{5,1},{6,2},{7,3},{8,12},{9,13},{10,... | collective-permute-start | bytes 2555912 | tf_op jit(solution)/shard_map/ppermute | solution.py:380
  10.2 9.1 %collective-permute-start.1 = (bf16[4,200,128]{2,1,0:T(8,128)(2,1)S(1)}, bf16[4,200,128]{2,1,0:T(8,128)(2,1)S(1)}, u32[]{:S(2)}, u32[]{:S(2)}) collective-permute-start(bf16[4,200,128]{2,1,0:T(8,128)(2,1)S(1)} %get-tuple-element.38), channel_id=1, source_target_pairs={{0,8},{1,9},{2,10},{3,11},{4,12},{5,13},{6,14},{7,15},{8,16},{9,17... | collective-permute-start | bytes 614408 | tf_op jit(solution)/shard_map/ppermute | solution.py:388
  10.3 12.1 %collective-permute-start.2 = (bf16[4,200,128]{2,1,0:T(8,128)(2,1)S(1)}, bf16[4,200,128]{2,1,0:T(8,128)(2,1)S(1)}, u32[]{:S(2)}, u32[]{:S(2)}) collective-permute-start(bf16[4,200,128]{2,1,0:T(8,128)(2,1)S(1)} %get-tuple-element.37), channel_id=1, source_target_pairs={{0,56},{1,57},{2,58},{3,59},{4,60},{5,61},{6,62},{7,63},{8,0},{9,1... | collective-permute-start | bytes 614408 | tf_op jit(solution)/shard_map/ppermute | solution.py:388
  14.2 12.3 %collective-permute-start.3 = (bf16[4,200,128]{2,1,0:T(8,128)(2,1)S(1)}, bf16[4,200,128]{2,1,0:T(8,128)(2,1)S(1)}, u32[]{:S(2)}, u32[]{:S(2)}) collective-permute-start(bf16[4,200,128]{2,1,0:T(8,128)(2,1)S(1)} %get-tuple-element.36), channel_id=1, source_target_pairs={{0,16},{1,17},{2,18},{3,19},{4,20},{5,21},{6,22},{7,23},{8,24},{9,... | collective-permute-start | bytes 614408 | tf_op jit(solution)/shard_map/ppermute | solution.py:388
  14.2 15.0 %collective-permute-start.4 = (bf16[4,200,128]{2,1,0:T(8,128)(2,1)S(1)}, bf16[4,200,128]{2,1,0:T(8,128)(2,1)S(1)}, u32[]{:S(2)}, u32[]{:S(2)}) collective-permute-start(bf16[4,200,128]{2,1,0:T(8,128)(2,1)S(1)} %get-tuple-element.35), channel_id=1, source_target_pairs={{0,48},{1,49},{2,50},{3,51},{4,52},{5,53},{6,54},{7,55},{8,56},{9,... | collective-permute-start | bytes 614408 | tf_op jit(solution)/shard_map/ppermute | solution.py:388
  17.7 25.0 %collective-permute-start.5 = (bf16[4,200,128]{2,1,0:T(8,128)(2,1)S(1)}, bf16[4,200,128]{2,1,0:T(8,128)(2,1)S(1)}, u32[]{:S(2)}, u32[]{:S(2)}) collective-permute-start(bf16[4,200,128]{2,1,0:T(8,128)(2,1)S(1)} %get-tuple-element.34), channel_id=1, source_target_pairs={{0,24},{1,25},{2,26},{3,27},{4,28},{5,29},{6,30},{7,31},{8,32},{9,... | collective-permute-start | bytes 614408 | tf_op jit(solution)/shard_map/ppermute | solution.py:388
  19.2 29.6 %collective-permute-start.6 = (bf16[4,200,128]{2,1,0:T(8,128)(2,1)S(1)}, bf16[4,200,128]{2,1,0:T(8,128)(2,1)S(1)}, u32[]{:S(2)}, u32[]{:S(2)}) collective-permute-start(bf16[4,200,128]{2,1,0:T(8,128)(2,1)S(1)} %get-tuple-element.33), channel_id=1, source_target_pairs={{0,40},{1,41},{2,42},{3,43},{4,44},{5,45},{6,46},{7,47},{8,48},{9,... | collective-permute-start | bytes 614408 | tf_op jit(solution)/shard_map/ppermute | solution.py:388
  22.4 26.5 %collective-permute-start.7 = (bf16[4,200,128]{2,1,0:T(8,128)(2,1)S(1)}, bf16[4,200,128]{2,1,0:T(8,128)(2,1)S(1)}, u32[]{:S(2)}, u32[]{:S(2)}) collective-permute-start(bf16[4,200,128]{2,1,0:T(8,128)(2,1)S(1)} %get-tuple-element.32), channel_id=1, source_target_pairs={{0,32},{1,33},{2,34},{3,35},{4,36},{5,37},{6,38},{7,39},{8,40},{9,... | collective-permute-start | bytes 614408 | tf_op jit(solution)/shard_map/ppermute | solution.py:388
  29.2 25.4 %collective-permute-start.8 = (bf16[5,200,128]{2,1,0:T(8,128)(2,1)S(1)}, bf16[5,200,128]{2,1,0:T(8,128)(2,1)S(1)}, u32[]{:S(2)}, u32[]{:S(2)}) collective-permute-start(bf16[5,200,128]{2,1,0:T(8,128)(2,1)S(1)} %get-tuple-element.63), channel_id=1, source_target_pairs={{0,192},{1,193},{2,194},{3,195},{4,7},{5,4},{6,5},{7,6},{8,200},{9... | collective-permute-start | bytes 768008 | tf_op jit(solution)/shard_map/ppermute | solution.py:396
  49.0 9.1 %collective-permute-start.9 = (bf16[3,200,128]{2,1,0:T(8,128)(2,1)S(1)}, bf16[3,200,128]{2,1,0:T(8,128)(2,1)S(1)}, u32[]{:S(2)}, u32[]{:S(2)}) collective-permute-start(bf16[3,200,128]{2,1,0:T(8,128)(2,1)S(1)} %pad_maximum_fusion.1), channel_id=1, source_target_pairs={{0,192},{1,193},{2,194},{3,195},{4,7},{5,4},{6,5},{7,6},{8,200},{9... | collective-permute-start | bytes 460808 | tf_op jit(solution)/shard_map/ppermute | solution.py:396
  51.5 7.0 %collective-permute-start.10 = (bf16[5,200,128]{2,1,0:T(8,128)(2,1)S(1)}, bf16[5,200,128]{2,1,0:T(8,128)(2,1)S(1)}, u32[]{:S(2)}, u32[]{:S(2)}) collective-permute-start(bf16[5,200,128]{2,1,0:T(8,128)(2,1)S(1)} %get-tuple-element.62), channel_id=1, source_target_pairs={{0,128},{1,129},{2,130},{3,131},{4,6},{5,7},{6,4},{7,5},{8,136},{9... | collective-permute-start | bytes 768008 | tf_op jit(solution)/shard_map/ppermute | solution.py:396
  52.0 8.1 %collective-permute-start.11 = (bf16[3,200,128]{2,1,0:T(8,128)(2,1)S(1)}, bf16[3,200,128]{2,1,0:T(8,128)(2,1)S(1)}, u32[]{:S(2)}, u32[]{:S(2)}) collective-permute-start(bf16[3,200,128]{2,1,0:T(8,128)(2,1)S(1)} %pad_maximum_fusion.2), channel_id=1, source_target_pairs={{0,128},{1,129},{2,130},{3,131},{4,6},{5,7},{6,4},{7,5},{8,136},{9... | collective-permute-start | bytes 460808 | tf_op jit(solution)/shard_map/ppermute | solution.py:396
  54.6 8.3 %collective-permute-start.12 = (bf16[5,200,128]{2,1,0:T(8,128)(2,1)S(1)}, bf16[5,200,128]{2,1,0:T(8,128)(2,1)S(1)}, u32[]{:S(2)}, u32[]{:S(2)}) collective-permute-start(bf16[5,200,128]{2,1,0:T(8,128)(2,1)S(1)} %get-tuple-element.61), channel_id=1, source_target_pairs={{0,64},{1,65},{2,66},{3,67},{4,5},{5,6},{6,7},{7,4},{8,72},{9,73},... | collective-permute-start | bytes 768008 | tf_op jit(solution)/shard_map/ppermute | solution.py:396
  63.0 14.0 %collective-permute-start.14 = (bf16[20,200,128]{2,1,0:T(8,128)(2,1)S(1)}, bf16[20,200,128]{2,1,0:T(8,128)(2,1)S(1)}, u32[]{:S(2)}, u32[]{:S(2)}) collective-permute-start(bf16[20,200,128]{2,1,0:T(8,128)(2,1)S(1)} %get-tuple-element.39), channel_id=1, source_target_pairs={{0,3},{1,0},{2,1},{3,2},{4,196},{5,197},{6,198},{7,199},{8,11},{9,... | collective-permute-start | bytes 3072008 | tf_op jit(solution)/shard_map/ppermute | solution.py:400
  65.5 5.3 %collective-permute-start.13 = (bf16[3,200,128]{2,1,0:T(8,128)(2,1)S(1)}, bf16[3,200,128]{2,1,0:T(8,128)(2,1)S(1)}, u32[]{:S(2)}, u32[]{:S(2)}) collective-permute-start(bf16[3,200,128]{2,1,0:T(8,128)(2,1)S(1)} %pad_maximum_fusion.3), channel_id=1, source_target_pairs={{0,64},{1,65},{2,66},{3,67},{4,5},{5,6},{6,7},{7,4},{8,72},{9,73},... | collective-permute-start | bytes 460808 | tf_op jit(solution)/shard_map/ppermute | solution.py:396
  70.9 12.6 %collective-permute-start.15 = (bf16[12,200,128]{2,1,0:T(8,128)(2,1)S(1)}, bf16[12,200,128]{2,1,0:T(8,128)(2,1)S(1)}, u32[]{:S(2)}, u32[]{:S(2)}) collective-permute-start(bf16[12,200,128]{2,1,0:T(8,128)(2,1)S(1)} %get-tuple-element.80), channel_id=1, source_target_pairs={{0,3},{1,0},{2,1},{3,2},{4,196},{5,197},{6,198},{7,199},{8,11},{9,... | collective-permute-start | bytes 1843208 | tf_op jit(solution)/shard_map/ppermute | solution.py:400
  71.4 21.5 %collective-permute-start.17 = (bf16[12,200,128]{2,1,0:T(8,128)(2,1)S(1)}, bf16[12,200,128]{2,1,0:T(8,128)(2,1)S(1)}, u32[]{:S(2)}, u32[]{:S(2)}) collective-permute-start(bf16[12,200,128]{2,1,0:T(8,128)(2,1)S(1)} %get-tuple-element.80), channel_id=1, source_target_pairs={{0,1},{1,2},{2,3},{3,0},{4,68},{5,69},{6,70},{7,71},{8,9},{9,10},{... | collective-permute-start | bytes 1843208 | tf_op jit(solution)/shard_map/ppermute | solution.py:399
  72.4 20.5 %collective-permute-start.16 = (bf16[20,200,128]{2,1,0:T(8,128)(2,1)S(1)}, bf16[20,200,128]{2,1,0:T(8,128)(2,1)S(1)}, u32[]{:S(2)}, u32[]{:S(2)}) collective-permute-start(bf16[20,200,128]{2,1,0:T(8,128)(2,1)S(1)} %get-tuple-element.39), channel_id=1, source_target_pairs={{0,1},{1,2},{2,3},{3,0},{4,68},{5,69},{6,70},{7,71},{8,9},{9,10},{... | collective-permute-start | bytes 3072008 | tf_op jit(solution)/shard_map/ppermute | solution.py:399
  110.2 11.7 %collective-permute-start.18 = (f32[32,128]{1,0:T(8,128)S(1)}, f32[32,128]{1,0:T(8,128)S(1)}, u32[]{:S(2)}, u32[]{:S(2)}) collective-permute-start(f32[32,128]{1,0:T(8,128)S(1)} %bitcast.13), channel_id=1, source_target_pairs={{0,4},{1,5},{2,6},{3,7},{4,0},{5,1},{6,2},{7,3},{8,12},{9,13},{10,... | collective-permute-start | bytes 49160 | tf_op jit(solution)/shard_map/ppermute | solution.py:418
  121.1 3.8 %collective-permute-start.19 = (f32[32,128]{1,0:T(8,128)S(1)}, f32[32,128]{1,0:T(8,128)S(1)}, u32[]{:S(2)}, u32[]{:S(2)}) collective-permute-start(f32[32,128]{1,0:T(8,128)S(1)} %bitcast.14), channel_id=1, source_target_pairs={{0,1},{1,2},{2,3},{3,0},{4,68},{5,69},{6,70},{7,71},{8,9},{9,10},{... | collective-permute-start | bytes 49160 | tf_op jit(solution)/shard_map/ppermute | solution.py:418
  121.5 4.4 %collective-permute-start.20 = (f32[32,128]{1,0:T(8,128)S(1)}, f32[32,128]{1,0:T(8,128)S(1)}, u32[]{:S(2)}, u32[]{:S(2)}) collective-permute-start(f32[32,128]{1,0:T(8,128)S(1)} %bitcast.15), channel_id=1, source_target_pairs={{0,5},{1,6},{2,7},{3,4},{4,64},{5,65},{6,66},{7,67},{8,13},{9,14},... | collective-permute-start | bytes 49160 | tf_op jit(solution)/shard_map/ppermute | solution.py:418

commit v8 on v5

--- a/solution.py
+++ b/solution.py
@@ -70,9 +70,9 @@
             ].reshape(each, GROUP, LANES)
 
 
-def send_kernel(where_ref, emb_ref, clu_ref, send_ref, notes_ref, unit_ref, rows_ref):
-    rows = emb_ref.shape[0]
-    half = send_ref.shape[0]
+def rank_kernel(where_ref, clu_ref, rows_ref, labels_ref):
+    half = labels_ref.shape[0] // 2
+    rows = clu_ref.shape[1]
     clusters = clu_ref[...]
     slot, away = slot_of(clusters, where_ref[1], half)
     hot = (iota((2 * half, rows), 0) == slot).astype(jnp.bfloat16)
@@ -84,12 +84,18 @@
     rows_ref[...] = jnp.concatenate([slot, spot, place, place] * 2, axis=0)
     bit = (clusters % 2).astype(jnp.float32)
     spots = jnp.where(iota((LANES, rows), 0) == spot, bit, 0.0).astype(jnp.bfloat16)
-    labels = dot(hot, spots, ((1,), (1,))).astype(jnp.bfloat16)
+    labels_ref[...] = dot(hot, spots, ((1,), (1,))).astype(jnp.bfloat16)
+
+
+def send_kernel(where_ref, emb_ref, rows_ref, labels_ref, send_ref, notes_ref, unit_ref):
+    rows = emb_ref.shape[0]
+    half = send_ref.shape[0]
+    labels = labels_ref[...]
     notes_ref[...] = jnp.broadcast_to(labels[:half, None, :], (half, NOTE, LANES))
     values = emb_ref[...].astype(jnp.float32)
     scale = lax.rsqrt(jnp.sum(values * values, axis=1, keepdims=True) + 1e-06)
     unit_ref[...] = (values * scale).astype(jnp.bfloat16)
-    put_rows(send_ref, unit_ref, place, rows // 2)
+    put_rows(send_ref, unit_ref, rows_ref[2:3, :], rows // 2)
     data = send_ref.shape[1] - NOTE
     send_ref[:, data:, :] = jnp.broadcast_to(labels[half:, None, :], (half, NOTE, LANES))
 
@@ -144,7 +150,13 @@
     return label * BITS, label * BITS + order_of(place, core, part).astype(jnp.float32)
 
 
-def column_codes(lab, rows, core, part):
+def column_orders(rows, core, part):
+    place = iota((rows, LANES), 0)
+    return order_of(place, core, part).astype(jnp.float32)
+
+
+def column_codes(lab, orders):
+    rows = orders.shape[0]
     sources = lab.shape[0]
     place = iota((rows, 1), 0)
     hot = (iota((rows, sources), 1) == source_of(place)).astype(jnp.bfloat16)
@@ -152,7 +164,7 @@
     chosen = iota((rows, LANES), 1) == lane_of(place)
     kept = jnp.where(chosen, spread, 0.0).astype(jnp.bfloat16)
     label = dot(kept, jnp.ones((LANES, LANES), jnp.bfloat16), ((1,), (0,)))
-    return label * BITS + order_of(place, core, part).astype(jnp.float32)
+    return label * BITS + orders
 
 
 def scan(best_ref, query_ref, key_ref, floor, ceiling, codes_ref, pick):
@@ -190,11 +202,9 @@
     rows = best.shape[1]
     mine = iota((sources, rows), 0) == source_of(iota((1, rows), 1))
     spots = (iota((rows, LANES), 1) == lane_of(iota((rows, 1), 0))).astype(jnp.bfloat16)
-    total = jnp.zeros((sources, LANES), jnp.float32)
-    for piece in split3(best):
-        spread = jnp.where(mine, piece.astype(jnp.float32), 0.0).astype(jnp.bfloat16)
-        total = total + dot(spread, spots, ((1,), (0,)))
-    out_ref[...] = total
+    pieces = [jnp.where(mine, piece.astype(jnp.float32), 0.0) for piece in split3(best)]
+    total = dot(jnp.concatenate(pieces, axis=0).astype(jnp.bfloat16), spots, ((1,), (0,)))
+    out_ref[...] = total[:sources] + total[sources : 2 * sources] + total[2 * sources :]
 
 
 def parts_of(where_ref):
@@ -209,28 +219,31 @@
     lab = notes_of(own_ref)
     floor, ceiling = row_codes(lab, rows, core, me)
     rows_ref[...] = jnp.concatenate([floor, ceiling] * 4, axis=0)
-    codes_ref[...] = column_codes(lab, rows, core, me)
+    codes_ref[...] = column_codes(lab, column_orders(rows, core, me))
     best_ref[...] = jnp.full((1, rows), -1.0, jnp.float32)
     scan(best_ref, own_ref, own_ref, floor, ceiling, codes_ref, lambda key, query: key <= query)
 
 
-def right_kernel(where_ref, alone_ref, own_ref, right_ref, rows_ref, best_ref, right_rows_ref, codes_ref):
+def right_kernel(
+    where_ref, alone_ref, own_ref, right_ref, rows_ref, best_ref, right_rows_ref, orders_ref, codes_ref
+):
     rows = best_ref.shape[1]
-    core, me, _, right = parts_of(where_ref)
+    core, me, left, right = parts_of(where_ref)
     best_ref[...] = alone_ref[...]
     lab = notes_of(right_ref)
     floor, ceiling = row_codes(lab, rows, core, right)
     right_rows_ref[...] = jnp.concatenate([floor, ceiling] * 4, axis=0)
-    codes_ref[...] = column_codes(lab, rows, core, right)
+    orders_ref[...] = column_orders(rows, core, left)
+    codes_ref[...] = column_codes(lab, column_orders(rows, core, right))
     scan_pair(
         best_ref, own_ref, right_ref, rows_ref[0:1, :], rows_ref[1:2, :], codes_ref, core, me, right
     )
 
 
-def cross_kernel(where_ref, left_ref, right_ref, rows_ref, out_ref, codes_ref, best_ref):
+def cross_kernel(where_ref, left_ref, right_ref, rows_ref, orders_ref, out_ref, codes_ref, best_ref):
     rows = best_ref.shape[1]
     core, _, left, right = parts_of(where_ref)
-    codes_ref[...] = column_codes(notes_of(left_ref), rows, core, left)
+    codes_ref[...] = column_codes(notes_of(left_ref), orders_ref[...])
     best_ref[...] = jnp.full((1, rows), -1.0, jnp.float32)
     scan_pair(
         best_ref, right_ref, left_ref, rows_ref[0:1, :], rows_ref[1:2, :], codes_ref, core, right, left
@@ -296,16 +309,23 @@
     core, y = dp % 2, dp // (2 * NZ)
     where = jnp.stack([jnp.where(core == 0, x, y), core, jnp.int32(NX)])
     half_float, full_float, whole = jnp.bfloat16, jnp.float32, jnp.int32
-    send, notes, unit, back = call(
+    back, labels = call(
+        rank_kernel,
+        "rank",
+        (where, clusters.reshape(1, rows)),
+        (((8, rows), whole), ((2 * half, LANES), half_float)),
+        flops=10**9,
+    )
+    send, notes, unit = call(
         send_kernel,
         "send",
-        (where, embeddings, clusters.reshape(1, rows)),
+        (where, embeddings, back, labels),
         (
             ((half, data + NOTE, LANES), half_float),
             ((half, NOTE, LANES), half_float),
             ((rows, depth), half_float),
-            ((8, rows), whole),
         ),
+        flops=10**9,
     )
     got = lax.ppermute(send, AXES, SWAP)
     (keep,) = call(
@@ -319,11 +339,11 @@
     best, own_rows, back = call(
         alone_kernel, "alone", (where, own, back), (row, lines, ((8, rows), whole)), (codes,), 10**9
     )
-    best, right_rows = call(
-        right_kernel, "right", (where, best, own, right, own_rows), (row, lines), (codes,), 10**9
+    best, right_rows, orders = call(
+        right_kernel, "right", (where, best, own, right, own_rows), (row, lines, codes), (codes,), 10**9
     )
     cross, left_codes = call(
-        cross_kernel, "cross", (where, left, right, right_rows), (groups, codes), (row,), 10**9
+        cross_kernel, "cross", (where, left, right, right_rows, orders), (groups, codes), (row,), 10**9
     )
     cross = lax.ppermute(cross, AXES, aside(1))
     (best,) = call(

time: 112 us -> 111 us (level)
  local copies, waits for them, and re-layouts: 2.15 us -> 0.99 us
    unnamed x4, local copies, waits for them, and re-layouts: 2.1 us -> 0.94 us
    pallas_call x7 -> x8, Pallas kernels: 12.6 us -> 12.8 us  [call(): pl.pallas_call(kernel, out_shape=tuple((jax.ShapeDtypeStruct(shape, kind)...]
where the time goes in v8:
time: 111 us
  blocking collectives  62.4 us (56%)
  waiting for transfers between devices  21.8 us (20%)
  Pallas kernels  12.8 us (12%)
  starting transfers between devices  12.6 us (11%)
    all_to_all x2, blocking collectives, exchange(): lax.all_to_all(array, AXES, split_axis=0, concat_axis=0, axis_index_group...  62.4 us
    ppermute x1, waiting for transfers between devices, shards(): lax.ppermute(own, AXES, aside(-1))  15.3 us
    pallas_call x8, Pallas kernels, call(): pl.pallas_call(kernel, out_shape=tuple((jax.ShapeDtypeStruct(shape, kind)...  12.8 us
    ppermute x1, starting transfers between devices, shards(): far = lax.ppermute(near, AXES, SWAP)  5.21 us
    ppermute x1, waiting for transfers between devices, shards(): cross = lax.ppermute(cross, AXES, aside(1))  3.62 us
    ppermute x1, starting transfers between devices, shards(): got = lax.ppermute(send, AXES, SWAP)  3.33 us
    ppermute x1, starting transfers between devices, shards(): lax.ppermute(own, AXES, aside(-1))  3.07 us
  transfers between devices with their start and end apart: 5, of which 5 were waited for; matrix products, arithmetic and copies ran while one was open for 0% of the time, Pallas kernels for 6%

profile of v8, /device:TPU:1, one launch (start us, length us, event | category | flops | bytes accessed | tf_op | source)
XLA Modules:
  0.0 111.0 jit_solution(13154538258567180864)
XLA Ops:
  0.0 0.1 pad_add_fusion.where_ref
  0.1 0.0 copy-start.1
  0.1 0.7 copy-done.1
  0.8 0.0 copy-start
  0.8 1.1 %rank.1 = (s32[8,1024]{1,0:T(8,128)S(1)}, bf16[64,128]{1,0:T(8,128)(2,1)S(1)}) custom-call(s32[3]{0:T(128)S(1)} %pad_add_fusion.where_ref, s32[1,1024]{1,0:T(1,128)S(1)} %bitcast.10), custom_call_target="tpu_custom_call" | custom-call | flops 1000000000 | bytes 1048576 | tf_op jit(solution)/shard_map/rank/pallas_call | solution.py:48
  1.9 0.3 copy-done
  2.2 1.9 %send.1 = (bf16[32,104,128]{2,1,0:T(8,128)(2,1)S(1)}, bf16[32,8,128]{2,1,0:T(8,128)(2,1)S(1)}, bf16[1024,768]{1,0:T(8,128)(2,1)S(1)}) custom-call(s32[3]{0:T(128)S(1)} %pad_add_fusion.where_ref, bf16[1024,768]{1,0:T(8,128)(2,1)S(1)} %copy-done, s32[8,1024]{1,0:T(8,128)S(1)} %get-tuple-element.18.rows_ref.back_ref, ...), custom_call_target="tpu_custom_call" | custom-call | flops 1000000000 | bytes 1048576 | tf_op jit(solution)/shard_map/send/pallas_call | solution.py:48
  4.1 3.3 %collective-permute-start = (bf16[32,104,128]{2,1,0:T(8,128)(2,1)S(1)}, bf16[32,104,128]{2,1,0:T(8,128)(2,1)S(1)}, u32[]{:S(2)}, u32[]{:S(2)}) collective-permute-start(bf16[32,104,128]{2,1,0:T(8,128)(2,1)S(1)} %get-tuple-element.21), channel_id=1, source_target_pairs={{0,4},{1,5},{2,6},{3,7},{4,0},{5,1},{6,2},{7,3},{8,12},{9,13},{10,... | collective-permute-start | bytes 2555912 | tf_op jit(solution)/shard_map/ppermute | solution.py:330
  7.4 1.5 %keep.1 = bf16[32,96,128]{2,1,0:T(8,128)(2,1)S(1)} custom-call(s32[3]{0:T(128)S(1)} %pad_add_fusion.where_ref, bf16[1024,768]{1,0:T(8,128)(2,1)S(1)} %get-tuple-element.20.unit_ref, s32[8,1024]{1,0:T(8,128)S(1)} %get-tuple-element.18.rows_ref.back_ref), custom_call_target="tpu_custom_call" | custom-call | flops 1000000000 | bytes 1048576 | tf_op jit(solution)/shard_map/keep/pallas_call | solution.py:48
  8.9 0.5 collective-permute-done
  9.4 0.1 slice.8
  9.5 0.1 pad_maximum_fusion
  9.6 49.0 %all_to_all.10.own_ref = bf16[32,200,128]{2,1,0:T(8,128)(2,1)S(1)} all-to-all(bf16[32,200,128]{2,1,0:T(8,128)(2,1)S(1)} %pad_maximum_fusion), channel_id=1, replica_groups={{0,8,16,24,32,40,48,56,64,72,80,88,96,104,112,120,128,136,144,152,160,1..., dimensions={0} | all-to-all | bytes 3276800 | tf_op jit(solution)/shard_map/all_to_all | solution.py:299
  58.6 3.1 %collective-permute-start.1 = (bf16[32,200,128]{2,1,0:T(8,128)(2,1)S(1)}, bf16[32,200,128]{2,1,0:T(8,128)(2,1)S(1)}, u32[]{:S(2)}, u32[]{:S(2)}) collective-permute-start(bf16[32,200,128]{2,1,0:T(8,128)(2,1)S(1)} %all_to_all.10.own_ref), channel_id=1, source_target_pairs={{0,3},{1,0},{2,1},{3,2},{4,196},{5,197},{6,198},{7,199},{8,11},{9,... | collective-permute-start | bytes 4915208 | tf_op jit(solution)/shard_map/ppermute | solution.py:336
  61.7 0.0 collective-permute-start.2
  61.7 2.8 %alone.1 = (f32[1,1024]{1,0:T(1,128)S(1)}, f32[8,1024]{1,0:T(8,128)S(1)}, s32[8,1024]{1,0:T(8,128)S(1)}) custom-call(s32[3]{0:T(128)S(1)} %pad_add_fusion.where_ref, bf16[32,200,128]{2,1,0:T(8,128)(2,1)S(1)} %all_to_all.10.own_ref, s32[8,1024]{1,0:T(8,128)S(1)} %get-tuple-element.18.rows_ref.back_ref), custom_call_target="tpu_custom_call" | custom-call | flops 1000000000 | bytes 1048576 | tf_op jit(solution)/shard_map/alone/pallas_call | solution.py:48
  64.5 15.3 %collective-permute-done.1.right_ref = bf16[32,200,128]{2,1,0:T(8,128)(2,1)S(1)} collective-permute-done((bf16[32,200,128]{2,1,0:T(8,128)(2,1)S(1)}, bf16[32,200,128]{2,1,0:T(8,128)(2,1)S(1)}, u32[]{:S(2)}, u32[]{:S(2)}) %collective-permute-start.1) | collective-permute-done | bytes 1638432 | tf_op jit(solution)/shard_map/ppermute | solution.py:336
  79.8 1.8 %right.1 = (f32[1,1024]{1,0:T(1,128)S(1)}, f32[8,1024]{1,0:T(8,128)S(1)}, f32[1024,128]{1,0:T(8,128)S(1)}) custom-call(s32[3]{0:T(128)S(1)} %pad_add_fusion.where_ref, f32[1,1024]{1,0:T(1,128)S(1)} %get-tuple-element.24.alone_ref, bf16[32,200,128]{2,1,0:T(8,128)(2,1)S(1)} %all_to_all.10.own_ref, bf16[32,200,128]{2,1,0:T(8,128)(2,1)S(1)} %collective-permute-done.1.right_ref, ...), custom_call_target="tpu_custom_call" | custom-call | flops 1000000000 | bytes 1048576 | tf_op jit(solution)/shard_map/right/pallas_call | solution.py:48
  81.6 1.6 %collective-permute-done.2.left_ref = bf16[32,200,128]{2,1,0:T(8,128)(2,1)S(1)} collective-permute-done((bf16[32,200,128]{2,1,0:T(8,128)(2,1)S(1)}, bf16[32,200,128]{2,1,0:T(8,128)(2,1)S(1)}, u32[]{:S(2)}, u32[]{:S(2)}) %collective-permute-start.2) | collective-permute-done | bytes 1638432 | tf_op jit(solution)/shard_map/ppermute | solution.py:336
  83.2 1.4 %cross.1 = (f32[32,128]{1,0:T(8,128)S(1)}, f32[1024,128]{1,0:T(8,128)S(1)}) custom-call(s32[3]{0:T(128)S(1)} %pad_add_fusion.where_ref, bf16[32,200,128]{2,1,0:T(8,128)(2,1)S(1)} %collective-permute-done.2.left_ref, bf16[32,200,128]{2,1,0:T(8,128)(2,1)S(1)} %collective-permute-done.1.right_ref, f32[8,1024]{1,0:T(8,128)S(1)} %get-tuple-element.27.rows_ref, ...), custom_call_target="tpu_custom_call" | custom-call | flops 1000000000 | bytes 1048576 | tf_op jit(solution)/shard_map/cross/pallas_call | solution.py:48
  84.6 1.0 collective-permute-start.3
  85.6 0.9 left.1
  86.5 3.6 %collective-permute-done.3 = f32[32,128]{1,0:T(8,128)S(1)} collective-permute-done((f32[32,128]{1,0:T(8,128)S(1)}, f32[32,128]{1,0:T(8,128)S(1)}, u32[]{:S(2)}, u32[]{:S(2)}) %collective-permute-start.3) | collective-permute-done | bytes 16416 | tf_op jit(solution)/shard_map/ppermute | solution.py:348
  90.1 13.4 %all_to_all.11 = f32[32,1,128]{2,1,0:T(1,128)S(1)} all-to-all(f32[32,1,128]{2,1,0:T(1,128)S(1)} %bitcast.11), channel_id=1, replica_groups={{0,8,16,24,32,40,48,56,64,72,80,88,96,104,112,120,128,136,144,152,160,1..., dimensions={0} | all-to-all | bytes 32768 | tf_op jit(solution)/shard_map/all_to_all | solution.py:299
  103.5 5.2 %collective-permute-start.4 = (f32[32,128]{1,0:T(8,128)S(1)}, f32[32,128]{1,0:T(8,128)S(1)}, u32[]{:S(2)}, u32[]{:S(2)}) collective-permute-start(f32[32,128]{1,0:T(8,128)S(1)} %bitcast.8), channel_id=1, source_target_pairs={{0,4},{1,5},{2,6},{3,7},{4,0},{5,1},{6,2},{7,3},{8,12},{9,13},{10,... | collective-permute-start | bytes 49160 | tf_op jit(solution)/shard_map/ppermute | solution.py:354
  108.8 0.8 collective-permute-done.4.far_ref
  109.6 1.4 %unpack.1 = f32[1,1024]{1,0:T(1,128)} custom-call(s32[3]{0:T(128)S(1)} %pad_add_fusion.where_ref, s32[8,1024]{1,0:T(8,128)S(1)} %get-tuple-element.23.back_ref, f32[32,128]{1,0:T(8,128)S(1)} %bitcast.9, f32[32,128]{1,0:T(8,128)S(1)} %collective-permute-done.4.far_ref), custom_call_target="tpu_custom_call" | custom-call | bytes 1048576 | tf_op jit(solution)/shard_map/unpack/pallas_call | solution.py:48
  (2 shorter events, 0.0 us)
Async XLA Ops:
  0.1 0.7 copy-start.1
  0.8 1.4 %copy-start = (bf16[1024,768]{1,0:T(8,128)(2,1)S(1)}, bf16[1024,768]{1,0:T(8,128)(2,1)}, u32[]{:S(2)}) copy-start(bf16[1024,768]{1,0:T(8,128)(2,1)} %emb_ref.1) | copy-start | bytes 4718596
  4.1 5.3 %collective-permute-start = (bf16[32,104,128]{2,1,0:T(8,128)(2,1)S(1)}, bf16[32,104,128]{2,1,0:T(8,128)(2,1)S(1)}, u32[]{:S(2)}, u32[]{:S(2)}) collective-permute-start(bf16[32,104,128]{2,1,0:T(8,128)(2,1)S(1)} %get-tuple-element.21), channel_id=1, source_target_pairs={{0,4},{1,5},{2,6},{3,7},{4,0},{5,1},{6,2},{7,3},{8,12},{9,13},{10,... | collective-permute-start | bytes 2555912 | tf_op jit(solution)/shard_map/ppermute | solution.py:330
  58.6 21.1 %collective-permute-start.1 = (bf16[32,200,128]{2,1,0:T(8,128)(2,1)S(1)}, bf16[32,200,128]{2,1,0:T(8,128)(2,1)S(1)}, u32[]{:S(2)}, u32[]{:S(2)}) collective-permute-start(bf16[32,200,128]{2,1,0:T(8,128)(2,1)S(1)} %all_to_all.10.own_ref), channel_id=1, source_target_pairs={{0,3},{1,0},{2,1},{3,2},{4,196},{5,197},{6,198},{7,199},{8,11},{9,... | collective-permute-start | bytes 4915208 | tf_op jit(solution)/shard_map/ppermute | solution.py:336
  61.7 21.5 %collective-permute-start.2 = (bf16[32,200,128]{2,1,0:T(8,128)(2,1)S(1)}, bf16[32,200,128]{2,1,0:T(8,128)(2,1)S(1)}, u32[]{:S(2)}, u32[]{:S(2)}) collective-permute-start(bf16[32,200,128]{2,1,0:T(8,128)(2,1)S(1)} %all_to_all.10.own_ref), channel_id=1, source_target_pairs={{0,1},{1,2},{2,3},{3,0},{4,68},{5,69},{6,70},{7,71},{8,9},{9,10},{... | collective-permute-start | bytes 4915208 | tf_op jit(solution)/shard_map/ppermute | solution.py:336
  84.6 5.5 %collective-permute-start.3 = (f32[32,128]{1,0:T(8,128)S(1)}, f32[32,128]{1,0:T(8,128)S(1)}, u32[]{:S(2)}, u32[]{:S(2)}) collective-permute-start(f32[32,128]{1,0:T(8,128)S(1)} %get-tuple-element.30), channel_id=1, source_target_pairs={{0,1},{1,2},{2,3},{3,0},{4,68},{5,69},{6,70},{7,71},{8,9},{9,10},{... | collective-permute-start | bytes 49160 | tf_op jit(solution)/shard_map/ppermute | solution.py:348
  103.5 6.1 %collective-permute-start.4 = (f32[32,128]{1,0:T(8,128)S(1)}, f32[32,128]{1,0:T(8,128)S(1)}, u32[]{:S(2)}, u32[]{:S(2)}) collective-permute-start(f32[32,128]{1,0:T(8,128)S(1)} %bitcast.8), channel_id=1, source_target_pairs={{0,4},{1,5},{2,6},{3,7},{4,0},{5,1},{6,2},{7,3},{8,12},{9,13},{10,... | collective-permute-start | bytes 49160 | tf_op jit(solution)/shard_map/ppermute | solution.py:354

commit v9 on v8

--- a/solution.py
+++ b/solution.py
@@ -155,14 +155,20 @@
     return order_of(place, core, part).astype(jnp.float32)
 
 
-def column_codes(lab, orders):
-    rows = orders.shape[0]
-    sources = lab.shape[0]
-    place = iota((rows, 1), 0)
-    hot = (iota((rows, sources), 1) == source_of(place)).astype(jnp.bfloat16)
-    spread = dot(hot, lab, ((1,), (0,)))
-    chosen = iota((rows, LANES), 1) == lane_of(place)
-    kept = jnp.where(chosen, spread, 0.0).astype(jnp.bfloat16)
+def spots_of(rows):
+    return (iota((rows, LANES), 1) == lane_of(iota((rows, 1), 0))).astype(jnp.bfloat16)
+
+
+def cells_of(rows, sources):
+    return (iota((rows, sources), 1) == source_of(iota((rows, 1), 0))).astype(jnp.bfloat16)
+
+
+def mine_of(sources, rows):
+    return (iota((sources, rows), 0) == source_of(iota((1, rows), 1))).astype(jnp.bfloat16)
+
+
+def column_codes(lab, orders, cells, spots):
+    kept = dot(cells, lab, ((1,), (0,))).astype(jnp.bfloat16) * spots
     label = dot(kept, jnp.ones((LANES, LANES), jnp.bfloat16), ((1,), (0,)))
     return label * BITS + orders
 
@@ -197,13 +203,10 @@
         scan(*args, lambda key, query: key > query)
 
 
-def store_groups(out_ref, best):
+def store_groups(out_ref, best, mine, spots):
     sources = out_ref.shape[0]
-    rows = best.shape[1]
-    mine = iota((sources, rows), 0) == source_of(iota((1, rows), 1))
-    spots = (iota((rows, LANES), 1) == lane_of(iota((rows, 1), 0))).astype(jnp.bfloat16)
-    pieces = [jnp.where(mine, piece.astype(jnp.float32), 0.0) for piece in split3(best)]
-    total = dot(jnp.concatenate(pieces, axis=0).astype(jnp.bfloat16), spots, ((1,), (0,)))
+    spread = jnp.concatenate([mine * piece for piece in split3(best)], axis=0)
+    total = dot(spread, spots, ((1,), (0,)))
     out_ref[...] = total[:sources] + total[sources : 2 * sources] + total[2 * sources :]
 
 
@@ -212,52 +215,66 @@
     return core, me, lax.rem(me + parts - 1, parts), lax.rem(me + 1, parts)
 
 
-def alone_kernel(where_ref, own_ref, back_ref, best_ref, rows_ref, kept_ref, codes_ref):
+def alone_kernel(
+    where_ref, own_ref, back_ref, best_ref, rows_ref, kept_ref, spots_ref, cells_ref, mine_ref,
+    left_orders_ref, right_orders_ref, codes_ref,
+):
     rows = best_ref.shape[1]
-    core, me, _, _ = parts_of(where_ref)
+    sources = own_ref.shape[0]
+    spots_ref[...] = spots_of(rows)
+    cells_ref[...] = cells_of(rows, sources)
+    mine_ref[...] = mine_of(sources, rows)
+    core, me, left, right = parts_of(where_ref)
+    left_orders_ref[...] = column_orders(rows, core, left)
+    right_orders_ref[...] = column_orders(rows, core, right)
     kept_ref[...] = back_ref[...]
     lab = notes_of(own_ref)
     floor, ceiling = row_codes(lab, rows, core, me)
     rows_ref[...] = jnp.concatenate([floor, ceiling] * 4, axis=0)
-    codes_ref[...] = column_codes(lab, column_orders(rows, core, me))
+    codes_ref[...] = column_codes(lab, column_orders(rows, core, me), cells_ref[...], spots_ref[...])
     best_ref[...] = jnp.full((1, rows), -1.0, jnp.float32)
     scan(best_ref, own_ref, own_ref, floor, ceiling, codes_ref, lambda key, query: key <= query)
 
 
 def right_kernel(
-    where_ref, alone_ref, own_ref, right_ref, rows_ref, best_ref, right_rows_ref, orders_ref, codes_ref
+    where_ref, alone_ref, own_ref, right_ref, rows_ref, orders_ref, spots_ref, cells_ref,
+    best_ref, right_rows_ref, codes_ref,
 ):
     rows = best_ref.shape[1]
-    core, me, left, right = parts_of(where_ref)
+    core, me, _, right = parts_of(where_ref)
     best_ref[...] = alone_ref[...]
     lab = notes_of(right_ref)
     floor, ceiling = row_codes(lab, rows, core, right)
     right_rows_ref[...] = jnp.concatenate([floor, ceiling] * 4, axis=0)
-    orders_ref[...] = column_orders(rows, core, left)
-    codes_ref[...] = column_codes(lab, column_orders(rows, core, right))
+    codes_ref[...] = column_codes(lab, orders_ref[...], cells_ref[...], spots_ref[...])
     scan_pair(
         best_ref, own_ref, right_ref, rows_ref[0:1, :], rows_ref[1:2, :], codes_ref, core, me, right
     )
 
 
-def cross_kernel(where_ref, left_ref, right_ref, rows_ref, orders_ref, out_ref, codes_ref, best_ref):
+def cross_kernel(
+    where_ref, left_ref, right_ref, rows_ref, orders_ref, spots_ref, cells_ref, mine_ref,
+    out_ref, codes_ref, best_ref,
+):
     rows = best_ref.shape[1]
     core, _, left, right = parts_of(where_ref)
-    codes_ref[...] = column_codes(notes_of(left_ref), orders_ref[...])
+    codes_ref[...] = column_codes(notes_of(left_ref), orders_ref[...], cells_ref[...], spots_ref[...])
     best_ref[...] = jnp.full((1, rows), -1.0, jnp.float32)
     scan_pair(
         best_ref, right_ref, left_ref, rows_ref[0:1, :], rows_ref[1:2, :], codes_ref, core, right, left
     )
-    store_groups(out_ref, best_ref[...])
-
-
-def left_kernel(where_ref, found_ref, own_ref, left_ref, rows_ref, codes_ref, out_ref, best_ref):
+    store_groups(out_ref, best_ref[...], mine_ref[...], spots_ref[...])
+
+
+def left_kernel(
+    where_ref, found_ref, own_ref, left_ref, rows_ref, codes_ref, spots_ref, mine_ref, out_ref, best_ref
+):
     core, me, left, _ = parts_of(where_ref)
     best_ref[...] = found_ref[...]
     scan_pair(
         best_ref, own_ref, left_ref, rows_ref[0:1, :], rows_ref[1:2, :], codes_ref, core, me, left
     )
-    store_groups(out_ref, best_ref[...])
+    store_groups(out_ref, best_ref[...], mine_ref[...], spots_ref[...])
 
 
 def unpack_kernel(where_ref, back_ref, near_ref, far_ref, out_ref):
@@ -336,18 +353,39 @@
     left, right = lax.ppermute(own, AXES, aside(1)), lax.ppermute(own, AXES, aside(-1))
     row, lines = ((1, rows), full_float), ((8, rows), full_float)
     codes, groups = ((rows, LANES), full_float), ((half, LANES), full_float)
-    best, own_rows, back = call(
-        alone_kernel, "alone", (where, own, back), (row, lines, ((8, rows), whole)), (codes,), 10**9
-    )
-    best, right_rows, orders = call(
-        right_kernel, "right", (where, best, own, right, own_rows), (row, lines, codes), (codes,), 10**9
+    spot_kind, cell_kind = ((rows, LANES), half_float), ((rows, half), half_float)
+    best, own_rows, back, spots, cells, mine, left_orders, right_orders = call(
+        alone_kernel,
+        "alone",
+        (where, own, back),
+        (row, lines, ((8, rows), whole), spot_kind, cell_kind, ((half, rows), half_float), codes, codes),
+        (codes,),
+        10**9,
+    )
+    best, right_rows = call(
+        right_kernel,
+        "right",
+        (where, best, own, right, own_rows, right_orders, spots, cells),
+        (row, lines),
+        (codes,),
+        10**9,
     )
     cross, left_codes = call(
-        cross_kernel, "cross", (where, left, right, right_rows, orders), (groups, codes), (row,), 10**9
+        cross_kernel,
+        "cross",
+        (where, left, right, right_rows, left_orders, spots, cells, mine),
+        (groups, codes),
+        (row,),
+        10**9,
     )
     cross = lax.ppermute(cross, AXES, aside(1))
     (best,) = call(
-        left_kernel, "left", (where, best, own, left, own_rows, left_codes), (groups,), (row,), 10**9
+        left_kernel,
+        "left",
+        (where, best, own, left, own_rows, left_codes, spots, mine),
+        (groups,),
+        (row,),
+        10**9,
     )
     best = jnp.maximum(best, cross)
     near = exchange(best.reshape(half, 1, LANES)).reshape(half, LANES)

time: 111 us -> 111 us (level)
  no operation moved by 1% of the time
where the time goes in v9:
time: 111 us
  blocking collectives  62.4 us (56%)
  waiting for transfers between devices  21.7 us (20%)
  starting transfers between devices  13.4 us (12%)
  Pallas kernels  12 us (11%)
    all_to_all x2, blocking collectives, exchange(): lax.all_to_all(array, AXES, split_axis=0, concat_axis=0, axis_index_group...  62.4 us
    ppermute x1, waiting for transfers between devices, shards(): lax.ppermute(own, AXES, aside(-1))  15 us
    pallas_call x8, Pallas kernels, call(): pl.pallas_call(kernel, out_shape=tuple((jax.ShapeDtypeStruct(shape, kind)...  12 us
    ppermute x1, starting transfers between devices, shards(): far = lax.ppermute(near, AXES, SWAP)  5.86 us
    ppermute x1, starting transfers between devices, shards(): got = lax.ppermute(send, AXES, SWAP)  3.33 us
    ppermute x1, starting transfers between devices, shards(): lax.ppermute(own, AXES, aside(-1))  3.07 us
    ppermute x1, waiting for transfers between devices, shards(): cross = lax.ppermute(cross, AXES, aside(1))  2.99 us
    ppermute x1, waiting for transfers between devices, shards(): lax.ppermute(own, AXES, aside(1))  2.35 us
  transfers between devices with their start and end apart: 5, of which 5 were waited for; matrix products, arithmetic and copies ran while one was open for 0% of the time, Pallas kernels for 6%

profile of v9, /device:TPU:1, one launch (start us, length us, event | category | flops | bytes accessed | tf_op | source)
XLA Modules:
  0.0 110.8 jit_solution(4587338840455491714)
XLA Ops:
  0.0 0.1 pad_add_fusion.where_ref
  0.1 0.0 copy-start.1
  0.1 0.7 copy-done.1
  0.8 0.0 copy-start
  0.8 1.1 %rank.1 = (s32[8,1024]{1,0:T(8,128)S(1)}, bf16[64,128]{1,0:T(8,128)(2,1)S(1)}) custom-call(s32[3]{0:T(128)S(1)} %pad_add_fusion.where_ref, s32[1,1024]{1,0:T(1,128)S(1)} %bitcast.10), custom_call_target="tpu_custom_call" | custom-call | flops 1000000000 | bytes 1048576 | tf_op jit(solution)/shard_map/rank/pallas_call | solution.py:48
  1.9 0.3 copy-done
  2.2 1.9 %send.1 = (bf16[32,104,128]{2,1,0:T(8,128)(2,1)S(1)}, bf16[32,8,128]{2,1,0:T(8,128)(2,1)S(1)}, bf16[1024,768]{1,0:T(8,128)(2,1)S(1)}) custom-call(s32[3]{0:T(128)S(1)} %pad_add_fusion.where_ref, bf16[1024,768]{1,0:T(8,128)(2,1)S(1)} %copy-done, s32[8,1024]{1,0:T(8,128)S(1)} %get-tuple-element.22.rows_ref.back_ref, ...), custom_call_target="tpu_custom_call" | custom-call | flops 1000000000 | bytes 1048576 | tf_op jit(solution)/shard_map/send/pallas_call | solution.py:48
  4.1 3.3 %collective-permute-start = (bf16[32,104,128]{2,1,0:T(8,128)(2,1)S(1)}, bf16[32,104,128]{2,1,0:T(8,128)(2,1)S(1)}, u32[]{:S(2)}, u32[]{:S(2)}) collective-permute-start(bf16[32,104,128]{2,1,0:T(8,128)(2,1)S(1)} %get-tuple-element.25), channel_id=1, source_target_pairs={{0,4},{1,5},{2,6},{3,7},{4,0},{5,1},{6,2},{7,3},{8,12},{9,13},{10,... | collective-permute-start | bytes 2555912 | tf_op jit(solution)/shard_map/ppermute | solution.py:347
  7.4 1.5 %keep.1 = bf16[32,96,128]{2,1,0:T(8,128)(2,1)S(1)} custom-call(s32[3]{0:T(128)S(1)} %pad_add_fusion.where_ref, bf16[1024,768]{1,0:T(8,128)(2,1)S(1)} %get-tuple-element.24.unit_ref, s32[8,1024]{1,0:T(8,128)S(1)} %get-tuple-element.22.rows_ref.back_ref), custom_call_target="tpu_custom_call" | custom-call | flops 1000000000 | bytes 1048576 | tf_op jit(solution)/shard_map/keep/pallas_call | solution.py:48
  8.9 0.5 collective-permute-done
  9.4 0.1 slice.8
  9.5 0.1 pad_maximum_fusion
  9.6 49.0 %all_to_all.10.own_ref = bf16[32,200,128]{2,1,0:T(8,128)(2,1)S(1)} all-to-all(bf16[32,200,128]{2,1,0:T(8,128)(2,1)S(1)} %pad_maximum_fusion), channel_id=1, replica_groups={{0,8,16,24,32,40,48,56,64,72,80,88,96,104,112,120,128,136,144,152,160,1..., dimensions={0} | all-to-all | bytes 3276800 | tf_op jit(solution)/shard_map/all_to_all | solution.py:316
  58.6 3.1 %collective-permute-start.1 = (bf16[32,200,128]{2,1,0:T(8,128)(2,1)S(1)}, bf16[32,200,128]{2,1,0:T(8,128)(2,1)S(1)}, u32[]{:S(2)}, u32[]{:S(2)}) collective-permute-start(bf16[32,200,128]{2,1,0:T(8,128)(2,1)S(1)} %all_to_all.10.own_ref), channel_id=1, source_target_pairs={{0,3},{1,0},{2,1},{3,2},{4,196},{5,197},{6,198},{7,199},{8,11},{9,... | collective-permute-start | bytes 4915208 | tf_op jit(solution)/shard_map/ppermute | solution.py:353
  61.7 0.0 collective-permute-start.2
  61.7 3.0 %alone.1 = (f32[1,1024]{1,0:T(1,128)S(1)}, f32[8,1024]{1,0:T(8,128)S(1)}, s32[8,1024]{1,0:T(8,128)S(1)}, bf16[1024,128]{1,0:T(8,128)(2,1)S(1)}, bf16[1024,32]{1,...) custom-call(s32[3]{0:T(128)S(1)} %pad_add_fusion.where_ref, ...), custom_call_target="tpu_custom_call" | custom-call | flops 1000000000 | bytes 1048576 | tf_op jit(solution)/shard_map/alone/pallas_call | solution.py:48
  64.7 15.0 %collective-permute-done.1.right_ref = bf16[32,200,128]{2,1,0:T(8,128)(2,1)S(1)} collective-permute-done((bf16[32,200,128]{2,1,0:T(8,128)(2,1)S(1)}, bf16[32,200,128]{2,1,0:T(8,128)(2,1)S(1)}, u32[]{:S(2)}, u32[]{:S(2)}) %collective-permute-start.1) | collective-permute-done | bytes 1638432 | tf_op jit(solution)/shard_map/ppermute | solution.py:353
  79.8 1.0 right.1
  80.8 2.4 %collective-permute-done.2.left_ref = bf16[32,200,128]{2,1,0:T(8,128)(2,1)S(1)} collective-permute-done((bf16[32,200,128]{2,1,0:T(8,128)(2,1)S(1)}, bf16[32,200,128]{2,1,0:T(8,128)(2,1)S(1)}, u32[]{:S(2)}, u32[]{:S(2)}) %collective-permute-start.2) | collective-permute-done | bytes 1638432 | tf_op jit(solution)/shard_map/ppermute | solution.py:353
  83.2 1.2 %cross.1 = (f32[32,128]{1,0:T(8,128)S(1)}, f32[1024,128]{1,0:T(8,128)S(1)}) custom-call(s32[3]{0:T(128)S(1)} %pad_add_fusion.where_ref, bf16[32,200,128]{2,1,0:T(8,128)(2,1)S(1)} %collective-permute-done.2.left_ref, bf16[32,200,128]{2,1,0:T(8,128)(2,1)S(1)} %collective-permute-done.1.right_ref, f32[8,1024]{1,0:T(8,128)S(1)} %get-tuple-element.34.rows_ref, ...), custom_call_target="tpu_custom_call" | custom-call | flops 1000000000 | bytes 1048576 | tf_op jit(solution)/shard_map/cross/pallas_call | solution.py:48
  84.3 1.2 %collective-permute-start.3 = (f32[32,128]{1,0:T(8,128)S(1)}, f32[32,128]{1,0:T(8,128)S(1)}, u32[]{:S(2)}, u32[]{:S(2)}) collective-permute-start(f32[32,128]{1,0:T(8,128)S(1)} %get-tuple-element.38), channel_id=1, source_target_pairs={{0,1},{1,2},{2,3},{3,0},{4,68},{5,69},{6,70},{7,71},{8,9},{9,10},{... | collective-permute-start | bytes 49160 | tf_op jit(solution)/shard_map/ppermute | solution.py:381
  85.5 0.8 left.1
  86.3 3.0 %collective-permute-done.3 = f32[32,128]{1,0:T(8,128)S(1)} collective-permute-done((f32[32,128]{1,0:T(8,128)S(1)}, f32[32,128]{1,0:T(8,128)S(1)}, u32[]{:S(2)}, u32[]{:S(2)}) %collective-permute-start.3) | collective-permute-done | bytes 16416 | tf_op jit(solution)/shard_map/ppermute | solution.py:381
  89.3 13.4 %all_to_all.11 = f32[32,1,128]{2,1,0:T(1,128)S(1)} all-to-all(f32[32,1,128]{2,1,0:T(1,128)S(1)} %bitcast.11), channel_id=1, replica_groups={{0,8,16,24,32,40,48,56,64,72,80,88,96,104,112,120,128,136,144,152,160,1..., dimensions={0} | all-to-all | bytes 32768 | tf_op jit(solution)/shard_map/all_to_all | solution.py:316
  102.7 5.9 %collective-permute-start.4 = (f32[32,128]{1,0:T(8,128)S(1)}, f32[32,128]{1,0:T(8,128)S(1)}, u32[]{:S(2)}, u32[]{:S(2)}) collective-permute-start(f32[32,128]{1,0:T(8,128)S(1)} %bitcast.8), channel_id=1, source_target_pairs={{0,4},{1,5},{2,6},{3,7},{4,0},{5,1},{6,2},{7,3},{8,12},{9,13},{10,... | collective-permute-start | bytes 49160 | tf_op jit(solution)/shard_map/ppermute | solution.py:392
  108.6 0.8 collective-permute-done.4.far_ref
  109.4 1.4 %unpack.1 = f32[1,1024]{1,0:T(1,128)} custom-call(s32[3]{0:T(128)S(1)} %pad_add_fusion.where_ref, s32[8,1024]{1,0:T(8,128)S(1)} %get-tuple-element.27.back_ref, f32[32,128]{1,0:T(8,128)S(1)} %bitcast.9, f32[32,128]{1,0:T(8,128)S(1)} %collective-permute-done.4.far_ref), custom_call_target="tpu_custom_call" | custom-call | bytes 1048576 | tf_op jit(solution)/shard_map/unpack/pallas_call | solution.py:48
  (2 shorter events, 0.0 us)
Async XLA Ops:
  0.1 0.7 copy-start.1
  0.8 1.4 %copy-start = (bf16[1024,768]{1,0:T(8,128)(2,1)S(1)}, bf16[1024,768]{1,0:T(8,128)(2,1)}, u32[]{:S(2)}) copy-start(bf16[1024,768]{1,0:T(8,128)(2,1)} %emb_ref.1) | copy-start | bytes 4718596
  4.1 5.3 %collective-permute-start = (bf16[32,104,128]{2,1,0:T(8,128)(2,1)S(1)}, bf16[32,104,128]{2,1,0:T(8,128)(2,1)S(1)}, u32[]{:S(2)}, u32[]{:S(2)}) collective-permute-start(bf16[32,104,128]{2,1,0:T(8,128)(2,1)S(1)} %get-tuple-element.25), channel_id=1, source_target_pairs={{0,4},{1,5},{2,6},{3,7},{4,0},{5,1},{6,2},{7,3},{8,12},{9,13},{10,... | collective-permute-start | bytes 2555912 | tf_op jit(solution)/shard_map/ppermute | solution.py:347
  58.6 21.1 %collective-permute-start.1 = (bf16[32,200,128]{2,1,0:T(8,128)(2,1)S(1)}, bf16[32,200,128]{2,1,0:T(8,128)(2,1)S(1)}, u32[]{:S(2)}, u32[]{:S(2)}) collective-permute-start(bf16[32,200,128]{2,1,0:T(8,128)(2,1)S(1)} %all_to_all.10.own_ref), channel_id=1, source_target_pairs={{0,3},{1,0},{2,1},{3,2},{4,196},{5,197},{6,198},{7,199},{8,11},{9,... | collective-permute-start | bytes 4915208 | tf_op jit(solution)/shard_map/ppermute | solution.py:353
  61.7 21.5 %collective-permute-start.2 = (bf16[32,200,128]{2,1,0:T(8,128)(2,1)S(1)}, bf16[32,200,128]{2,1,0:T(8,128)(2,1)S(1)}, u32[]{:S(2)}, u32[]{:S(2)}) collective-permute-start(bf16[32,200,128]{2,1,0:T(8,128)(2,1)S(1)} %all_to_all.10.own_ref), channel_id=1, source_target_pairs={{0,1},{1,2},{2,3},{3,0},{4,68},{5,69},{6,70},{7,71},{8,9},{9,10},{... | collective-permute-start | bytes 4915208 | tf_op jit(solution)/shard_map/ppermute | solution.py:353
  84.3 5.0 %collective-permute-start.3 = (f32[32,128]{1,0:T(8,128)S(1)}, f32[32,128]{1,0:T(8,128)S(1)}, u32[]{:S(2)}, u32[]{:S(2)}) collective-permute-start(f32[32,128]{1,0:T(8,128)S(1)} %get-tuple-element.38), channel_id=1, source_target_pairs={{0,1},{1,2},{2,3},{3,0},{4,68},{5,69},{6,70},{7,71},{8,9},{9,10},{... | collective-permute-start | bytes 49160 | tf_op jit(solution)/shard_map/ppermute | solution.py:381
  102.7 6.7 %collective-permute-start.4 = (f32[32,128]{1,0:T(8,128)S(1)}, f32[32,128]{1,0:T(8,128)S(1)}, u32[]{:S(2)}, u32[]{:S(2)}) collective-permute-start(f32[32,128]{1,0:T(8,128)S(1)} %bitcast.8), channel_id=1, source_target_pairs={{0,4},{1,5},{2,6},{3,7},{4,0},{5,1},{6,2},{7,3},{8,12},{9,13},{10,... | collective-permute-start | bytes 49160 | tf_op jit(solution)/shard_map/ppermute | solution.py:392

commit v10 on v9

--- a/solution.py
+++ b/solution.py
@@ -216,7 +216,7 @@
 
 
 def alone_kernel(
-    where_ref, own_ref, back_ref, best_ref, rows_ref, kept_ref, spots_ref, cells_ref, mine_ref,
+    where_ref, own_ref, back_ref, best_ref, rows_ref, hot_ref, mark_ref, spots_ref, cells_ref, mine_ref,
     left_orders_ref, right_orders_ref, codes_ref,
 ):
     rows = best_ref.shape[1]
@@ -227,7 +227,8 @@
     core, me, left, right = parts_of(where_ref)
     left_orders_ref[...] = column_orders(rows, core, left)
     right_orders_ref[...] = column_orders(rows, core, right)
-    kept_ref[...] = back_ref[...]
+    hot_ref[...] = (iota(hot_ref.shape, 0) == back_ref[0:1, :]).astype(jnp.bfloat16)
+    mark_ref[...] = (iota(mark_ref.shape, 0) == back_ref[1:2, :]).astype(jnp.float32)
     lab = notes_of(own_ref)
     floor, ceiling = row_codes(lab, rows, core, me)
     rows_ref[...] = jnp.concatenate([floor, ceiling] * 4, axis=0)
@@ -277,17 +278,13 @@
     store_groups(out_ref, best_ref[...], mine_ref[...], spots_ref[...])
 
 
-def unpack_kernel(where_ref, back_ref, near_ref, far_ref, out_ref):
-    half = near_ref.shape[0]
-    rows = back_ref.shape[1]
-    width = 2 * GROUP
-    hot = (iota((2 * half, rows), 0) == back_ref[0:1, :]).astype(jnp.bfloat16)
+def unpack_kernel(where_ref, hot_ref, mine_ref, near_ref, far_ref, out_ref):
+    width = mine_ref.shape[0]
     results = jnp.concatenate([near_ref[:, :width], far_ref[:, :width]], axis=0)
-    total = jnp.zeros((width, rows), jnp.float32)
-    for piece in split3(results):
-        total = total + dot(piece, hot, ((0,), (0,)))
-    mine = iota((width, rows), 0) == back_ref[1:2, :]
-    out_ref[...] = jnp.sum(jnp.where(mine, total, 0.0), axis=0, keepdims=True)
+    pieces = jnp.concatenate(split3(results), axis=1)
+    total = dot(pieces, hot_ref[...], ((0,), (0,)))
+    total = total[:width] + total[width : 2 * width] + total[2 * width :]
+    out_ref[...] = jnp.sum(total * mine_ref[...], axis=0, keepdims=True)
 
 
 AXES = ("dp", "help")
@@ -354,11 +351,11 @@
     row, lines = ((1, rows), full_float), ((8, rows), full_float)
     codes, groups = ((rows, LANES), full_float), ((half, LANES), full_float)
     spot_kind, cell_kind = ((rows, LANES), half_float), ((rows, half), half_float)
-    best, own_rows, back, spots, cells, mine, left_orders, right_orders = call(
+    best, own_rows, hot, marks, spots, cells, mine, left_orders, right_orders = call(
         alone_kernel,
         "alone",
         (where, own, back),
-        (row, lines, ((8, rows), whole), spot_kind, cell_kind, ((half, rows), half_float), codes, codes),
+        (row, lines, ((2 * half, rows), half_float), ((2 * GROUP, rows), full_float), spot_kind, cell_kind, ((half, rows), half_float), codes, codes),
         (codes,),
         10**9,
     )
@@ -390,7 +387,7 @@
     best = jnp.maximum(best, cross)
     near = exchange(best.reshape(half, 1, LANES)).reshape(half, LANES)
     far = lax.ppermute(near, AXES, SWAP)
-    (out,) = call(unpack_kernel, "unpack", (where, back, near, far), (row,))
+    (out,) = call(unpack_kernel, "unpack", (where, hot, marks, near, far), (row,))
     return out.reshape(rows)
 
 

time: 111 us -> 111 us (level)
  no operation moved by 1% of the time
where the time goes in v10:
time: 111 us
  blocking collectives  62.4 us (56%)
  waiting for transfers between devices  21.6 us (19%)
  starting transfers between devices  13.3 us (12%)
  Pallas kernels  12.3 us (11%)
    all_to_all x2, blocking collectives, exchange(): lax.all_to_all(array, AXES, split_axis=0, concat_axis=0, axis_index_group...  62.4 us
    ppermute x1, waiting for transfers between devices, shards(): lax.ppermute(own, AXES, aside(-1))  14.9 us
    pallas_call x8, Pallas kernels, call(): pl.pallas_call(kernel, out_shape=tuple((jax.ShapeDtypeStruct(shape, kind)...  12.3 us
    ppermute x1, starting transfers between devices, shards(): far = lax.ppermute(near, AXES, SWAP)  5.86 us
    ppermute x1, starting transfers between devices, shards(): got = lax.ppermute(send, AXES, SWAP)  3.33 us
    ppermute x1, starting transfers between devices, shards(): lax.ppermute(own, AXES, aside(-1))  3.07 us
    ppermute x1, waiting for transfers between devices, shards(): cross = lax.ppermute(cross, AXES, aside(1))  3 us
    ppermute x1, waiting for transfers between devices, shards(): lax.ppermute(own, AXES, aside(1))  2.35 us
  transfers between devices with their start and end apart: 5, of which 5 were waited for; matrix products, arithmetic and copies ran while one was open for 0% of the time, Pallas kernels for 6%

profile of v10, /device:TPU:1, one launch (start us, length us, event | category | flops | bytes accessed | tf_op | source)
XLA Modules:
  0.0 110.9 jit_solution(9549721964856991135)
XLA Ops:
  0.0 0.1 pad_add_fusion.where_ref
  0.1 0.0 copy-start.1
  0.1 0.7 copy-done.1
  0.8 0.0 copy-start
  0.8 1.1 %rank.1 = (s32[8,1024]{1,0:T(8,128)S(1)}, bf16[64,128]{1,0:T(8,128)(2,1)S(1)}) custom-call(s32[3]{0:T(128)S(1)} %pad_add_fusion.where_ref, s32[1,1024]{1,0:T(1,128)S(1)} %bitcast.10), custom_call_target="tpu_custom_call" | custom-call | flops 1000000000 | bytes 1048576 | tf_op jit(solution)/shard_map/rank/pallas_call | solution.py:48
  1.9 0.3 copy-done
  2.2 1.9 %send.1 = (bf16[32,104,128]{2,1,0:T(8,128)(2,1)S(1)}, bf16[32,8,128]{2,1,0:T(8,128)(2,1)S(1)}, bf16[1024,768]{1,0:T(8,128)(2,1)S(1)}) custom-call(s32[3]{0:T(128)S(1)} %pad_add_fusion.where_ref, bf16[1024,768]{1,0:T(8,128)(2,1)S(1)} %copy-done, s32[8,1024]{1,0:T(8,128)S(1)} %get-tuple-element.23.rows_ref.back_ref, ...), custom_call_target="tpu_custom_call" | custom-call | flops 1000000000 | bytes 1048576 | tf_op jit(solution)/shard_map/send/pallas_call | solution.py:48
  4.1 3.3 %collective-permute-start = (bf16[32,104,128]{2,1,0:T(8,128)(2,1)S(1)}, bf16[32,104,128]{2,1,0:T(8,128)(2,1)S(1)}, u32[]{:S(2)}, u32[]{:S(2)}) collective-permute-start(bf16[32,104,128]{2,1,0:T(8,128)(2,1)S(1)} %get-tuple-element.26), channel_id=1, source_target_pairs={{0,4},{1,5},{2,6},{3,7},{4,0},{5,1},{6,2},{7,3},{8,12},{9,13},{10,... | collective-permute-start | bytes 2555912 | tf_op jit(solution)/shard_map/ppermute | solution.py:344
  7.4 1.5 %keep.1 = bf16[32,96,128]{2,1,0:T(8,128)(2,1)S(1)} custom-call(s32[3]{0:T(128)S(1)} %pad_add_fusion.where_ref, bf16[1024,768]{1,0:T(8,128)(2,1)S(1)} %get-tuple-element.25.unit_ref, s32[8,1024]{1,0:T(8,128)S(1)} %get-tuple-element.23.rows_ref.back_ref), custom_call_target="tpu_custom_call" | custom-call | flops 1000000000 | bytes 1048576 | tf_op jit(solution)/shard_map/keep/pallas_call | solution.py:48
  8.9 0.5 collective-permute-done
  9.4 0.1 slice.8
  9.5 0.1 pad_maximum_fusion
  9.6 49.0 %all_to_all.10.own_ref = bf16[32,200,128]{2,1,0:T(8,128)(2,1)S(1)} all-to-all(bf16[32,200,128]{2,1,0:T(8,128)(2,1)S(1)} %pad_maximum_fusion), channel_id=1, replica_groups={{0,8,16,24,32,40,48,56,64,72,80,88,96,104,112,120,128,136,144,152,160,1..., dimensions={0} | all-to-all | bytes 3276800 | tf_op jit(solution)/shard_map/all_to_all | solution.py:313
  58.6 3.1 %collective-permute-start.1 = (bf16[32,200,128]{2,1,0:T(8,128)(2,1)S(1)}, bf16[32,200,128]{2,1,0:T(8,128)(2,1)S(1)}, u32[]{:S(2)}, u32[]{:S(2)}) collective-permute-start(bf16[32,200,128]{2,1,0:T(8,128)(2,1)S(1)} %all_to_all.10.own_ref), channel_id=1, source_target_pairs={{0,3},{1,0},{2,1},{3,2},{4,196},{5,197},{6,198},{7,199},{8,11},{9,... | collective-permute-start | bytes 4915208 | tf_op jit(solution)/shard_map/ppermute | solution.py:350
  61.7 0.0 collective-permute-start.2
  61.7 3.1 %alone.1 = (f32[1,1024]{1,0:T(1,128)S(1)}, f32[8,1024]{1,0:T(8,128)S(1)}, bf16[64,1024]{1,0:T(8,128)(2,1)S(1)}, f32[32,1024]{1,0:T(8,128)S(1)}, bf16[1024,128]{1...) custom-call(s32[3]{0:T(128)S(1)} %pad_add_fusion.where_ref, ...), custom_call_target="tpu_custom_call" | custom-call | flops 1000000000 | bytes 1048576 | tf_op jit(solution)/shard_map/alone/pallas_call | solution.py:48
  64.8 14.9 %collective-permute-done.1.right_ref = bf16[32,200,128]{2,1,0:T(8,128)(2,1)S(1)} collective-permute-done((bf16[32,200,128]{2,1,0:T(8,128)(2,1)S(1)}, bf16[32,200,128]{2,1,0:T(8,128)(2,1)S(1)}, u32[]{:S(2)}, u32[]{:S(2)}) %collective-permute-start.1) | collective-permute-done | bytes 1638432 | tf_op jit(solution)/shard_map/ppermute | solution.py:350
  79.7 1.0 right.1
  80.8 2.4 %collective-permute-done.2.left_ref = bf16[32,200,128]{2,1,0:T(8,128)(2,1)S(1)} collective-permute-done((bf16[32,200,128]{2,1,0:T(8,128)(2,1)S(1)}, bf16[32,200,128]{2,1,0:T(8,128)(2,1)S(1)}, u32[]{:S(2)}, u32[]{:S(2)}) %collective-permute-start.2) | collective-permute-done | bytes 1638432 | tf_op jit(solution)/shard_map/ppermute | solution.py:350
  83.2 1.3 %cross.1 = (f32[32,128]{1,0:T(8,128)S(1)}, f32[1024,128]{1,0:T(8,128)S(1)}) custom-call(s32[3]{0:T(128)S(1)} %pad_add_fusion.where_ref, bf16[32,200,128]{2,1,0:T(8,128)(2,1)S(1)} %collective-permute-done.2.left_ref, bf16[32,200,128]{2,1,0:T(8,128)(2,1)S(1)} %collective-permute-done.1.right_ref, f32[8,1024]{1,0:T(8,128)S(1)} %get-tuple-element.36.rows_ref, ...), custom_call_target="tpu_custom_call" | custom-call | flops 1000000000 | bytes 1048576 | tf_op jit(solution)/shard_map/cross/pallas_call | solution.py:48
  84.5 1.0 collective-permute-start.3
  85.5 0.8 left.1
  86.3 3.0 %collective-permute-done.3 = f32[32,128]{1,0:T(8,128)S(1)} collective-permute-done((f32[32,128]{1,0:T(8,128)S(1)}, f32[32,128]{1,0:T(8,128)S(1)}, u32[]{:S(2)}, u32[]{:S(2)}) %collective-permute-start.3) | collective-permute-done | bytes 16416 | tf_op jit(solution)/shard_map/ppermute | solution.py:378
  89.3 13.4 %all_to_all.11 = f32[32,1,128]{2,1,0:T(1,128)S(1)} all-to-all(f32[32,1,128]{2,1,0:T(1,128)S(1)} %bitcast.11), channel_id=1, replica_groups={{0,8,16,24,32,40,48,56,64,72,80,88,96,104,112,120,128,136,144,152,160,1..., dimensions={0} | all-to-all | bytes 32768 | tf_op jit(solution)/shard_map/all_to_all | solution.py:313
  102.7 5.9 %collective-permute-start.4 = (f32[32,128]{1,0:T(8,128)S(1)}, f32[32,128]{1,0:T(8,128)S(1)}, u32[]{:S(2)}, u32[]{:S(2)}) collective-permute-start(f32[32,128]{1,0:T(8,128)S(1)} %bitcast.8), channel_id=1, source_target_pairs={{0,4},{1,5},{2,6},{3,7},{4,0},{5,1},{6,2},{7,3},{8,12},{9,13},{10,... | collective-permute-start | bytes 49160 | tf_op jit(solution)/shard_map/ppermute | solution.py:389
  108.6 0.8 collective-permute-done.4.far_ref
  109.4 1.5 %unpack.1 = f32[1,1024]{1,0:T(1,128)} custom-call(s32[3]{0:T(128)S(1)} %pad_add_fusion.where_ref, bf16[64,1024]{1,0:T(8,128)(2,1)S(1)} %get-tuple-element.28.hot_ref, f32[32,1024]{1,0:T(8,128)S(1)} %get-tuple-element.29.mine_ref, f32[32,128]{1,0:T(8,128)S(1)} %bitcast.9, f32[32,128]{1,0:T(8,128)S(1)} %collective-permute-done.4.far_ref), custom_call_target="tpu_custom_call" | custom-call | bytes 1048576 | tf_op jit(solution)/shard_map/unpack/pallas_call | solution.py:48
  (2 shorter events, 0.0 us)
Async XLA Ops:
  0.1 0.7 copy-start.1
  0.8 1.4 %copy-start = (bf16[1024,768]{1,0:T(8,128)(2,1)S(1)}, bf16[1024,768]{1,0:T(8,128)(2,1)}, u32[]{:S(2)}) copy-start(bf16[1024,768]{1,0:T(8,128)(2,1)} %emb_ref.1) | copy-start | bytes 4718596
  4.1 5.3 %collective-permute-start = (bf16[32,104,128]{2,1,0:T(8,128)(2,1)S(1)}, bf16[32,104,128]{2,1,0:T(8,128)(2,1)S(1)}, u32[]{:S(2)}, u32[]{:S(2)}) collective-permute-start(bf16[32,104,128]{2,1,0:T(8,128)(2,1)S(1)} %get-tuple-element.26), channel_id=1, source_target_pairs={{0,4},{1,5},{2,6},{3,7},{4,0},{5,1},{6,2},{7,3},{8,12},{9,13},{10,... | collective-permute-start | bytes 2555912 | tf_op jit(solution)/shard_map/ppermute | solution.py:344
  58.6 21.1 %collective-permute-start.1 = (bf16[32,200,128]{2,1,0:T(8,128)(2,1)S(1)}, bf16[32,200,128]{2,1,0:T(8,128)(2,1)S(1)}, u32[]{:S(2)}, u32[]{:S(2)}) collective-permute-start(bf16[32,200,128]{2,1,0:T(8,128)(2,1)S(1)} %all_to_all.10.own_ref), channel_id=1, source_target_pairs={{0,3},{1,0},{2,1},{3,2},{4,196},{5,197},{6,198},{7,199},{8,11},{9,... | collective-permute-start | bytes 4915208 | tf_op jit(solution)/shard_map/ppermute | solution.py:350
  61.7 21.5 %collective-permute-start.2 = (bf16[32,200,128]{2,1,0:T(8,128)(2,1)S(1)}, bf16[32,200,128]{2,1,0:T(8,128)(2,1)S(1)}, u32[]{:S(2)}, u32[]{:S(2)}) collective-permute-start(bf16[32,200,128]{2,1,0:T(8,128)(2,1)S(1)} %all_to_all.10.own_ref), channel_id=1, source_target_pairs={{0,1},{1,2},{2,3},{3,0},{4,68},{5,69},{6,70},{7,71},{8,9},{9,10},{... | collective-permute-start | bytes 4915208 | tf_op jit(solution)/shard_map/ppermute | solution.py:350
  84.5 4.8 %collective-permute-start.3 = (f32[32,128]{1,0:T(8,128)S(1)}, f32[32,128]{1,0:T(8,128)S(1)}, u32[]{:S(2)}, u32[]{:S(2)}) collective-permute-start(f32[32,128]{1,0:T(8,128)S(1)} %get-tuple-element.40), channel_id=1, source_target_pairs={{0,1},{1,2},{2,3},{3,0},{4,68},{5,69},{6,70},{7,71},{8,9},{9,10},{... | collective-permute-start | bytes 49160 | tf_op jit(solution)/shard_map/ppermute | solution.py:378
  102.7 6.7 %collective-permute-start.4 = (f32[32,128]{1,0:T(8,128)S(1)}, f32[32,128]{1,0:T(8,128)S(1)}, u32[]{:S(2)}, u32[]{:S(2)}) collective-permute-start(f32[32,128]{1,0:T(8,128)S(1)} %bitcast.8), channel_id=1, source_target_pairs={{0,4},{1,5},{2,6},{3,7},{4,0},{5,1},{6,2},{7,3},{8,12},{9,13},{10,... | collective-permute-start | bytes 49160 | tf_op jit(solution)/shard_map/ppermute | solution.py:389

commit v11 on v9

--- a/solution.py
+++ b/solution.py
@@ -59,9 +59,10 @@
 
 def put_rows(out_ref, unit_ref, place, base):
     rows = unit_ref.shape[0]
-    each = TILE // GROUP
-    for start in range(0, rows // 2, TILE):
-        pick = (iota((TILE, rows), 0) + (base + start) == place).astype(jnp.bfloat16)
+    size = rows // 2
+    each = size // GROUP
+    for start in range(0, size, size):
+        pick = (iota((size, rows), 0) + (base + start) == place).astype(jnp.bfloat16)
         block = dot(pick, unit_ref[...], ((1,), (0,))).astype(jnp.bfloat16)
         first = start // GROUP
         for lane in range(block.shape[1] // LANES):

time: 111 us -> 111 us (level)
  no operation moved by 1% of the time
where the time goes in v11:
time: 111 us
  blocking collectives  62.5 us (56%)
  waiting for transfers between devices  21.7 us (20%)
  starting transfers between devices  13.2 us (12%)
  Pallas kernels  12.2 us (11%)
    all_to_all x2, blocking collectives, exchange(): lax.all_to_all(array, AXES, split_axis=0, concat_axis=0, axis_index_group...  62.5 us
    ppermute x1, waiting for transfers between devices, shards(): lax.ppermute(own, AXES, aside(-1))  15 us
    pallas_call x8, Pallas kernels, call(): pl.pallas_call(kernel, out_shape=tuple((jax.ShapeDtypeStruct(shape, kind)...  12.2 us
    ppermute x1, starting transfers between devices, shards(): far = lax.ppermute(near, AXES, SWAP)  5.84 us
    ppermute x1, starting transfers between devices, shards(): got = lax.ppermute(send, AXES, SWAP)  3.33 us
    ppermute x1, starting transfers between devices, shards(): lax.ppermute(own, AXES, aside(-1))  3.05 us
    ppermute x1, waiting for transfers between devices, shards(): cross = lax.ppermute(cross, AXES, aside(1))  2.99 us
    ppermute x1, waiting for transfers between devices, shards(): lax.ppermute(own, AXES, aside(1))  2.35 us
  transfers between devices with their start and end apart: 5, of which 5 were waited for; matrix products, arithmetic and copies ran while one was open for 0% of the time, Pallas kernels for 6%

profile of v11, /device:TPU:1, one launch (start us, length us, event | category | flops | bytes accessed | tf_op | source)
XLA Modules:
  0.0 110.9 jit_solution(13281298947561945011)
XLA Ops:
  0.0 0.1 pad_add_fusion.where_ref
  0.1 0.0 copy-start.1
  0.1 0.7 copy-done.1
  0.8 0.0 copy-start
  0.8 1.1 %rank.1 = (s32[8,1024]{1,0:T(8,128)S(1)}, bf16[64,128]{1,0:T(8,128)(2,1)S(1)}) custom-call(s32[3]{0:T(128)S(1)} %pad_add_fusion.where_ref, s32[1,1024]{1,0:T(1,128)S(1)} %bitcast.10), custom_call_target="tpu_custom_call" | custom-call | flops 1000000000 | bytes 1048576 | tf_op jit(solution)/shard_map/rank/pallas_call | solution.py:48
  1.9 0.3 copy-done
  2.2 2.0 %send.1 = (bf16[32,104,128]{2,1,0:T(8,128)(2,1)S(1)}, bf16[32,8,128]{2,1,0:T(8,128)(2,1)S(1)}, bf16[1024,768]{1,0:T(8,128)(2,1)S(1)}) custom-call(s32[3]{0:T(128)S(1)} %pad_add_fusion.where_ref, bf16[1024,768]{1,0:T(8,128)(2,1)S(1)} %copy-done, s32[8,1024]{1,0:T(8,128)S(1)} %get-tuple-element.22.rows_ref.back_ref, ...), custom_call_target="tpu_custom_call" | custom-call | flops 1000000000 | bytes 1048576 | tf_op jit(solution)/shard_map/send/pallas_call | solution.py:48
  4.2 3.3 %collective-permute-start = (bf16[32,104,128]{2,1,0:T(8,128)(2,1)S(1)}, bf16[32,104,128]{2,1,0:T(8,128)(2,1)S(1)}, u32[]{:S(2)}, u32[]{:S(2)}) collective-permute-start(bf16[32,104,128]{2,1,0:T(8,128)(2,1)S(1)} %get-tuple-element.25), channel_id=1, source_target_pairs={{0,4},{1,5},{2,6},{3,7},{4,0},{5,1},{6,2},{7,3},{8,12},{9,13},{10,... | collective-permute-start | bytes 2555912 | tf_op jit(solution)/shard_map/ppermute | solution.py:348
  7.5 1.5 %keep.1 = bf16[32,96,128]{2,1,0:T(8,128)(2,1)S(1)} custom-call(s32[3]{0:T(128)S(1)} %pad_add_fusion.where_ref, bf16[1024,768]{1,0:T(8,128)(2,1)S(1)} %get-tuple-element.24.unit_ref, s32[8,1024]{1,0:T(8,128)S(1)} %get-tuple-element.22.rows_ref.back_ref), custom_call_target="tpu_custom_call" | custom-call | flops 1000000000 | bytes 1048576 | tf_op jit(solution)/shard_map/keep/pallas_call | solution.py:48
  9.0 0.5 collective-permute-done
  9.5 0.1 slice.8
  9.6 0.1 pad_maximum_fusion
  9.7 49.0 %all_to_all.10.own_ref = bf16[32,200,128]{2,1,0:T(8,128)(2,1)S(1)} all-to-all(bf16[32,200,128]{2,1,0:T(8,128)(2,1)S(1)} %pad_maximum_fusion), channel_id=1, replica_groups={{0,8,16,24,32,40,48,56,64,72,80,88,96,104,112,120,128,136,144,152,160,1..., dimensions={0} | all-to-all | bytes 3276800 | tf_op jit(solution)/shard_map/all_to_all | solution.py:317
  58.7 3.0 %collective-permute-start.1 = (bf16[32,200,128]{2,1,0:T(8,128)(2,1)S(1)}, bf16[32,200,128]{2,1,0:T(8,128)(2,1)S(1)}, u32[]{:S(2)}, u32[]{:S(2)}) collective-permute-start(bf16[32,200,128]{2,1,0:T(8,128)(2,1)S(1)} %all_to_all.10.own_ref), channel_id=1, source_target_pairs={{0,3},{1,0},{2,1},{3,2},{4,196},{5,197},{6,198},{7,199},{8,11},{9,... | collective-permute-start | bytes 4915208 | tf_op jit(solution)/shard_map/ppermute | solution.py:354
  61.7 0.0 collective-permute-start.2
  61.7 3.0 %alone.1 = (f32[1,1024]{1,0:T(1,128)S(1)}, f32[8,1024]{1,0:T(8,128)S(1)}, s32[8,1024]{1,0:T(8,128)S(1)}, bf16[1024,128]{1,0:T(8,128)(2,1)S(1)}, bf16[1024,32]{1,...) custom-call(s32[3]{0:T(128)S(1)} %pad_add_fusion.where_ref, ...), custom_call_target="tpu_custom_call" | custom-call | flops 1000000000 | bytes 1048576 | tf_op jit(solution)/shard_map/alone/pallas_call | solution.py:48
  64.8 15.0 %collective-permute-done.1.right_ref = bf16[32,200,128]{2,1,0:T(8,128)(2,1)S(1)} collective-permute-done((bf16[32,200,128]{2,1,0:T(8,128)(2,1)S(1)}, bf16[32,200,128]{2,1,0:T(8,128)(2,1)S(1)}, u32[]{:S(2)}, u32[]{:S(2)}) %collective-permute-start.1) | collective-permute-done | bytes 1638432 | tf_op jit(solution)/shard_map/ppermute | solution.py:354
  79.8 1.0 right.1
  80.9 2.4 %collective-permute-done.2.left_ref = bf16[32,200,128]{2,1,0:T(8,128)(2,1)S(1)} collective-permute-done((bf16[32,200,128]{2,1,0:T(8,128)(2,1)S(1)}, bf16[32,200,128]{2,1,0:T(8,128)(2,1)S(1)}, u32[]{:S(2)}, u32[]{:S(2)}) %collective-permute-start.2) | collective-permute-done | bytes 1638432 | tf_op jit(solution)/shard_map/ppermute | solution.py:354
  83.2 1.3 %cross.1 = (f32[32,128]{1,0:T(8,128)S(1)}, f32[1024,128]{1,0:T(8,128)S(1)}) custom-call(s32[3]{0:T(128)S(1)} %pad_add_fusion.where_ref, bf16[32,200,128]{2,1,0:T(8,128)(2,1)S(1)} %collective-permute-done.2.left_ref, bf16[32,200,128]{2,1,0:T(8,128)(2,1)S(1)} %collective-permute-done.1.right_ref, f32[8,1024]{1,0:T(8,128)S(1)} %get-tuple-element.34.rows_ref, ...), custom_call_target="tpu_custom_call" | custom-call | flops 1000000000 | bytes 1048576 | tf_op jit(solution)/shard_map/cross/pallas_call | solution.py:48
  84.6 1.0 collective-permute-start.3
  85.6 0.8 left.1
  86.3 3.0 %collective-permute-done.3 = f32[32,128]{1,0:T(8,128)S(1)} collective-permute-done((f32[32,128]{1,0:T(8,128)S(1)}, f32[32,128]{1,0:T(8,128)S(1)}, u32[]{:S(2)}, u32[]{:S(2)}) %collective-permute-start.3) | collective-permute-done | bytes 16416 | tf_op jit(solution)/shard_map/ppermute | solution.py:382
  89.3 13.5 %all_to_all.11 = f32[32,1,128]{2,1,0:T(1,128)S(1)} all-to-all(f32[32,1,128]{2,1,0:T(1,128)S(1)} %bitcast.11), channel_id=1, replica_groups={{0,8,16,24,32,40,48,56,64,72,80,88,96,104,112,120,128,136,144,152,160,1..., dimensions={0} | all-to-all | bytes 32768 | tf_op jit(solution)/shard_map/all_to_all | solution.py:317
  102.8 5.8 %collective-permute-start.4 = (f32[32,128]{1,0:T(8,128)S(1)}, f32[32,128]{1,0:T(8,128)S(1)}, u32[]{:S(2)}, u32[]{:S(2)}) collective-permute-start(f32[32,128]{1,0:T(8,128)S(1)} %bitcast.8), channel_id=1, source_target_pairs={{0,4},{1,5},{2,6},{3,7},{4,0},{5,1},{6,2},{7,3},{8,12},{9,13},{10,... | collective-permute-start | bytes 49160 | tf_op jit(solution)/shard_map/ppermute | solution.py:393
  108.6 0.8 collective-permute-done.4.far_ref
  109.5 1.4 %unpack.1 = f32[1,1024]{1,0:T(1,128)} custom-call(s32[3]{0:T(128)S(1)} %pad_add_fusion.where_ref, s32[8,1024]{1,0:T(8,128)S(1)} %get-tuple-element.27.back_ref, f32[32,128]{1,0:T(8,128)S(1)} %bitcast.9, f32[32,128]{1,0:T(8,128)S(1)} %collective-permute-done.4.far_ref), custom_call_target="tpu_custom_call" | custom-call | bytes 1048576 | tf_op jit(solution)/shard_map/unpack/pallas_call | solution.py:48
  (2 shorter events, 0.0 us)
Async XLA Ops:
  0.1 0.7 copy-start.1
  0.8 1.4 %copy-start = (bf16[1024,768]{1,0:T(8,128)(2,1)S(1)}, bf16[1024,768]{1,0:T(8,128)(2,1)}, u32[]{:S(2)}) copy-start(bf16[1024,768]{1,0:T(8,128)(2,1)} %emb_ref.1) | copy-start | bytes 4718596
  4.2 5.3 %collective-permute-start = (bf16[32,104,128]{2,1,0:T(8,128)(2,1)S(1)}, bf16[32,104,128]{2,1,0:T(8,128)(2,1)S(1)}, u32[]{:S(2)}, u32[]{:S(2)}) collective-permute-start(bf16[32,104,128]{2,1,0:T(8,128)(2,1)S(1)} %get-tuple-element.25), channel_id=1, source_target_pairs={{0,4},{1,5},{2,6},{3,7},{4,0},{5,1},{6,2},{7,3},{8,12},{9,13},{10,... | collective-permute-start | bytes 2555912 | tf_op jit(solution)/shard_map/ppermute | solution.py:348
  58.7 21.1 %collective-permute-start.1 = (bf16[32,200,128]{2,1,0:T(8,128)(2,1)S(1)}, bf16[32,200,128]{2,1,0:T(8,128)(2,1)S(1)}, u32[]{:S(2)}, u32[]{:S(2)}) collective-permute-start(bf16[32,200,128]{2,1,0:T(8,128)(2,1)S(1)} %all_to_all.10.own_ref), channel_id=1, source_target_pairs={{0,3},{1,0},{2,1},{3,2},{4,196},{5,197},{6,198},{7,199},{8,11},{9,... | collective-permute-start | bytes 4915208 | tf_op jit(solution)/shard_map/ppermute | solution.py:354
  61.7 21.5 %collective-permute-start.2 = (bf16[32,200,128]{2,1,0:T(8,128)(2,1)S(1)}, bf16[32,200,128]{2,1,0:T(8,128)(2,1)S(1)}, u32[]{:S(2)}, u32[]{:S(2)}) collective-permute-start(bf16[32,200,128]{2,1,0:T(8,128)(2,1)S(1)} %all_to_all.10.own_ref), channel_id=1, source_target_pairs={{0,1},{1,2},{2,3},{3,0},{4,68},{5,69},{6,70},{7,71},{8,9},{9,10},{... | collective-permute-start | bytes 4915208 | tf_op jit(solution)/shard_map/ppermute | solution.py:354
  84.6 4.8 %collective-permute-start.3 = (f32[32,128]{1,0:T(8,128)S(1)}, f32[32,128]{1,0:T(8,128)S(1)}, u32[]{:S(2)}, u32[]{:S(2)}) collective-permute-start(f32[32,128]{1,0:T(8,128)S(1)} %get-tuple-element.38), channel_id=1, source_target_pairs={{0,1},{1,2},{2,3},{3,0},{4,68},{5,69},{6,70},{7,71},{8,9},{9,10},{... | collective-permute-start | bytes 49160 | tf_op jit(solution)/shard_map/ppermute | solution.py:382
  102.8 6.7 %collective-permute-start.4 = (f32[32,128]{1,0:T(8,128)S(1)}, f32[32,128]{1,0:T(8,128)S(1)}, u32[]{:S(2)}, u32[]{:S(2)}) collective-permute-start(f32[32,128]{1,0:T(8,128)S(1)} %bitcast.8), channel_id=1, source_target_pairs={{0,4},{1,5},{2,6},{3,7},{4,0},{5,1},{6,2},{7,3},{8,12},{9,13},{10,... | collective-permute-start | bytes 49160 | tf_op jit(solution)/shard_map/ppermute | solution.py:393
